TPU v7x, 128 devices: a whole 4x4x4 slice. The times are simulated.
128 devices in a mesh: ep: 32 (over x, z, core), tp: 4 (over y).
Axes of the slice: x: 4, y: 4, z: 4, core: 2. Of those that a mesh axis runs over, the one named last changes fastest.
Arguments:
- inputs: bfloat16 [32768, 1024], P(('ep', 'tp')), may hold values from -6 to 6
- first_gain: bfloat16 [1024], replicated, may hold values from 0.25 to 1.75
- query_weight: bfloat16 [1024, 1024], P(None, 'tp'), may hold values from -0.1875 to 0.1875
- key_weight: bfloat16 [1024, 512], P(None, 'tp'), may hold values from -0.1875 to 0.1875
- value_weight: bfloat16 [1024, 512], P(None, 'tp'), may hold values from -0.1875 to 0.1875
- query_gain: bfloat16 [64], replicated, may hold values from 0.25 to 1.75
- key_gain: bfloat16 [64], replicated, may hold values from 0.25 to 1.75
- output_weight: bfloat16 [1024, 1024], P('tp'), may hold values from -1.5 to 1.5
- second_gain: bfloat16 [1024], replicated, may hold values from 0.25 to 1.75
- router_weight: bfloat16 [1024, 32], replicated, may hold values from -0.09375 to 0.09375
- gate_weight: bfloat16 [32, 1024, 512], P('ep', None, 'tp'), may hold values from -0.1875 to 0.1875
- up_weight: bfloat16 [32, 1024, 512], P('ep', None, 'tp'), may hold values from -0.1875 to 0.1875
- down_weight: bfloat16 [32, 512, 1024], P('ep', 'tp'), may hold values from -1 to 1
- segments: int32 [32768], P('ep'), may hold values from 0 to 2, as said below
- live_mask: int32 [32768], P('ep'), may hold values from 0 to 1, as said below
- routes: int32 [32768, 8], P(('ep', 'tp')), may hold values from 0 to 31, all different within a row; in each aligned block of 256 rows (0 to 255, 256 to 511, ...) at most 96 rows name the same one
- cotangent: bfloat16 [32768, 1024], P(('ep', 'tp')), may hold values from -6 to 6
Outputs:
- result: bfloat16 [32768, 1024], P(('ep', 'tp'))
- grad_inputs: bfloat16 [32768, 1024], P(('ep', 'tp'))
- grad_first_gain: float32 [1024], replicated
- grad_query_weight: float32 [1024, 1024], P(None, 'tp')
- grad_key_weight: float32 [1024, 512], P(None, 'tp')
- grad_value_weight: float32 [1024, 512], P(None, 'tp')
- grad_query_gain: float32 [64], replicated
- grad_key_gain: float32 [64], replicated
- grad_output_weight: float32 [1024, 1024], P('tp')
- grad_second_gain: float32 [1024], replicated
- grad_router_weight: float32 [1024, 32], replicated
- grad_gate_weight: float32 [32, 1024, 512], P('ep', None, 'tp')
- grad_up_weight: float32 [32, 1024, 512], P('ep', None, 'tp')
- grad_down_weight: float32 [32, 512, 1024], P('ep', 'tp')
Inputs may be any that keep to these rules, and one draw needn't show every extreme that they name: `segments`: in each sequence of 1024 tokens the numbers never fall and mark three documents 0, 1, 2; document 1 holds 800 tokens and begins within the first eighth. `live_mask`: in each sequence the zeros form a tail inside document 2, which keeps live tokens. `routes`: A token's 8 experts are distinct; in the rows of one device (aligned blocks of 256 tokens) no expert is named by more than 96 tokens, a bound that some block reaches.
All inputs are finite; a program needn't handle non-finite values.
Results may differ from a plain program's by a relative error of at most 0.025.
Values may be sent and summed in bfloat16 or wider, within the bound.
A program may use at most 192 MiB of HBM per device.

v0:
```python
import jax
import jax.numpy as jnp
from jax import lax
from jax.sharding import PartitionSpec as P

SEQ_LEN = 1024


HIGHEST_PRECISION = lax.Precision.HIGHEST
CONTRACT_ROWS = (((0,), (0,)), ((), ()))
CONTRACT_LAST = (((1,), (1,)), ((), ()))


def norm_rows(values, gain_vec, epsilon):
    return (
        values * lax.rsqrt(jnp.mean(values * values, axis=-1, keepdims=True) + epsilon) * gain_vec
    )


def norm_plain(values, gain_vec):
    return norm_rows(values, gain_vec, 1e-05)


def softmax_rows(values):
    shifted = jnp.exp(values - jnp.max(values, axis=-1, keepdims=True))
    return shifted / jnp.sum(shifted, axis=-1, keepdims=True)


def silu_values(values):
    return values * jax.nn.sigmoid(values)


def rotate(values, cosine_table, sine_table):
    half_dim = values.shape[-1] // 2
    first_half = values[..., :half_dim]
    second_half = values[..., half_dim:]
    return jnp.concatenate(
        [
            first_half * cosine_table - second_half * sine_table,
            second_half * cosine_table + first_half * sine_table,
        ],
        axis=-1,
    )


def rotary_tables(row_total, head_dim, seq_len):
    half_dim = head_dim // 2
    position = (jnp.arange(row_total) % seq_len).astype(jnp.float32)
    frequency = 10000.0 ** (-(jnp.arange(half_dim).astype(jnp.float32) * 2.0) / head_dim)
    angles = position[:, None] * frequency[None, :]
    return (jnp.cos(angles)[:, None, :], jnp.sin(angles)[:, None, :])


def prepare(query_raw, key_raw, query_scale, key_scale, cosine_table, sine_table, head_dim):
    row_total = query_raw.shape[0]
    query_heads = norm_rows(query_raw.reshape(row_total, -1, head_dim), query_scale, 1e-06)
    key_heads = norm_rows(key_raw.reshape(row_total, -1, head_dim), key_scale, 1e-06)
    query_rot = rotate(query_heads, cosine_table, sine_table).reshape(row_total, -1)
    key_rot = rotate(key_heads, cosine_table, sine_table).reshape(row_total, -1)
    return (query_rot, key_rot)


def allowed_pairs(segments, live_mask, seq_start, query_start, block_rows, seq_len):
    seg_query = lax.dynamic_slice_in_dim(segments, query_start, block_rows)
    query_pos = query_start + jnp.arange(block_rows)
    key_pos = seq_start + jnp.arange(seq_len)
    same_doc = seg_query[:, None] == segments[None, :]
    return same_doc & ((live_mask[None, :] == 1) | (query_pos[:, None] == key_pos[None, :]))


def block_scores(query_heads, key_heads, head_dim, allowed):
    scores = jnp.einsum(
        "qgrd,kgd->grqk", query_heads, key_heads, preferred_element_type=jnp.float32
    ) * head_dim ** (-0.5)
    return jnp.where(allowed[None, None], scores, -1e30)


def attend_forward(query, keys, values, segments, live_mask, seq_len, head_dim, groups):
    total_rows = query.shape[0]
    block_rows = min(512, seq_len)
    block_count = total_rows // block_rows

    def one_block(block_index):
        query_start = block_index * block_rows
        seq_start = query_start // seq_len * seq_len
        query_heads = lax.dynamic_slice_in_dim(query, query_start, block_rows).reshape(
            block_rows, groups, -1, head_dim
        )
        key_heads = keys.reshape(seq_len, groups, head_dim)
        value_heads = values.reshape(seq_len, groups, head_dim)
        allowed = allowed_pairs(segments, live_mask, seq_start, query_start, block_rows, seq_len)
        scores = block_scores(query_heads, key_heads, head_dim, allowed)
        maximum = jnp.max(scores, axis=-1, keepdims=True)
        exponent = jnp.exp(scores - maximum)
        denominator = jnp.sum(exponent, axis=-1, keepdims=True)
        weights = (exponent / denominator).astype(jnp.bfloat16)
        mixed_heads = jnp.einsum(
            "grqk,kgd->qgrd", weights, value_heads, preferred_element_type=jnp.float32
        )
        return (
            mixed_heads.reshape(block_rows, -1).astype(jnp.bfloat16),
            (maximum + jnp.log(denominator))[..., 0],
        )

    mixed_blocks, logsum = lax.map(one_block, jnp.arange(block_count))
    return (mixed_blocks.reshape(total_rows, -1), logsum)


def attend_backward(
    query, keys, values, grad_mixed, logsum, segments, live_mask, seq_len, head_dim, groups
):
    total_rows = query.shape[0]
    block_rows = min(512, seq_len)
    block_count = total_rows // block_rows
    per_sequence = seq_len // block_rows
    scale_factor = head_dim ** (-0.5)

    def one_block(pieces):
        block_index, block_logsum = pieces
        query_start = block_index * block_rows
        seq_start = query_start // seq_len * seq_len
        query_heads = lax.dynamic_slice_in_dim(query, query_start, block_rows).reshape(
            block_rows, groups, -1, head_dim
        )
        grad_heads = lax.dynamic_slice_in_dim(grad_mixed, query_start, block_rows).reshape(
            block_rows, groups, -1, head_dim
        )
        key_heads = keys.reshape(seq_len, groups, head_dim)
        value_heads = values.reshape(seq_len, groups, head_dim)
        allowed = allowed_pairs(segments, live_mask, seq_start, query_start, block_rows, seq_len)
        scores = block_scores(query_heads, key_heads, head_dim, allowed)
        weights = jnp.exp(scores - block_logsum[..., None])
        grad_weights = jnp.einsum(
            "qgrd,kgd->grqk", grad_heads, value_heads, preferred_element_type=jnp.float32
        )
        inner_sum = jnp.sum(weights * grad_weights, axis=-1, keepdims=True)
        grad_scores = (weights * (grad_weights - inner_sum)).astype(jnp.bfloat16)
        grad_query = (
            jnp.einsum("grqk,kgd->qgrd", grad_scores, key_heads, preferred_element_type=jnp.float32)
            * scale_factor
        )
        grad_keys = (
            jnp.einsum(
                "grqk,qgrd->kgd", grad_scores, query_heads, preferred_element_type=jnp.float32
            )
            * scale_factor
        )
        grad_values = jnp.einsum(
            "grqk,qgrd->kgd",
            weights.astype(jnp.bfloat16),
            grad_heads,
            preferred_element_type=jnp.float32,
        )
        return (
            grad_query.reshape(block_rows, -1),
            grad_keys.reshape(seq_len, -1),
            grad_values.reshape(seq_len, -1),
        )

    grad_query, grad_keys, grad_values = lax.map(one_block, (jnp.arange(block_count), logsum))
    sequences = total_rows // seq_len
    grad_keys = jnp.sum(grad_keys.reshape(sequences, per_sequence, seq_len, -1), axis=1).reshape(
        total_rows, -1
    )
    grad_values = jnp.sum(
        grad_values.reshape(sequences, per_sequence, seq_len, -1), axis=1
    ).reshape(total_rows, -1)
    return (grad_query.reshape(total_rows, -1), grad_keys, grad_values)


def shards(
    inputs,
    first_gain,
    query_weight,
    key_weight,
    value_weight,
    query_gain,
    key_gain,
    output_weight,
    second_gain,
    router_weight,
    gate_weight,
    up_weight,
    down_weight,
    segments,
    live_mask,
    routes,
    cotangent,
):
    row_count = inputs.shape[0]
    model_width = inputs.shape[1]
    head_dim = query_gain.shape[0]
    groups = key_weight.shape[1] // head_dim
    experts = router_weight.shape[1]
    top_count = routes.shape[1]
    local_experts = gate_weight.shape[0]
    ep_size = lax.axis_size("ep")
    capacity = min(row_count, row_count * top_count * 3 // (2 * experts))
    gain_one = first_gain.astype(jnp.float32)
    gain_two = second_gain.astype(jnp.float32)
    query_scale = query_gain.astype(jnp.float32)
    key_scale = key_gain.astype(jnp.float32)
    router_float = router_weight.astype(jnp.float32)
    hidden = inputs.astype(jnp.float32)
    normed_one = norm_plain(hidden, gain_one)
    gathered = lax.all_gather(normed_one.astype(jnp.bfloat16), "tp", axis=0, tiled=True)
    group_rows = gathered.shape[0]
    query_raw = jnp.dot(gathered, query_weight, preferred_element_type=jnp.float32)
    key_raw = jnp.dot(gathered, key_weight, preferred_element_type=jnp.float32)
    value_raw = jnp.dot(gathered, value_weight, preferred_element_type=jnp.float32)
    cosine_table, sine_table = rotary_tables(group_rows, head_dim, SEQ_LEN)

    def prepare_local(query_part, key_part, query_factor, key_factor):
        return prepare(
            query_part, key_part, query_factor, key_factor, cosine_table, sine_table, head_dim
        )

    (query_rot, key_rot), prepare_back = jax.vjp(
        prepare_local, query_raw, key_raw, query_scale, key_scale
    )
    query_low = query_rot.astype(jnp.bfloat16)
    key_low = key_rot.astype(jnp.bfloat16)
    value_low = value_raw.astype(jnp.bfloat16)
    mixed_heads, logsum = attend_forward(
        query_low, key_low, value_low, segments, live_mask, SEQ_LEN, head_dim, groups
    )
    attended = lax.psum_scatter(
        jnp.dot(mixed_heads, output_weight, preferred_element_type=jnp.float32).astype(
            jnp.bfloat16
        ),
        "tp",
        scatter_dimension=0,
        tiled=True,
    ).astype(jnp.float32)
    residual = hidden + attended
    normed_two, norm_two_back = jax.vjp(norm_plain, residual, gain_two)
    logits = jnp.dot(normed_two, router_float, precision=HIGHEST_PRECISION)
    gate_probs = softmax_rows(jnp.take_along_axis(logits, routes, axis=1))
    flat_routes = routes.reshape(-1)
    onehot_int = (flat_routes[:, None] == jnp.arange(experts)[None, :]).astype(jnp.int32)
    slot_index = jnp.sum(jnp.cumsum(onehot_int, axis=0) * onehot_int, axis=1) - 1
    destination = flat_routes * capacity + slot_index
    token_of_copy = jnp.arange(row_count * top_count) // top_count
    send_rows = normed_two.astype(jnp.bfloat16)
    empty_rows = jnp.zeros((experts * capacity, model_width), jnp.bfloat16)
    outgoing = empty_rows.at[destination].set(send_rows[token_of_copy])

    def owner_layout(rows_in):
        return (
            rows_in.reshape(ep_size, local_experts, capacity, model_width)
            .transpose(1, 0, 2, 3)
            .reshape(local_experts, ep_size * capacity, model_width)
        )

    def source_layout(rows_out):
        return (
            rows_out.reshape(local_experts, ep_size, capacity, model_width)
            .transpose(1, 0, 2, 3)
            .reshape(experts * capacity, model_width)
        )

    arrived = lax.all_to_all(outgoing, "ep", split_axis=0, concat_axis=0, tiled=True)
    full_gate, full_up, full_down = (
        lax.all_gather(gate_weight, "tp", axis=2, tiled=True),
        lax.all_gather(up_weight, "tp", axis=2, tiled=True),
        lax.all_gather(down_weight, "tp", axis=1, tiled=True),
    )

    def expert_hidden(expert_rows):
        gate_pre = jnp.einsum(
            "erd,edf->erf", expert_rows, full_gate, preferred_element_type=jnp.float32
        )
        up_pre = jnp.einsum(
            "erd,edf->erf", expert_rows, full_up, preferred_element_type=jnp.float32
        )
        return (gate_pre, up_pre)

    expert_rows = owner_layout(arrived)
    gate_pre, up_pre = expert_hidden(expert_rows)
    activated = (silu_values(gate_pre) * up_pre).astype(jnp.bfloat16)
    expert_out = jnp.einsum(
        "erf,efd->erd", activated, full_down, preferred_element_type=jnp.float32
    ).astype(jnp.bfloat16)
    returned = lax.all_to_all(
        source_layout(expert_out), "ep", split_axis=0, concat_axis=0, tiled=True
    )
    copy_float = (
        returned[destination].reshape(row_count, top_count, model_width).astype(jnp.float32)
    )
    combined = jnp.sum(gate_probs[:, :, None] * copy_float, axis=1)
    result = (residual + combined).astype(jnp.bfloat16)
    grad_out = cotangent.astype(jnp.float32)
    grad_gates = jnp.sum(grad_out[:, None, :] * copy_float, axis=-1)
    grad_selected = gate_probs * (
        grad_gates - jnp.sum(gate_probs * grad_gates, axis=-1, keepdims=True)
    )
    onehot_float = onehot_int.reshape(row_count, top_count, experts).astype(jnp.float32)
    grad_logits = jnp.sum(grad_selected[:, :, None] * onehot_float, axis=1)
    grad_copies = (
        (gate_probs[:, :, None] * grad_out[:, None, :])
        .astype(jnp.bfloat16)
        .reshape(-1, model_width)
    )
    grad_outgoing = empty_rows.at[destination].set(grad_copies)
    grad_arrived, arrived_again = (
        lax.all_to_all(grad_outgoing, "ep", split_axis=0, concat_axis=0, tiled=True),
        lax.all_to_all(outgoing, "ep", split_axis=0, concat_axis=0, tiled=True),
    )
    rows_again = owner_layout(arrived_again)
    gate_again, up_again = expert_hidden(rows_again)
    act_again = (silu_values(gate_again) * up_again).astype(jnp.bfloat16)
    grad_expert = owner_layout(grad_arrived)
    grad_act = jnp.einsum(
        "erd,efd->erf", grad_expert, full_down, preferred_element_type=jnp.float32
    )
    grad_down_full = jnp.einsum(
        "erf,erd->efd", act_again, grad_expert, preferred_element_type=jnp.float32
    )
    sigmoid_gate = jax.nn.sigmoid(gate_again)
    grad_gate_pre = (
        grad_act * up_again * sigmoid_gate * (1.0 + gate_again * (1.0 - sigmoid_gate))
    ).astype(jnp.bfloat16)
    grad_up_pre = (grad_act * gate_again * sigmoid_gate).astype(jnp.bfloat16)
    grad_gate_full = jnp.einsum(
        "erd,erf->edf", rows_again, grad_gate_pre, preferred_element_type=jnp.float32
    )
    grad_up_full = jnp.einsum(
        "erd,erf->edf", rows_again, grad_up_pre, preferred_element_type=jnp.float32
    )
    grad_expert_rows = jnp.einsum(
        "erf,edf->erd", grad_gate_pre, full_gate, preferred_element_type=jnp.float32
    )
    grad_expert_rows = grad_expert_rows + jnp.einsum(
        "erf,edf->erd", grad_up_pre, full_up, preferred_element_type=jnp.float32
    )
    grad_gate_shard, grad_up_shard, grad_down_shard = (
        lax.psum_scatter(
            grad_gate_full.astype(jnp.bfloat16), "tp", scatter_dimension=2, tiled=True
        ).astype(jnp.float32),
        lax.psum_scatter(
            grad_up_full.astype(jnp.bfloat16), "tp", scatter_dimension=2, tiled=True
        ).astype(jnp.float32),
        lax.psum_scatter(
            grad_down_full.astype(jnp.bfloat16), "tp", scatter_dimension=1, tiled=True
        ).astype(jnp.float32),
    )
    grad_returned = lax.all_to_all(
        source_layout(grad_expert_rows.astype(jnp.bfloat16)),
        "ep",
        split_axis=0,
        concat_axis=0,
        tiled=True,
    )
    grad_normed_two = jnp.sum(
        grad_returned[destination].reshape(row_count, top_count, model_width).astype(jnp.float32),
        axis=1,
    )
    grad_normed_two = grad_normed_two + lax.dot_general(
        grad_logits, router_float, CONTRACT_LAST, precision=HIGHEST_PRECISION
    )
    grad_router = lax.dot_general(
        normed_two, grad_logits, CONTRACT_ROWS, precision=HIGHEST_PRECISION
    )
    grad_residual_norm, grad_gain_two = norm_two_back(grad_normed_two)
    grad_residual = grad_out + grad_residual_norm
    grad_attn_all = lax.all_gather(grad_residual.astype(jnp.bfloat16), "tp", axis=0, tiled=True)
    grad_output_mat = lax.dot_general(
        mixed_heads, grad_attn_all, CONTRACT_ROWS, preferred_element_type=jnp.float32
    )
    grad_mixed = lax.dot_general(
        grad_attn_all, output_weight, CONTRACT_LAST, preferred_element_type=jnp.float32
    ).astype(jnp.bfloat16)
    grad_query, grad_keys, grad_values = attend_backward(
        query_low,
        key_low,
        value_low,
        grad_mixed,
        logsum,
        segments,
        live_mask,
        SEQ_LEN,
        head_dim,
        groups,
    )
    grad_query_raw, grad_key_raw, grad_query_scale, grad_key_scale = prepare_back(
        (grad_query, grad_keys)
    )
    grad_query_low = grad_query_raw.astype(jnp.bfloat16)
    grad_key_low = grad_key_raw.astype(jnp.bfloat16)
    grad_value_low = grad_values.astype(jnp.bfloat16)
    grad_query_mat = lax.dot_general(
        gathered, grad_query_low, CONTRACT_ROWS, preferred_element_type=jnp.float32
    )
    grad_key_mat = lax.dot_general(
        gathered, grad_key_low, CONTRACT_ROWS, preferred_element_type=jnp.float32
    )
    grad_value_mat = lax.dot_general(
        gathered, grad_value_low, CONTRACT_ROWS, preferred_element_type=jnp.float32
    )
    summed = lax.dot_general(
        grad_query_low, query_weight, CONTRACT_LAST, preferred_element_type=jnp.float32
    )
    summed = summed + lax.dot_general(
        grad_key_low, key_weight, CONTRACT_LAST, preferred_element_type=jnp.float32
    )
    grad_normed_one = lax.psum_scatter(
        (
            summed
            + lax.dot_general(
                grad_value_low, value_weight, CONTRACT_LAST, preferred_element_type=jnp.float32
            )
        ).astype(jnp.bfloat16),
        "tp",
        scatter_dimension=0,
        tiled=True,
    ).astype(jnp.float32)
    unused_norm, norm_one_back = jax.vjp(norm_plain, hidden, gain_one)
    grad_hidden_norm, grad_gain_one = norm_one_back(grad_normed_one)
    grad_inputs = (grad_residual + grad_hidden_norm).astype(jnp.bfloat16)
    grad_query_mat, grad_key_mat, grad_value_mat, grad_output_mat = (
        lax.psum(grad_query_mat.astype(jnp.bfloat16), "ep").astype(jnp.float32),
        lax.psum(grad_key_mat.astype(jnp.bfloat16), "ep").astype(jnp.float32),
        lax.psum(grad_value_mat.astype(jnp.bfloat16), "ep").astype(jnp.float32),
        lax.psum(grad_output_mat.astype(jnp.bfloat16), "ep").astype(jnp.float32),
    )
    grad_gain_one, grad_gain_two, grad_query_scale, grad_key_scale, grad_router = lax.psum(
        (grad_gain_one, grad_gain_two, grad_query_scale, grad_key_scale, grad_router), ("ep", "tp")
    )
    return (
        result,
        grad_inputs,
        grad_gain_one,
        grad_query_mat,
        grad_key_mat,
        grad_value_mat,
        grad_query_scale,
        grad_key_scale,
        grad_output_mat,
        grad_gain_two,
        grad_router,
        grad_gate_shard,
        grad_up_shard,
        grad_down_shard,
    )


def solution(mesh):
    return jax.shard_map(
        shards,
        mesh=mesh,
        in_specs=(
            P(("ep", "tp"), None),
            P(),
            P(None, "tp"),
            P(None, "tp"),
            P(None, "tp"),
            P(),
            P(),
            P("tp", None),
            P(),
            P(),
            P("ep", None, "tp"),
            P("ep", None, "tp"),
            P("ep", "tp", None),
            P("ep"),
            P("ep"),
            P(("ep", "tp"), None),
            P(("ep", "tp"), None),
        ),
        out_specs=(
            P(("ep", "tp"), None),
            P(("ep", "tp"), None),
            P(),
            P(None, "tp"),
            P(None, "tp"),
            P(None, "tp"),
            P(),
            P(),
            P("tp", None),
            P(),
            P(),
            P("ep", None, "tp"),
            P("ep", None, "tp"),
            P("ep", "tp", None),
        ),
        check_vma=False,
    )
```

profile of v0, /device:TPU:1, one launch (start us, length us, event | category | flops | bytes accessed | tf_op | source)
XLA Modules:
  0.0 971.7 jit_solution(15271099006954167019)
XLA Ops:
  13.8 32.2 %all-gather.6.cloned.1.call-done = bf16[1024,1024]{1,0:T(8,128)(2,1)} async-done(((bf16[256,1024]{1,0:T(8,128)(2,1)}), bf16[1024,1024]{1,0:T(8,128)(2,1)}) %all-gather.6.cloned.1.call-update) | async-done | bytes 2097168 | tf_op jit(solution)/shard_map/all_gather | solution.py:206
  55.9 20.9 %while.30 = (s32[]{:T(128)}, bf16[2,512,256]{2,1,0:T(8,128)(2,1)S(1)}, f32[2,2,2,512]{3,2,1,0:T(2,128)}, s32[2]{0:T(128)S(1)}, s32[1024]{0:T(1024)S(1)}, /*index...) while((s32[]{:T(128)}, ...), condition=%wide.region_6.7_spmd, body=%wide.region_3.6_spmd.sunk | while | flops 564265472 | bytes 29979016 | solution.py:105
  79.6 9.1 reduce-window.6
  89.6 19.2 %reduce-scatter.10.cloned.1.call-done = bf16[256,1024]{1,0:T(8,128)(2,1)} async-done(((bf16[1024,1024]{1,0:T(8,128)(2,1)}), bf16[256,1024]{1,0:T(8,128)(2,1)}) %reduce-scatter.10.cloned.1.call-update) | async-done | bytes 524304 | tf_op jit(solution)/shard_map/reduce_scatter | solution.py:227
  111.4 28.8 %scatter_custom_fusion = bf16[3072,1024]{1,0:T(8,128)(2,1)} fusion(s32[2048]{0:T(1024)S(1)} %bitcast.337, bf16[256,1024]{1,0:T(8,128)(2,1)S(1)} %fusion.52, s32[2048]{0:T(1024)S(1)} %broadcast_clamp_fusion.1, bf16[]{:T(256)} %constant.225.clone.1), kind=kCustom, calls=%fused_computation.61 | custom fusion | bytes 6291458 | tf_op jit(solution)/shard_map/scatter | solution.py:246
  140.2 8.2 all-to-all-start
  149.7 16.8 %gather_fusion.2 = f32[2048]{0:T(1024)S(1)} fusion(f32[256,32]{0,1:T(8,128)S(1)} %fusion.53, s32[2048]{0:T(1024)S(1)} %reshape.763), kind=kCustom, calls=%fused_computation.3 | custom fusion | bytes 32768 | tf_op jit(solution)/shard_map/jit(take_along_axis)/gather | solution.py:238
  166.9 14.3 %scatter_custom_fusion.1 = bf16[3072,1024]{1,0:T(8,128)(2,1)} fusion(s32[2048]{0:T(1024)S(1)} %bitcast.338, f32[256,1024]{1,0:T(8,128)S(1)} %convert_element_type.309, f32[2048]{0:T(1024)S(1)} %mul.725, bf16[]{:T(256)} %constant.225.clone.1), kind=kCustom, calls=%fused_computation.60 | custom fusion | flops 4194304 | bytes 7348226 | tf_op jit(solution)/shard_map/scatter | solution.py:304
  181.2 44.9 %all-to-all-done = bf16[32,96,1024]{2,1,0:T(8,128)(2,1)} async-done(((bf16[32,96,1024]{2,1,0:T(8,128)(2,1)}), bf16[32,96,1024]{2,1,0:T(8,128)(2,1)}, u32[]{:S(2)}, u32[]{:S(2)}) %all-to-all-start) | async-done | bytes 6291488 | tf_op jit(solution)/shard_map/all_to_all | solution.py:262
  226.1 14.3 %all-to-all-start.2 = ((bf16[32,96,1024]{2,1,0:T(8,128)(2,1)}), bf16[32,96,1024]{2,1,0:T(8,128)(2,1)}, u32[]{:S(2)}, u32[]{:S(2)}) async-start(bf16[32,96,1024]{2,1,0:T(8,128)(2,1)} %bitcast.314), calls=%async_computation.3 | async-start | bytes 12582912 | tf_op jit(solution)/shard_map/all_to_all | solution.py:306
  242.4 25.2 %all-gather.10.cloned.1.call-done = bf16[1,1024,512]{2,1,0:T(8,128)(2,1)} async-done(((bf16[1,1024,128]{2,1,0:T(8,128)(2,1)}), bf16[1,1024,512]{2,1,0:T(8,128)(2,1)}) %all-gather.10.cloned.1.call-update) | async-done | bytes 1048592 | tf_op jit(solution)/shard_map/all_gather | solution.py:265
  267.5 9.2 fusion.45
  276.7 19.3 %all-gather.8.cloned.1.call-done = bf16[1,1024,512]{2,1,0:T(8,128)(2,1)} async-done(((bf16[1,1024,128]{2,1,0:T(8,128)(2,1)}), bf16[1,1024,512]{2,1,0:T(8,128)(2,1)}) %all-gather.8.cloned.1.call-update) | async-done | bytes 1048592 | tf_op jit(solution)/shard_map/all_gather | solution.py:264
  296.0 9.1 fusion.49
  305.1 17.5 %all-gather.12.cloned.1.call-done = bf16[1,512,1024]{2,1,0:T(8,128)(2,1)} async-done(((bf16[1,128,1024]{2,1,0:T(8,128)(2,1)}), bf16[1,512,1024]{2,1,0:T(8,128)(2,1)}) %all-gather.12.cloned.1.call-update) | async-done | bytes 1048592 | tf_op jit(solution)/shard_map/all_gather | solution.py:266
  322.6 13.9 %multiply_convert_fusion = (bf16[3072,512]{1,0:T(8,128)(2,1)}, bf16[3072,512]{1,0:T(8,128)(2,1)}, bf16[3072,512]{1,0:T(8,128)(2,1)S(1)}) fusion(f32[3072,512]{1,0:T(8,128)} %fusion.49, f32[3072,512]{1,0:T(8,128)} %fusion.45, bf16[3072,1024]{1,0:T(8,128)(2,1)} %bitcast.56, bf16[1,512,1024]{2,1,0:T(8,128)(2,1)} %all-gather.12.cloned.1.call-done), kind=kOutput, calls=%fused_computation.55 | convolution fusion | flops 3246391296 | bytes 29360128 | tf_op jit(solution)/shard_map/erd,efd->erf/dot_general | solution.py:313
  341.8 11.0 %all-to-all-start.1 = ((bf16[32,96,1024]{2,1,0:T(8,128)(2,1)}), bf16[32,96,1024]{2,1,0:T(8,128)(2,1)}, u32[]{:S(2)}, u32[]{:S(2)}) async-start(bf16[32,96,1024]{2,1,0:T(8,128)(2,1)} %bitcast.324), calls=%async_computation.2 | async-start | bytes 12582912 | tf_op jit(solution)/shard_map/all_to_all | solution.py:284
  366.5 64.1 %all-to-all-done.1 = bf16[32,96,1024]{2,1,0:T(8,128)(2,1)} async-done(((bf16[32,96,1024]{2,1,0:T(8,128)(2,1)}), bf16[32,96,1024]{2,1,0:T(8,128)(2,1)}, u32[]{:S(2)}, u32[]{:S(2)}) %all-to-all-start.1) | async-done | bytes 6291488 | tf_op jit(solution)/shard_map/all_to_all | solution.py:284
  430.5 14.3 %all-to-all-start.3 = ((bf16[32,96,1024]{2,1,0:T(8,128)(2,1)}), bf16[32,96,1024]{2,1,0:T(8,128)(2,1)}, u32[]{:S(2)}, u32[]{:S(2)}) async-start(bf16[32,96,1024]{2,1,0:T(8,128)(2,1)} %bitcast.323), calls=%async_computation.4 | async-start | bytes 12582912 | tf_op jit(solution)/shard_map/all_to_all | solution.py:347
  444.9 14.6 %gather_fusion = bf16[2048,1024]{1,0:T(8,128)(2,1)} fusion(bf16[3072,1024]{1,0:T(8,128)(2,1)} %bitcast.52, s32[2048]{0:T(1024)S(1)} %broadcast_clamp_fusion), kind=kCustom, calls=%fused_computation.1 | custom fusion | bytes 8396800 | tf_op jit(solution)/shard_map/gather | solution.py:288
  465.9 56.9 %all-to-all-done.3 = bf16[32,96,1024]{2,1,0:T(8,128)(2,1)} async-done(((bf16[32,96,1024]{2,1,0:T(8,128)(2,1)}), bf16[32,96,1024]{2,1,0:T(8,128)(2,1)}, u32[]{:S(2)}, u32[]{:S(2)}) %all-to-all-start.3) | async-done | bytes 6291488 | tf_op jit(solution)/shard_map/all_to_all | solution.py:347
  522.8 14.6 %gather_fusion.1 = bf16[2048,1024]{1,0:T(8,128)(2,1)} fusion(bf16[3072,1024]{1,0:T(8,128)(2,1)} %bitcast.58, s32[2048]{0:T(1024)S(1)} %broadcast_clamp_fusion), kind=kCustom, calls=%fused_computation.2 | custom fusion | bytes 8396800 | tf_op jit(solution)/shard_map/gather | solution.py:355
  546.9 8.1 fusion.28
  561.2 8.6 fusion.29
  576.1 8.2 fusion.30
  587.9 56.7 %while.31 = (s32[]{:T(128)}, f32[2,512,256]{1,0,2:T(2,128)}, f32[2,1024,128]{1,2,0:T(8,128)}, f32[2,1024,128]{1,2,0:T(8,128)}, s32[2]{0:T(128)S(1)}, /*index=5*/...) while((s32[]{:T(128)}, f32[2,512,256]{1,0,2:T(2,128)}, ...), condition=%wide.region_24.25_spmd, body=%wide.region_22.24_spmd.sunk | while | flops 1375994368 | bytes 74273184 | solution.py:160
  604.7 10.3 %dynamic_update_slice.45 = f32[2,512,256]{1,0,2:T(2,128)} dynamic-update-slice(f32[2,512,256]{1,0,2:T(2,128)} %get-tuple-element.706, f32[1,512,256]{1,0,2:T(1,128)S(1)} %copy.168, s32[]{:T(128)S(6)} %copy.187, s32[]{:T(128)} %constant.224.clone.1..sunk.1, s32[]{:T(128)} %constant.224.clone.1..sunk.1) | dynamic-update-slice | bytes 1048580 | tf_op jit(solution)/shard_map/while/body/jit(dynamic_update_index_in_dim)/dynamic_update_slice | solution.py:160
  632.9 10.3 %dynamic_update_slice.45 = f32[2,512,256]{1,0,2:T(2,128)} dynamic-update-slice(f32[2,512,256]{1,0,2:T(2,128)} %get-tuple-element.706, f32[1,512,256]{1,0,2:T(1,128)S(1)} %copy.168, s32[]{:T(128)S(6)} %copy.187, s32[]{:T(128)} %constant.224.clone.1..sunk.1, s32[]{:T(128)} %constant.224.clone.1..sunk.1) | dynamic-update-slice | bytes 1048580 | tf_op jit(solution)/shard_map/while/body/jit(dynamic_update_index_in_dim)/dynamic_update_slice | solution.py:160
  689.5 96.1 %all-reduce.11.cloned.1.call-done = (bf16[1024,256]{1,0:T(8,128)(2,1)}, bf16[1024,128]{1,0:T(8,128)(2,1)}, bf16[1024,128]{1,0:T(8,128)(2,1)}, bf16[256,1024]{1,0:T(8,128)(2,1)}) async-done(((bf16[1024,256]{1,0:T(8,128)(2,1)}, bf16[1024,128]{1,0:T(8,128)(2,1)}, bf16[1024,128]{1,0:T(8,128)(2,1)}, bf16[256,1024]{1,0:T(8,128)(2,1)}), (bf16[1024,256]{1,0:T(8,128)(2,1)}, bf16[1024,128]{1,0:T(8,128)(2,1)}, ...) | async-done | bytes 1572880 | tf_op jit(solution)/shard_map/psum | solution.py:421
  793.3 24.4 %reduce-scatter.12.cloned.1.call-done = bf16[256,1024]{1,0:T(8,128)(2,1)} async-done(((bf16[1024,1024]{1,0:T(8,128)(2,1)}), bf16[256,1024]{1,0:T(8,128)(2,1)}) %reduce-scatter.12.cloned.1.call-update) | async-done | bytes 524304 | tf_op jit(solution)/shard_map/reduce_scatter | solution.py:406
  822.3 65.2 %all-reduce.4 = (f32[1024]{0:T(1024)}, f32[64]{0:T(128)}, f32[64]{0:T(128)}, f32[1024]{0:T(1024)}) all-reduce(f32[1024]{0:T(1024)S(1)} %get-tuple-element.418, f32[64]{0:T(128)S(1)} %get-tuple-element.416, f32[64]{0:T(128)S(1)} %get-tuple-element.420, f32[1024]{0:T(1024)S(1)} %copy-done.50), channel_id=1, replica_groups=mesh['ep'=32,'tp'=4] {'ep','tp'}, use_global_device_ids=true, to_apply=%region_32.33 | all-reduce | flops 2176 | bytes 17408 | tf_op jit(solution)/shard_map/psum | solution.py:426
  887.5 75.3 %all-reduce.9.cloned.1.call-done = f32[1024,32]{0,1:T(8,128)} async-done(((f32[1024,32]{0,1:T(8,128)}), f32[1024,32]{0,1:T(8,128)}) %all-reduce.9.cloned.1.call-update) | async-done | bytes 131088 | tf_op jit(solution)/shard_map/psum | solution.py:426
  (330 shorter events, 188.6 us)
Async XLA Ops:
  7.2 45.1 %copy-start = (bf16[1024,256]{1,0:T(8,128)(2,1)S(1)}, bf16[1024,256]{1,0:T(8,128)(2,1)}, u32[]{:S(2)}) copy-start(bf16[1024,256]{1,0:T(8,128)(2,1)} %param.23) | copy-start | bytes 1572868
  7.2 38.9 %all-gather.6.cloned.1.call-start = ((), (), s32[]{:S(2)}) async-start(), calls=%async_computation.9 | async-start | bytes 2621440 | tf_op jit(solution)/shard_map/all_gather | solution.py:206
  11.8 97.0 %reduce-scatter.10.cloned.1.call-start = ((), (), s32[]{:S(2)}) async-start(), calls=%async_computation.10 | async-start | bytes 2621440 | tf_op jit(solution)/shard_map/reduce_scatter | solution.py:227
  12.6 43.0 %copy-start.58 = (f32[64]{0:T(128)}, f32[64]{0:T(128)S(1)}, u32[]{:S(2)}) copy-start(f32[64]{0:T(128)S(1)} %convert_element_type.292) | copy-start | bytes 772
  76.8 63.3 %copy-start.3 = (bf16[1024,128]{0,1:T(8,128)(2,1)}, bf16[1024,128]{0,1:T(8,128)(2,1)S(1)}, u32[]{:S(2)}) copy-start(bf16[1024,128]{0,1:T(8,128)(2,1)S(1)} %get-tuple-element.777) | copy-start | bytes 786436
  76.8 63.3 %copy-start.6 = (bf16[1024,256]{0,1:T(8,128)(2,1)}, bf16[1024,256]{0,1:T(8,128)(2,1)S(1)}, u32[]{:S(2)}) copy-start(bf16[1024,256]{0,1:T(8,128)(2,1)S(1)} %get-tuple-element.782) | copy-start | bytes 1572868
  76.8 63.3 %copy-start.26 = (bf16[2,512,256]{2,1,0:T(8,128)(2,1)}, bf16[2,512,256]{2,1,0:T(8,128)(2,1)S(1)}, u32[]{:S(2)}) copy-start(bf16[2,512,256]{2,1,0:T(8,128)(2,1)S(1)} %get-tuple-element.281) | copy-start | bytes 1572868
  79.3 465.1 %copy-start.42 = (f32[1024]{0:T(1024)}, f32[1024]{0:T(1024)S(1)}, u32[]{:S(2)}) copy-start(f32[1024]{0:T(1024)S(1)} %convert_element_type.301) | copy-start | bytes 12292
  110.1 434.3 %copy-start.48 = (f32[256]{0:T(256)}, f32[256]{0:T(256)S(1)}, u32[]{:S(2)}) copy-start(f32[256]{0:T(256)S(1)} %fusion.73) | copy-start | bytes 3076
  140.2 85.9 %all-to-all-start = ((bf16[32,96,1024]{2,1,0:T(8,128)(2,1)}), bf16[32,96,1024]{2,1,0:T(8,128)(2,1)}, u32[]{:S(2)}, u32[]{:S(2)}) async-start(bf16[32,96,1024]{2,1,0:T(8,128)(2,1)} %bitcast.315), calls=%async_computation.1 | async-start | bytes 12582912 | tf_op jit(solution)/shard_map/all_to_all | solution.py:262
  226.1 96.5 %all-to-all-start.2 = ((bf16[32,96,1024]{2,1,0:T(8,128)(2,1)}), bf16[32,96,1024]{2,1,0:T(8,128)(2,1)}, u32[]{:S(2)}, u32[]{:S(2)}) async-start(bf16[32,96,1024]{2,1,0:T(8,128)(2,1)} %bitcast.314), calls=%async_computation.3 | async-start | bytes 12582912 | tf_op jit(solution)/shard_map/all_to_all | solution.py:306
  240.5 27.1 %all-gather.10.cloned.1.call-start = ((), (), s32[]{:S(2)}) async-start(), calls=%async_computation.12 | async-start | bytes 1310720 | tf_op jit(solution)/shard_map/all_gather | solution.py:265
  241.2 54.8 %all-gather.8.cloned.1.call-start = ((), (), s32[]{:S(2)}) async-start(), calls=%async_computation.11 | async-start | bytes 1310720 | tf_op jit(solution)/shard_map/all_gather | solution.py:264
  241.8 80.8 %all-gather.12.cloned.1.call-start = ((), (), s32[]{:S(2)}) async-start(), calls=%async_computation.13 | async-start | bytes 1310720 | tf_op jit(solution)/shard_map/all_gather | solution.py:266
  341.8 88.7 %all-to-all-start.1 = ((bf16[32,96,1024]{2,1,0:T(8,128)(2,1)}), bf16[32,96,1024]{2,1,0:T(8,128)(2,1)}, u32[]{:S(2)}, u32[]{:S(2)}) async-start(bf16[32,96,1024]{2,1,0:T(8,128)(2,1)} %bitcast.324), calls=%async_computation.2 | async-start | bytes 12582912 | tf_op jit(solution)/shard_map/all_to_all | solution.py:284
  430.5 92.3 %all-to-all-start.3 = ((bf16[32,96,1024]{2,1,0:T(8,128)(2,1)}), bf16[32,96,1024]{2,1,0:T(8,128)(2,1)}, u32[]{:S(2)}, u32[]{:S(2)}) async-start(bf16[32,96,1024]{2,1,0:T(8,128)(2,1)} %bitcast.323), calls=%async_computation.4 | async-start | bytes 12582912 | tf_op jit(solution)/shard_map/all_to_all | solution.py:347
  444.9 139.8 %all-gather.14.cloned.1.call-start = ((), (), s32[]{:S(2)}) async-start(), calls=%async_computation.14 | async-start | bytes 2621440 | tf_op jit(solution)/shard_map/all_gather | solution.py:366
  465.9 77.0 %copy-start.40 = (f32[256,32]{0,1:T(8,128)}, f32[256,32]{0,1:T(8,128)S(1)}, u32[]{:S(2)}) copy-start(f32[256,32]{0,1:T(8,128)S(1)} %multiply_reduce_fusion.9) | copy-start | bytes 98308
  546.7 131.0 %reduce-scatter.16.cloned.1.call-start = ((), (), s32[]{:S(2)}) async-start(), calls=%async_computation.18 | async-start | bytes 1310720
  561.1 120.8 %reduce-scatter.18.cloned.1.call-start = ((), (), s32[]{:S(2)}) async-start(), calls=%async_computation.19 | async-start | bytes 1310720
  576.0 110.0 %reduce-scatter.14.cloned.1.call-start = ((), (), s32[]{:S(2)}) async-start(), calls=%async_computation.17 | async-start | bytes 1310720 | tf_op jit(solution)/shard_map/reduce_scatter | solution.py:343
  584.4 201.2 %all-reduce.11.cloned.1.call-start = ((), (), s32[]{:S(2)}) async-start(), calls=%async_computation.20 | async-start | bytes 3145728 | tf_op jit(solution)/shard_map/psum | solution.py:421
  587.9 58.0 %copy-start.19 = (f32[1024,32]{0,1:T(8,128)S(1)}, f32[1024,32]{0,1:T(8,128)}, u32[]{:S(2)}) copy-start(f32[1024,32]{0,1:T(8,128)} %copy-done.18) | copy-start | bytes 393220
  673.1 144.6 %reduce-scatter.12.cloned.1.call-start = ((), (), s32[]{:S(2)}) async-start(), calls=%async_computation.15 | async-start | bytes 2621440 | tf_op jit(solution)/shard_map/reduce_scatter | solution.py:406
  677.5 140.2 %copy-start.47 = (f32[1024]{0:T(1024)S(1)}, f32[1024]{0:T(1024)}, u32[]{:S(2)}) copy-start(f32[1024]{0:T(1024)} %copy-done.46) | copy-start | bytes 12292
  677.5 140.2 %copy-start.52 = (f32[256]{0:T(256)S(1)}, f32[256]{0:T(256)}, u32[]{:S(2)}) copy-start(f32[256]{0:T(256)} %copy-done.51) | copy-start | bytes 3076
  677.5 141.7 %copy-start.56 = (f32[256]{0:T(256)S(1)}, f32[256]{0:T(256)}, u32[]{:S(2)}) copy-start(f32[256]{0:T(256)} %copy-done.55) | copy-start | bytes 3076
  677.5 141.7 %copy-start.13 = (f32[256,1024]{1,0:T(8,128)S(1)}, f32[256,1024]{1,0:T(8,128)}, u32[]{:S(2)}) copy-start(f32[256,1024]{1,0:T(8,128)} %copy-done.12) | copy-start | bytes 3145732
  677.6 141.7 %copy-start.15 = (bf16[256,1024]{1,0:T(8,128)(2,1)S(1)}, bf16[256,1024]{1,0:T(8,128)(2,1)}, u32[]{:S(2)}) copy-start(bf16[256,1024]{1,0:T(8,128)(2,1)} %param.37) | copy-start | bytes 1572868
  677.6 141.7 %copy-start.54 = (f32[256]{0:T(256)S(1)}, f32[256]{0:T(256)}, u32[]{:S(2)}) copy-start(f32[256]{0:T(256)} %copy-done.53) | copy-start | bytes 3076
  677.6 285.2 %all-reduce.9.cloned.1.call-start = ((), (), s32[]{:S(2)}) async-start(), calls=%async_computation.16 | async-start | bytes 262144 | tf_op jit(solution)/shard_map/psum | solution.py:426
  687.9 134.5 %copy-start.50 = (f32[1024]{0:T(1024)S(1)}, f32[1024]{0:T(1024)}, u32[]{:S(2)}) copy-start(f32[1024]{0:T(1024)} %get-tuple-element.414) | copy-start | bytes 12292
  (47 other events, 449.6 us)
Sparse Core Ops, SparseCore 0:
  12.0 34.0 all-gather.5
  79.1 29.7 reduce-scatter.9
  243.1 24.4 all-gather.9
  269.1 26.8 all-gather.7
  297.6 24.9 all-gather.11
  546.8 37.4 all-gather.13
  586.8 21.5 reduce-scatter.15
  610.8 23.7 reduce-scatter.17
  637.2 22.5 reduce-scatter.13
  673.2 112.3 all-reduce.10
  788.1 29.5 reduce-scatter.11
  822.9 139.8 all-reduce.8
where the time goes:
time: 983 us; the launch traced here: 972 us
  waiting for transfers between devices  477 us (49%)
  matrix products  137 us (14%)
  local copies, waits for them, and re-layouts  135 us (14%)
  other arithmetic  89.7 us (9%)
  blocking collectives  65.2 us (7%)
  starting transfers between devices  49 us (5%)
  between operations  15.8 us (2%)
    psum x1, waiting for transfers between devices, shards(): lax.psum(grad_query_mat.astype(jnp.bfloat16), 'ep').astype(jnp.float32)  96.1 us
    psum x1, waiting for transfers between devices, shards(): lax.psum((grad_gain_one, grad_gain_two, grad_query_scale, grad_key_scale,...  75.3 us
    psum x1, blocking collectives, shards(): lax.psum((grad_gain_one, grad_gain_two, grad_query_scale, grad_key_scale,...  65.2 us
    all_to_all x1, waiting for transfers between devices, shards(): lax.all_to_all(source_layout(expert_out), 'ep', split_axis=0, concat_axis...  64.1 us
    all_to_all x1, waiting for transfers between devices, shards(): lax.all_to_all(source_layout(grad_expert_rows.astype(jnp.bfloat16)), 'ep'...  56.9 us
    all_to_all x1, waiting for transfers between devices, shards(): lax.all_to_all(outgoing, 'ep', split_axis=0, concat_axis=0, tiled=True)  44.9 us
    all_gather x1, waiting for transfers between devices, shards(): lax.all_gather(normed_one.astype(jnp.bfloat16), 'tp', axis=0, tiled=True)  32.2 us
    scatter x1, local copies, waits for them, and re-layouts, shards(): outgoing = empty_rows.at[destination].set(send_rows[token_of_copy])  28.8 us
  transfers between devices with their start and end apart: 16, of which 11 were waited for; matrix products, arithmetic and copies ran while one was open for 26% of the time, Pallas kernels for 0%

commit v1 on v0

v1 whole, which is shorter than its diff:
```python
import functools

import jax
import jax.numpy as jnp
from jax import lax
from jax.experimental import pallas as pl
from jax.experimental.pallas import tpu as pltpu
from jax.sharding import PartitionSpec as P

SEQ_LEN = 1024
HIGHEST_PRECISION = lax.Precision.HIGHEST
CONTRACT_ROWS = (((0,), (0,)), ((), ()))
CONTRACT_LAST = (((1,), (1,)), ((), ()))
MESH = pl.DeviceIdType.MESH
ANY = pl.BlockSpec(memory_space=pl.ANY)
VMEM = pl.BlockSpec(memory_space=pltpu.VMEM)
F32 = jnp.float32
BF16 = jnp.bfloat16
SLOTS = 96
EXTRA = 16


def wrap(value):
    return lax.rem(value + 4, 4)


def pick(core, first, second):
    return first * (1 - core) + second * core


def plane_place():
    ep = lax.axis_index("ep")
    core = lax.rem(ep, 2)
    z = lax.rem(lax.div(ep, 2), 4)
    x = lax.div(ep, 8)
    return (pick(core, x, z), pick(core, z, x), core)


def plane_index(a, b, core):
    a, b = wrap(a), wrap(b)
    return (pick(core, a, b) * 4 + pick(core, b, a)) * 2 + core


def plane_partners():
    a, b, core = plane_place()
    tp = lax.axis_index("tp")
    return (
        (plane_index(a + 1, b, core), tp),
        (plane_index(a - 1, b, core), tp),
        (plane_index(a, b + 1, core), tp),
        (plane_index(a, b - 1, core), tp),
        (plane_index(b, a, 1 - core), tp),
    )


def line_partners():
    ep, tp = lax.axis_index("ep"), lax.axis_index("tp")
    return ((ep, wrap(tp + 1)), (ep, wrap(tp - 1)))


def greet(partners):
    barrier = pltpu.get_barrier_semaphore()
    for partner in partners:
        pl.semaphore_signal(barrier, inc=1, device_id=partner, device_id_type=MESH)
    pl.semaphore_wait(barrier, len(partners))


def halves(rows):
    top = (rows // 2 + 15) // 16 * 16
    return (pl.ds(0, top), pl.ds(top, rows - top))


class Post:
    def __init__(self, send_sems, recv_sems):
        self.send_sems, self.recv_sems, self.started = send_sems, recv_sems, []

    def go(self, src, dst, partner):
        number = len(self.started)
        copy = pltpu.make_async_remote_copy(
            src_ref=src,
            dst_ref=dst,
            send_sem=self.send_sems.at[number],
            recv_sem=self.recv_sems.at[number],
            device_id=partner,
            device_id_type=MESH,
        )
        copy.start()
        self.started.append(copy)
        return copy

    def finish(self):
        for copy in self.started:
            copy.wait_send()


def plane_gather_body(post, own_ref, all_ref):
    a, b, core = plane_place()
    me = plane_index(a, b, core)
    ahead_a, behind_a, ahead_b, behind_b, sibling = plane_partners()
    top, bottom = halves(own_ref.shape[0])
    go = post.go
    a_ahead = go(own_ref, all_ref.at[me], ahead_a)
    a_behind = go(own_ref, all_ref.at[me], behind_a)

    def along_b(src, index):
        return (go(src, all_ref.at[index], ahead_b), go(src, all_ref.at[index], behind_b))

    def across(src, index):
        return go(src, all_ref.at[index], sibling)

    b_copies = {0: along_b(own_ref, me)}
    others = [across(own_ref, me)]
    from_behind = plane_index(a - 1, b, core)
    from_ahead = plane_index(a + 1, b, core)
    from_far = plane_index(a + 2, b, core)
    a_ahead.wait_recv()
    far_top = go(all_ref.at[from_behind, top], all_ref.at[from_behind, top], ahead_a)
    a_behind.wait_recv()
    far_bottom = go(all_ref.at[from_ahead, bottom], all_ref.at[from_ahead, bottom], behind_a)
    b_copies[1] = along_b(all_ref.at[from_behind], from_behind)
    others.append(across(all_ref.at[from_behind], from_behind))
    b_copies[2] = along_b(all_ref.at[from_ahead], from_ahead)
    others.append(across(all_ref.at[from_ahead], from_ahead))
    column = (a, a - 1, a + 1, a + 2)
    fars = {}

    def onward(k):
        below = plane_index(column[k], b - 1, core)
        above = plane_index(column[k], b + 1, core)
        b_copies[k][0].wait_recv()
        first = go(all_ref.at[below, top], all_ref.at[below, top], ahead_b)
        b_copies[k][1].wait_recv()
        second = go(all_ref.at[above, bottom], all_ref.at[above, bottom], behind_b)
        fars[k] = (first, second)
        others.append(across(all_ref.at[below], below))
        others.append(across(all_ref.at[above], above))

    onward(0)
    far_top.wait_recv()
    far_bottom.wait_recv()
    b_copies[3] = along_b(all_ref.at[from_far], from_far)
    others.append(across(all_ref.at[from_far], from_far))
    onward(1)
    onward(2)
    onward(3)
    for k in range(4):
        index = plane_index(column[k], b + 2, core)
        fars[k][0].wait_recv()
        fars[k][1].wait_recv()
        others.append(across(all_ref.at[index], index))
    for copy in others:
        copy.wait_recv()


PLANE_COPIES = 36


def plane_gather_kernel(own_ref, all_ref, send_sems, recv_sems, local_sem):
    me = lax.axis_index("ep")
    greet(plane_partners())
    post = Post(send_sems, recv_sems)
    local = pltpu.make_async_copy(own_ref, all_ref.at[me], local_sem)
    local.start()
    plane_gather_body(post, own_ref, all_ref)
    post.finish()
    local.wait()


def plane_gather(own, number):
    return pl.pallas_call(
        plane_gather_kernel,
        out_shape=jax.ShapeDtypeStruct((32,) + own.shape, own.dtype),
        in_specs=[ANY],
        out_specs=ANY,
        scratch_shapes=[
            pltpu.SemaphoreType.DMA((PLANE_COPIES,)),
            pltpu.SemaphoreType.DMA((PLANE_COPIES,)),
            pltpu.SemaphoreType.DMA,
        ],
        compiler_params=pltpu.CompilerParams(collective_id=number, has_side_effects=True),
        name="plane_gather",
    )(own)


def add_rows(dst, sources, start, rows):
    step = 16

    @pl.loop(0, rows // step)
    def _(i):
        at = pl.multiple_of(i * step, step)
        total = None
        for ref, first in sources:
            part = ref[pl.ds(first + at, step), :].astype(F32)
            total = part if total is None else total + part
        dst[pl.ds(start + at, step), :] = total.astype(dst.dtype)


def plane_scatter_body(post, parts_ref, sum_ref, scratch):
    mine, other, b_far, b_near, a_far, a_near, local_sems = scratch
    a, b, core = plane_place()
    ahead_a, behind_a, ahead_b, behind_b, sibling = plane_partners()
    rows = mine.shape[2]
    top, bottom = halves(rows)
    high = top.size
    low = rows - high
    offsets = (2, 1, -1, 0)
    go = post.go
    loads, crossing = {}, {}
    order = [(k, 0) for k in range(4)] + [(k, j) for k in range(4) for j in (1, 2)]
    order += [(k, 3) for k in range(4)]
    for number, (k, j) in enumerate(order):
        there = plane_index(b + offsets[k], a + offsets[j], 1 - core)
        crossing[k, j] = go(parts_ref.at[there], other.at[k, j], sibling)
        here = plane_index(a + offsets[k], b + offsets[j], core)
        loads[k, j] = pltpu.make_async_copy(
            parts_ref.at[here], mine.at[k, j], local_sems.at[number]
        )
        loads[k, j].start()

    def ready(k, j):
        crossing[k, j].wait_recv()
        loads[k, j].wait()

    far_b, near_b = {}, {}
    for k in range(4):
        ready(k, 0)
        block, extra = mine.at[k, 0], other.at[k, 0]
        add_rows(block, [(block, 0), (extra, 0)], 0, rows)
        far_b[k] = (
            go(block.at[top], b_far.at[k, top], ahead_b),
            go(block.at[bottom], b_far.at[k, bottom], behind_b),
        )
    for k in range(4):
        far = b_far.at[k]
        ready(k, 1)
        block, extra = mine.at[k, 1], other.at[k, 1]
        far_b[k][0].wait_recv()
        add_rows(block, [(block, 0), (extra, 0), (far, 0)], 0, high)
        add_rows(block, [(block, high), (extra, high)], high, low)
        first = go(block, b_near.at[0, k], ahead_b)
        ready(k, 2)
        block, extra = mine.at[k, 2], other.at[k, 2]
        far_b[k][1].wait_recv()
        add_rows(block, [(block, 0), (extra, 0)], 0, high)
        add_rows(block, [(block, high), (extra, high), (far, high)], high, low)
        near_b[k] = (first, go(block, b_near.at[1, k], behind_b))
    far_a, near_a = [], []
    for k in range(4):
        ready(k, 3)
        block, extra = mine.at[k, 3], other.at[k, 3]
        near_b[k][0].wait_recv()
        near_b[k][1].wait_recv()
        base = [block, extra, b_near.at[0, k], b_near.at[1, k]]
        upper = [(ref, 0) for ref in base]
        lower = [(ref, high) for ref in base]
        if k == 0:
            add_rows(block, upper, 0, high)
            add_rows(block, lower, high, low)
            far_a = [
                go(block.at[top], a_far.at[top], ahead_a),
                go(block.at[bottom], a_far.at[bottom], behind_a),
            ]
        elif k == 1:
            far_a[0].wait_recv()
            add_rows(block, upper + [(a_far, 0)], 0, high)
            add_rows(block, lower, high, low)
            near_a.append(go(block, a_near.at[0], ahead_a))
        elif k == 2:
            far_a[1].wait_recv()
            add_rows(block, upper, 0, high)
            add_rows(block, lower + [(a_far, high)], high, low)
            near_a.append(go(block, a_near.at[1], behind_a))
        else:
            near_a[0].wait_recv()
            near_a[1].wait_recv()
            add_rows(sum_ref, upper + [(a_near.at[0], 0), (a_near.at[1], 0)], 0, rows)


def plane_scatter_scratch(rows, columns, kind):
    return [
        pltpu.VMEM((4, 4, rows, columns), kind),
        pltpu.VMEM((4, 4, rows, columns), kind),
        pltpu.VMEM((4, rows, columns), kind),
        pltpu.VMEM((2, 4, rows, columns), kind),
        pltpu.VMEM((rows, columns), kind),
        pltpu.VMEM((2, rows, columns), kind),
        pltpu.SemaphoreType.DMA((16,)),
    ]


def plane_scatter_kernel(parts_ref, sum_ref, *rest):
    post = Post(rest[-2], rest[-1])
    greet(plane_partners())
    plane_scatter_body(post, parts_ref, sum_ref, rest[:-2])
    post.finish()


def plane_scatter(parts, number):
    _, rows, columns = parts.shape
    return pl.pallas_call(
        plane_scatter_kernel,
        out_shape=jax.ShapeDtypeStruct((rows, columns), F32),
        in_specs=[ANY],
        out_specs=VMEM,
        scratch_shapes=plane_scatter_scratch(rows, columns, parts.dtype)
        + [
            pltpu.SemaphoreType.DMA((PLANE_COPIES,)),
            pltpu.SemaphoreType.DMA((PLANE_COPIES,)),
        ],
        compiler_params=pltpu.CompilerParams(
            collective_id=number, has_side_effects=True, vmem_limit_bytes=56 << 20
        ),
        name="plane_scatter",
    )(parts)


def everywhere_kernel(
    dense_ref, small_ref, dense_out, small_out, dense_own, small_own, small_line, small_sum, *rest
):
    post = Post(rest[-2], rest[-1])
    me = lax.axis_index("ep")
    ahead, behind = line_partners()
    tp = lax.axis_index("tp")
    ep = lax.axis_index("ep")
    across = (ep, wrap(tp + 2))
    greet(plane_partners() + (ahead, behind, across))
    plane_scatter_body(post, small_ref, small_own, rest[7:14])
    line = [
        post.go(small_own, small_line.at[0], ahead),
        post.go(small_own, small_line.at[1], behind),
        post.go(small_own, small_line.at[2], across),
    ]
    plane_scatter_body(post, dense_ref, dense_own, rest[:7])
    for copy in line:
        copy.wait_recv()
    small_sum[...] = small_own[...] + small_line[0] + small_line[1] + small_line[2]
    small_out[me] = small_sum[...]
    dense_out[me] = dense_own[...]
    plane_gather_body(post, small_sum, small_out)
    plane_gather_body(post, dense_own, dense_out)
    post.finish()


def everywhere(dense, small, number):
    _, rows, columns = dense.shape
    _, small_rows, small_columns = small.shape
    copies = 4 * PLANE_COPIES + 3
    return pl.pallas_call(
        everywhere_kernel,
        out_shape=[
            jax.ShapeDtypeStruct(dense.shape, dense.dtype),
            jax.ShapeDtypeStruct(small.shape, small.dtype),
        ],
        in_specs=[VMEM, VMEM],
        out_specs=[VMEM, VMEM],
        scratch_shapes=[
            pltpu.VMEM((rows, columns), dense.dtype),
            pltpu.VMEM((small_rows, small_columns), F32),
            pltpu.VMEM((3, small_rows, small_columns), F32),
            pltpu.VMEM((small_rows, small_columns), F32),
        ]
        + plane_scatter_scratch(rows, columns, dense.dtype)
        + plane_scatter_scratch(small_rows, small_columns, F32)
        + [pltpu.SemaphoreType.DMA((copies,)), pltpu.SemaphoreType.DMA((copies,))],
        compiler_params=pltpu.CompilerParams(
            collective_id=number, has_side_effects=True, vmem_limit_bytes=48 << 20
        ),
        name="everywhere",
    )(dense, small)


def line_gather_kernel(own_ref, all_ref, send_sems, recv_sems, local_sem):
    tp = lax.axis_index("tp")
    ahead, behind = line_partners()
    top, bottom = halves(own_ref.shape[0])
    greet((ahead, behind))
    post = Post(send_sems, recv_sems)
    local = pltpu.make_async_copy(own_ref, all_ref.at[tp], local_sem)
    local.start()
    first = post.go(own_ref, all_ref.at[tp], ahead)
    second = post.go(own_ref, all_ref.at[tp], behind)
    before, after = wrap(tp - 1), wrap(tp + 1)
    first.wait_recv()
    third = post.go(all_ref.at[before, top], all_ref.at[before, top], ahead)
    second.wait_recv()
    fourth = post.go(all_ref.at[after, bottom], all_ref.at[after, bottom], behind)
    third.wait_recv()
    fourth.wait_recv()
    post.finish()
    local.wait()


def line_gather(own, number):
    return pl.pallas_call(
        line_gather_kernel,
        out_shape=jax.ShapeDtypeStruct((4,) + own.shape, own.dtype),
        in_specs=[ANY],
        out_specs=ANY,
        scratch_shapes=[
            pltpu.SemaphoreType.DMA((4,)),
            pltpu.SemaphoreType.DMA((4,)),
            pltpu.SemaphoreType.DMA,
        ],
        compiler_params=pltpu.CompilerParams(collective_id=number, has_side_effects=True),
        name="line_gather",
    )(own)


def line_scatter_kernel(parts_ref, sum_ref, mine, far, near, send_sems, recv_sems, local_sems):
    tp = lax.axis_index("tp")
    ahead, behind = line_partners()
    rows = mine.shape[1]
    top, bottom = halves(rows)
    high = top.size
    low = rows - high
    loads = []
    for number, offset in enumerate((2, 1, -1, 0)):
        load = pltpu.make_async_copy(
            parts_ref.at[wrap(tp + offset)], mine.at[number], local_sems.at[number]
        )
        load.start()
        loads.append(load)
    greet((ahead, behind))
    post = Post(send_sems, recv_sems)
    there = wrap(tp + 2)
    first = post.go(parts_ref.at[there, top], far.at[top], ahead)
    second = post.go(parts_ref.at[there, bottom], far.at[bottom], behind)
    loads[0].wait()
    loads[1].wait()
    block = mine.at[1]
    first.wait_recv()
    add_rows(block, [(block, 0), (far, 0)], 0, high)
    third = post.go(block, near.at[0], ahead)
    loads[2].wait()
    block = mine.at[2]
    second.wait_recv()
    add_rows(block, [(block, high), (far, high)], high, low)
    fourth = post.go(block, near.at[1], behind)
    loads[3].wait()
    third.wait_recv()
    fourth.wait_recv()
    add_rows(sum_ref, [(mine.at[3], 0), (near.at[0], 0), (near.at[1], 0)], 0, rows)
    post.finish()


def line_scatter(parts, number):
    _, rows, columns = parts.shape
    kind = parts.dtype
    return pl.pallas_call(
        line_scatter_kernel,
        out_shape=jax.ShapeDtypeStruct((rows, columns), F32),
        in_specs=[ANY],
        out_specs=VMEM,
        scratch_shapes=[
            pltpu.VMEM((4, rows, columns), kind),
            pltpu.VMEM((rows, columns), kind),
            pltpu.VMEM((2, rows, columns), kind),
            pltpu.SemaphoreType.DMA((4,)),
            pltpu.SemaphoreType.DMA((4,)),
            pltpu.SemaphoreType.DMA((4,)),
        ],
        compiler_params=pltpu.CompilerParams(
            collective_id=number, has_side_effects=True, vmem_limit_bytes=32 << 20
        ),
        name="line_scatter",
    )(parts)


def exchange(values):
    return jnp.concatenate([values[:, 64:], values[:, :64]], axis=1)


def head_pairs(block):
    rows = block.shape[0]
    low = lax.broadcasted_iota(jnp.int32, (rows, 128), 1) < 64
    left, right = block[:, :128], block[:, 128:]
    zero = jnp.zeros_like(left)
    straight = jnp.concatenate([jnp.where(low, left, zero), jnp.where(low, zero, right)], axis=0)
    crossed = jnp.concatenate([jnp.where(low, zero, left), jnp.where(low, right, zero)], axis=0)
    return (straight, crossed)


def heads_back(straight, crossed):
    rows = straight.shape[0] // 2
    low = lax.broadcasted_iota(jnp.int32, (rows, 128), 1) < 64
    left = jnp.where(low, straight[:rows], crossed[:rows])
    right = jnp.where(low, crossed[rows:], straight[rows:])
    return jnp.concatenate([left, right], axis=1)


def attend_kernel(query, keys, values, seg_column, seg_row, live_row, mixed):
    rows = query.shape[0]
    start = pl.program_id(0) * rows
    total = keys.shape[0]
    position = start + lax.broadcasted_iota(jnp.int32, (rows, total), 0)
    key_position = lax.broadcasted_iota(jnp.int32, (rows, total), 1)
    allowed = (seg_column[...] == seg_row[...]) & (
        (live_row[...] == 1) | (position == key_position)
    )
    bias = jnp.where(allowed, 0.0, -1e30).astype(F32)
    outs = []
    for pair, key_part, value_part in zip(
        head_pairs(query[...]),
        (keys[...], exchange(keys[...])),
        (values[...], exchange(values[...])),
        strict=True,
    ):
        halves_out = []
        for number in range(2):
            part = pair[number * rows : (number + 1) * rows]
            scores = lax.dot_general(part, key_part, CONTRACT_LAST, preferred_element_type=F32)
            weights = jnp.exp(scores * 0.125 + bias)
            total_weight = jnp.sum(weights, axis=1, keepdims=True)
            out = jnp.dot(weights.astype(BF16), value_part, preferred_element_type=F32)
            halves_out.append(out / total_weight)
        outs.append(jnp.concatenate(halves_out, axis=0))
    mixed[...] = heads_back(*outs).astype(BF16)


def attend(query, keys, values, seg_column, seg_row, live_row):
    total, width = query.shape
    rows = 256
    return pl.pallas_call(
        attend_kernel,
        out_shape=jax.ShapeDtypeStruct((total, width), BF16),
        grid=(total // rows,),
        in_specs=[
            pl.BlockSpec((rows, width), lambda i: (i, 0)),
            pl.BlockSpec((total, 128), lambda i: (0, 0)),
            pl.BlockSpec((total, 128), lambda i: (0, 0)),
            pl.BlockSpec((rows, 1), lambda i: (i, 0)),
            pl.BlockSpec((1, total), lambda i: (0, 0)),
            pl.BlockSpec((1, total), lambda i: (0, 0)),
        ],
        out_specs=pl.BlockSpec((rows, width), lambda i: (i, 0)),
        compiler_params=pltpu.CompilerParams(vmem_limit_bytes=48 << 20),
        name="attend",
    )(query, keys, values, seg_column, seg_row, live_row)


def attend_back_kernel(
    query, grad, keys, values, seg_column, seg_row, live_column,
    grad_query, grad_keys, grad_values, keys_sum, values_sum,
):
    rows = query.shape[0]
    step = pl.program_id(0)
    total = keys.shape[0]
    key_position = lax.broadcasted_iota(jnp.int32, (total, rows), 0)
    position = step * rows + lax.broadcasted_iota(jnp.int32, (total, rows), 1)
    allowed = (seg_column[...] == seg_row[...]) & (
        (live_column[...] == 1) | (position == key_position)
    )
    bias = jnp.where(allowed, 0.0, -1e30).astype(F32)

    @pl.when(step == 0)
    def _():
        keys_sum[...] = jnp.zeros_like(keys_sum)
        values_sum[...] = jnp.zeros_like(values_sum)

    query_pairs = head_pairs(query[...])
    grad_pairs = head_pairs(grad[...])
    key_parts = (keys[...], exchange(keys[...]))
    value_parts = (values[...], exchange(values[...]))
    outs = []
    for side in range(2):
        halves_out = []
        for number in range(2):
            part = query_pairs[side][number * rows : (number + 1) * rows]
            grad_part = grad_pairs[side][number * rows : (number + 1) * rows]
            scores = lax.dot_general(
                key_parts[side], part, CONTRACT_LAST, preferred_element_type=F32
            )
            raw = jnp.exp(scores * 0.125 + bias)
            weights = raw * (1.0 / jnp.sum(raw, axis=0, keepdims=True))
            grad_weights = lax.dot_general(
                value_parts[side], grad_part, CONTRACT_LAST, preferred_element_type=F32
            )
            inner = jnp.sum(weights * grad_weights, axis=0, keepdims=True)
            grad_scores = (weights * (grad_weights - inner)).astype(BF16)
            halves_out.append(
                lax.dot_general(
                    grad_scores, key_parts[side], CONTRACT_ROWS, preferred_element_type=F32
                )
            )
            keys_sum[side] += jnp.dot(grad_scores, part, preferred_element_type=F32)
            values_sum[side] += jnp.dot(
                weights.astype(BF16), grad_part, preferred_element_type=F32
            )
        outs.append(jnp.concatenate(halves_out, axis=0))
    grad_query[...] = heads_back(*outs) * 0.125

    @pl.when(step == pl.num_programs(0) - 1)
    def _():
        grad_keys[...] = (keys_sum[0] + exchange(keys_sum[1])) * 0.125
        grad_values[...] = (values_sum[0] + exchange(values_sum[1])).astype(BF16)


def attend_back(query, grad, keys, values, seg_column, seg_row, live_column):
    total, width = query.shape
    rows = 256
    return pl.pallas_call(
        attend_back_kernel,
        out_shape=[
            jax.ShapeDtypeStruct((total, width), F32),
            jax.ShapeDtypeStruct((total, 128), F32),
            jax.ShapeDtypeStruct((total, 128), BF16),
        ],
        grid=(total // rows,),
        in_specs=[
            pl.BlockSpec((rows, width), lambda i: (i, 0)),
            pl.BlockSpec((rows, width), lambda i: (i, 0)),
            pl.BlockSpec((total, 128), lambda i: (0, 0)),
            pl.BlockSpec((total, 128), lambda i: (0, 0)),
            pl.BlockSpec((total, 1), lambda i: (0, 0)),
            pl.BlockSpec((1, rows), lambda i: (0, i)),
            pl.BlockSpec((total, 1), lambda i: (0, 0)),
        ],
        out_specs=[
            pl.BlockSpec((rows, width), lambda i: (i, 0)),
            pl.BlockSpec((total, 128), lambda i: (0, 0)),
            pl.BlockSpec((total, 128), lambda i: (0, 0)),
        ],
        scratch_shapes=[pltpu.VMEM((2, total, 128), F32), pltpu.VMEM((2, total, 128), F32)],
        compiler_params=pltpu.CompilerParams(vmem_limit_bytes=48 << 20),
        name="attend_back",
    )(query, grad, keys, values, seg_column, seg_row, live_column)


GROUP = 4


def split_float(values):
    high = values.astype(BF16)
    return (high, (values - high.astype(F32)).astype(BF16))


def experts_kernel(
    number_ref, rows_ref, grads_ref, pair_ref, down_ref,
    out_ref, back_ref, weight_grads_ref,
    gate_full, up_full, gate_sum, up_sum, down_sum, rows_own, grads_own, gates_own, select,
):
    step = pl.program_id(0)
    expert = number_ref[0]
    lane_row = lax.rem(expert, 16)
    upper = expert >= 16

    @pl.when(step == 0)
    def _():
        for part in range(4):
            columns = slice(part * 128, (part + 1) * 128)
            gate_full[:, columns] = pair_ref[part, :1024, :]
            up_full[:, columns] = pair_ref[part, 1024:, :]
        gate_sum[...] = jnp.zeros_like(gate_sum)
        up_sum[...] = jnp.zeros_like(up_sum)
        down_sum[...] = jnp.zeros_like(down_sum)

    earlier = (
        lax.broadcasted_iota(jnp.int32, (256, 256), 0)
        <= lax.broadcasted_iota(jnp.int32, (256, 256), 1)
    ).astype(BF16)
    slot = lax.broadcasted_iota(jnp.int32, (SLOTS, 256), 0).astype(F32)
    extra_row = lax.broadcasted_iota(jnp.int32, (EXTRA, 1024), 0) == lane_row
    for part in range(GROUP):
        extras = jnp.where(extra_row, rows_ref[part, 256:, :].astype(F32), 0.0)
        extras = jnp.sum(extras, axis=0, keepdims=True)
        gates = jnp.where(
            upper, extras[:, 512:768] + extras[:, 768:], extras[:, :256] + extras[:, 256:512]
        )
        named = jnp.broadcast_to(gates, (16, 256)) > 0.0
        rank = jnp.dot(named.astype(BF16), earlier, preferred_element_type=F32)[:1] - 1.0
        chosen = (slot == rank) & (gates > 0.0)
        chosen_low = chosen.astype(BF16)
        at = slice(part * SLOTS, (part + 1) * SLOTS)
        select[at, :] = chosen_low
        rows_own[at, :] = jnp.dot(
            chosen_low, rows_ref[part, :256, :], preferred_element_type=F32
        ).astype(BF16)
        grads_own[at, :] = jnp.dot(
            chosen_low, grads_ref[part], preferred_element_type=F32
        ).astype(BF16)
        gates_own[at, :] = jnp.sum(jnp.where(chosen, gates, 0.0), axis=1, keepdims=True)

    rows_in = rows_own[...]
    gate_pre = jnp.dot(rows_in, gate_full[...], preferred_element_type=F32)
    up_pre = jnp.dot(rows_in, up_full[...], preferred_element_type=F32)
    sigmoid = 1.0 / (1.0 + jnp.exp(-gate_pre))
    silu = gate_pre * sigmoid
    act = (silu * up_pre).astype(BF16)
    out = jnp.dot(act, down_ref[...], preferred_element_type=F32).astype(BF16).astype(F32)
    gate_factor = gates_own[...]
    grads_in = grads_own[...].astype(F32)
    grad_gates = jnp.sum(grads_in * out, axis=1, keepdims=True)
    weighted = (gate_factor * out).astype(BF16)
    grad_out = (gate_factor * grads_in).astype(BF16)
    grad_act = lax.dot_general(
        grad_out, down_ref[...], CONTRACT_LAST, preferred_element_type=F32
    )
    down_sum[...] += lax.dot_general(
        grad_out, act, CONTRACT_ROWS, preferred_element_type=F32
    )
    grad_gate_pre = (grad_act * up_pre * sigmoid * (1.0 + gate_pre * (1.0 - sigmoid))).astype(BF16)
    grad_up_pre = (grad_act * silu).astype(BF16)
    gate_sum[...] += lax.dot_general(
        rows_in, grad_gate_pre, CONTRACT_ROWS, preferred_element_type=F32
    )
    up_sum[...] += lax.dot_general(
        rows_in, grad_up_pre, CONTRACT_ROWS, preferred_element_type=F32
    )
    grad_rows = lax.dot_general(
        grad_gate_pre, gate_full[...], CONTRACT_LAST, preferred_element_type=F32
    )
    grad_rows = grad_rows + lax.dot_general(
        grad_up_pre, up_full[...], CONTRACT_LAST, preferred_element_type=F32
    )
    grad_rows = grad_rows.astype(BF16)
    nothing = jnp.zeros((1, 512), F32)
    for part in range(GROUP):
        at = slice(part * SLOTS, (part + 1) * SLOTS)
        chosen_low = select[at, :]
        out_ref[part] = lax.dot_general(
            chosen_low, weighted[at], CONTRACT_ROWS, preferred_element_type=F32
        ).astype(BF16)
        back_ref[part, :256, :] = lax.dot_general(
            chosen_low, grad_rows[at], CONTRACT_ROWS, preferred_element_type=F32
        ).astype(BF16)
        spread = jnp.sum(chosen_low.astype(F32) * grad_gates[at], axis=0, keepdims=True)
        high = spread.astype(BF16).astype(F32)
        both = jnp.concatenate([high, spread - high], axis=1)
        line = jnp.concatenate(
            [jnp.where(upper, nothing, both), jnp.where(upper, both, nothing)], axis=1
        )
        back_ref[part, 256:, :] = jnp.where(extra_row, line, 0.0).astype(BF16)

    @pl.when(step == pl.num_programs(0) - 1)
    def _():
        for part in range(4):
            columns = slice(part * 128, (part + 1) * 128)
            weight_grads_ref[part, :1024, :] = gate_sum[:, columns].astype(BF16)
            weight_grads_ref[part, 1024:2048, :] = up_sum[:, columns].astype(BF16)
            weight_grads_ref[part, 2048:, :] = down_sum[:, columns].astype(BF16)


def run_experts(number, rows, grads, pair, down):
    sources = rows.shape[0]
    count = GROUP * SLOTS
    return pl.pallas_call(
        experts_kernel,
        out_shape=[
            jax.ShapeDtypeStruct((sources, 256, 1024), BF16),
            jax.ShapeDtypeStruct((sources, 256 + EXTRA, 1024), BF16),
            jax.ShapeDtypeStruct((4, 3072, 128), BF16),
        ],
        grid=(sources // GROUP,),
        in_specs=[
            pl.BlockSpec(memory_space=pltpu.SMEM),
            pl.BlockSpec((GROUP, 256 + EXTRA, 1024), lambda i: (i, 0, 0)),
            pl.BlockSpec((GROUP, 256, 1024), lambda i: (i, 0, 0)),
            pl.BlockSpec((4, 2048, 128), lambda i: (0, 0, 0)),
            pl.BlockSpec((512, 1024), lambda i: (0, 0)),
        ],
        out_specs=[
            pl.BlockSpec((GROUP, 256, 1024), lambda i: (i, 0, 0)),
            pl.BlockSpec((GROUP, 256 + EXTRA, 1024), lambda i: (i, 0, 0)),
            pl.BlockSpec((4, 3072, 128), lambda i: (0, 0, 0)),
        ],
        scratch_shapes=[
            pltpu.VMEM((1024, 512), BF16),
            pltpu.VMEM((1024, 512), BF16),
            pltpu.VMEM((1024, 512), F32),
            pltpu.VMEM((1024, 512), F32),
            pltpu.VMEM((1024, 512), F32),
            pltpu.VMEM((count, 1024), BF16),
            pltpu.VMEM((count, 1024), BF16),
            pltpu.VMEM((count, 1), F32),
            pltpu.VMEM((count, 256), BF16),
        ],
        compiler_params=pltpu.CompilerParams(vmem_limit_bytes=60 << 20),
        name="run_experts",
    )(number, rows, grads, pair, down)


def norm_rows(values, gain_vec, epsilon):
    return (
        values * lax.rsqrt(jnp.mean(values * values, axis=-1, keepdims=True) + epsilon) * gain_vec
    )


def norm_plain(values, gain_vec):
    return norm_rows(values, gain_vec, 1e-05)


def rotate(values, cosine_table, sine_table):
    half_dim = values.shape[-1] // 2
    first_half = values[..., :half_dim]
    second_half = values[..., half_dim:]
    return jnp.concatenate(
        [
            first_half * cosine_table - second_half * sine_table,
            second_half * cosine_table + first_half * sine_table,
        ],
        axis=-1,
    )


def rotary_tables(row_total, head_dim, seq_len):
    half_dim = head_dim // 2
    position = (jnp.arange(row_total) % seq_len).astype(jnp.float32)
    frequency = 10000.0 ** (-(jnp.arange(half_dim).astype(jnp.float32) * 2.0) / head_dim)
    angles = position[:, None] * frequency[None, :]
    return (jnp.cos(angles)[:, None, :], jnp.sin(angles)[:, None, :])


def prepare(query_raw, key_raw, query_scale, key_scale, cosine_table, sine_table, head_dim):
    row_total = query_raw.shape[0]
    query_heads = norm_rows(query_raw.reshape(row_total, -1, head_dim), query_scale, 1e-06)
    key_heads = norm_rows(key_raw.reshape(row_total, -1, head_dim), key_scale, 1e-06)
    query_rot = rotate(query_heads, cosine_table, sine_table).reshape(row_total, -1)
    key_rot = rotate(key_heads, cosine_table, sine_table).reshape(row_total, -1)
    return (query_rot, key_rot)


def gate_lines(table):
    high, low = split_float(table.T)
    return jnp.concatenate([high[:16], low[:16], high[16:], low[16:]], axis=1)


def gate_table(lines):
    first = lines[:, :256] + lines[:, 256:512]
    second = lines[:, 512:768] + lines[:, 768:]
    return jnp.concatenate([first, second], axis=0).T


def shards(
    inputs,
    first_gain,
    query_weight,
    key_weight,
    value_weight,
    query_gain,
    key_gain,
    output_weight,
    second_gain,
    router_weight,
    gate_weight,
    up_weight,
    down_weight,
    segments,
    live_mask,
    routes,
    cotangent,
):
    row_count, model_width = inputs.shape
    head_dim = query_gain.shape[0]
    experts = router_weight.shape[1]
    gain_one = first_gain.astype(F32)
    gain_two = second_gain.astype(F32)
    query_scale = query_gain.astype(F32)
    key_scale = key_gain.astype(F32)
    router_float = router_weight.astype(F32)
    hidden = inputs.astype(F32)
    grad_all = lax.all_gather(cotangent, "ep", axis=0)
    pair = jnp.concatenate([gate_weight[0], up_weight[0]], axis=0)
    pair_all = lax.all_gather(pair, "tp", axis=0)
    down_all = lax.all_gather(down_weight[0], "tp", axis=0, tiled=True)

    normed_one = norm_plain(hidden, gain_one)
    gathered = line_gather(normed_one.astype(BF16), 1).reshape(-1, model_width)
    group_rows = gathered.shape[0]
    query_raw = jnp.dot(gathered, query_weight, preferred_element_type=F32)
    key_raw = jnp.dot(gathered, key_weight, preferred_element_type=F32)
    value_raw = jnp.dot(gathered, value_weight, preferred_element_type=F32)
    cosine_table, sine_table = rotary_tables(group_rows, head_dim, SEQ_LEN)

    def prepare_local(query_part, key_part, query_factor, key_factor):
        return prepare(
            query_part, key_part, query_factor, key_factor, cosine_table, sine_table, head_dim
        )

    (query_rot, key_rot), prepare_back = jax.vjp(
        prepare_local, query_raw, key_raw, query_scale, key_scale
    )
    query_low = query_rot.astype(BF16)
    key_low = key_rot.astype(BF16)
    value_low = value_raw.astype(BF16)
    seg_column, seg_row = segments.reshape(-1, 1), segments.reshape(1, -1)
    live_column, live_row = live_mask.reshape(-1, 1), live_mask.reshape(1, -1)
    mixed_heads = attend(query_low, key_low, value_low, seg_column, seg_row, live_row)
    attended = line_scatter(
        jnp.dot(mixed_heads, output_weight, preferred_element_type=F32)
        .astype(BF16)
        .reshape(-1, row_count, model_width),
        2,
    )
    residual = hidden + attended
    normed_two, norm_two_back = jax.vjp(norm_plain, residual, gain_two)
    logits = jnp.dot(normed_two, router_float, precision=HIGHEST_PRECISION)
    named = jnp.any(routes[:, :, None] == jnp.arange(experts)[None, None, :], axis=1)
    top_logit = jnp.max(jnp.where(named, logits, -jnp.inf), axis=1, keepdims=True)
    raised = jnp.where(named, jnp.exp(jnp.where(named, logits - top_logit, 0.0)), 0.0)
    gate_probs = raised / jnp.sum(raised, axis=1, keepdims=True)
    block = jnp.concatenate([normed_two.astype(BF16), gate_lines(gate_probs)], axis=0)
    rows_all = plane_gather(block, 3)
    number = lax.axis_index("ep").astype(jnp.int32).reshape(1)
    out_parts, back_parts, weight_parts = run_experts(
        number, rows_all, grad_all, pair_all, down_all
    )
    back_sum = plane_scatter(back_parts, 4)
    combined = lax.psum_scatter(out_parts, "ep", scatter_dimension=0).astype(F32)
    weight_sums = lax.psum_scatter(weight_parts, "tp", scatter_dimension=0).astype(F32)
    result = (residual + combined).astype(BF16)
    grad_out = cotangent.astype(F32)
    grad_gates = gate_table(back_sum[row_count:])
    grad_logits = gate_probs * (
        grad_gates - jnp.sum(gate_probs * grad_gates, axis=-1, keepdims=True)
    )
    grad_normed_two = back_sum[:row_count] + lax.dot_general(
        grad_logits, router_float, CONTRACT_LAST, precision=HIGHEST_PRECISION
    )
    grad_router = lax.dot_general(
        normed_two, grad_logits, CONTRACT_ROWS, precision=HIGHEST_PRECISION
    )
    grad_residual_norm, grad_gain_two = norm_two_back(grad_normed_two)
    grad_residual = grad_out + grad_residual_norm
    grad_attn_all = line_gather(grad_residual.astype(BF16), 5).reshape(-1, model_width)
    grad_output_mat = lax.dot_general(
        mixed_heads, grad_attn_all, CONTRACT_ROWS, preferred_element_type=F32
    )
    grad_mixed = lax.dot_general(
        grad_attn_all, output_weight, CONTRACT_LAST, preferred_element_type=F32
    ).astype(BF16)
    grad_query, grad_keys, grad_value_low = attend_back(
        query_low, grad_mixed, key_low, value_low, seg_column, seg_row, live_column
    )
    grad_query_raw, grad_key_raw, grad_query_scale, grad_key_scale = prepare_back(
        (grad_query, grad_keys)
    )
    grad_low = jnp.concatenate(
        [grad_query_raw.astype(BF16), grad_key_raw.astype(BF16), grad_value_low], axis=1
    )
    weights_in = jnp.concatenate([query_weight, key_weight, value_weight], axis=1)
    summed = lax.dot_general(grad_low, weights_in, CONTRACT_LAST, preferred_element_type=F32)
    grad_normed_one = line_scatter(
        summed.astype(BF16).reshape(-1, row_count, model_width), 6
    )
    grad_in_mats = lax.dot_general(gathered, grad_low, CONTRACT_ROWS, preferred_element_type=F32)
    unused_norm, norm_one_back = jax.vjp(norm_plain, hidden, gain_one)
    grad_hidden_norm, grad_gain_one = norm_one_back(grad_normed_one)
    grad_inputs = (grad_residual + grad_hidden_norm).astype(BF16)
    dense = jnp.concatenate(
        [grad_in_mats.astype(BF16), grad_output_mat.astype(BF16).reshape(1024, 256)], axis=1
    ).reshape(32, 32, 768)
    small = jnp.concatenate(
        [
            grad_router.reshape(-1),
            grad_gain_one,
            grad_gain_two,
            grad_query_scale,
            grad_key_scale,
        ]
    )
    length = small.shape[0]
    small = jnp.pad(small, (0, 32 * 32 * 128 - length)).reshape(32, 32, 128)
    dense, small = everywhere(dense, small, 7)
    dense = dense.reshape(1024, 768).astype(F32)
    small = small.reshape(-1)
    base = model_width * experts
    return (
        result,
        grad_inputs,
        small[base : base + 1024],
        dense[:, :256],
        dense[:, 256:384],
        dense[:, 384:512],
        small[base + 2048 : base + 2112],
        small[base + 2112 : base + 2176],
        dense[:, 512:].reshape(256, 1024),
        small[base + 1024 : base + 2048],
        small[:base].reshape(model_width, experts),
        weight_sums[None, :1024],
        weight_sums[None, 1024:2048],
        weight_sums[2048:].T[None],
    )


def solution(mesh):
    return jax.shard_map(
        shards,
        mesh=mesh,
        in_specs=(
            P(("ep", "tp"), None),
            P(),
            P(None, "tp"),
            P(None, "tp"),
            P(None, "tp"),
            P(),
            P(),
            P("tp", None),
            P(),
            P(),
            P("ep", None, "tp"),
            P("ep", None, "tp"),
            P("ep", "tp", None),
            P("ep"),
            P("ep"),
            P(("ep", "tp"), None),
            P(("ep", "tp"), None),
        ),
        out_specs=(
            P(("ep", "tp"), None),
            P(("ep", "tp"), None),
            P(),
            P(None, "tp"),
            P(None, "tp"),
            P(None, "tp"),
            P(),
            P(),
            P("tp", None),
            P(),
            P(),
            P("ep", None, "tp"),
            P("ep", None, "tp"),
            P("ep", "tp", None),
        ),
        check_vma=False,
    )
```

time: 983 us -> 495 us (0.50)
  waiting for transfers between devices: 477 us -> 1.99 us
  Pallas kernels: 0 us -> 410 us
  matrix products: 137 us -> 22 us
  local copies, waits for them, and re-layouts: 135 us -> 25.3 us
  other arithmetic: 89.7 us -> 16.5 us
  blocking collectives: 65.2 us -> 0 us
  starting transfers between devices: 49 us -> 0.2 us
    pallas_call x0 -> x10, Pallas kernels: none -> 410 us  [the longest x1 98.6 us: plane_gather(): pl.pallas_call(plane_gather_kernel, out_shape=jax.ShapeDtypeStruct((32,)...]
    psum x2 -> x0, waiting for transfers between devices: 171 us -> none  [the longest x1 96.1 us: shards(): lax.psum(grad_query_mat.astype(jnp.bfloat16), 'ep').astype(jnp.float32)]
    all_to_all x4 -> x0, waiting for transfers between devices: 166 us -> none  [the longest x1 64.1 us: shards(): lax.all_to_all(source_layout(expert_out), 'ep', split_axis=0, concat_axis...]
    dot_general x33 -> x6, matrix products: 128 us -> 12 us  [the longest x1 2.92 us: shards(): lax.dot_general(gathered, grad_low, CONTRACT_ROWS, preferred_element_type...]
    all_gather x5 -> x3, waiting for transfers between devices: 94.2 us -> 0.06 us  [the longest x1 0.02 us: shards(): down_all = lax.all_gather(down_weight[0], 'tp', axis=0, tiled=True)]
    psum x1 -> x0, blocking collectives: 65.2 us -> none  [shards(): lax.psum((grad_gain_one, grad_gain_two, grad_query_scale, grad_key_scale,...]
    all_to_all x4 -> x0, starting transfers between devices: 47.9 us -> none  [the longest x1 14.3 us: shards(): lax.all_to_all(grad_outgoing, 'ep', split_axis=0, concat_axis=0, tiled=True)]
    gather x7 -> x0, local copies, waits for them, and re-layouts: 46.3 us -> none  [the longest x5 17.2 us: shards(): gate_probs = softmax_rows(jnp.take_along_axis(logits, routes, axis=1))]
  transfers between devices with their start and end apart: 16 -> 5, of which waited for: 11 -> 0; matrix products, arithmetic and copies ran while one was open for 26% -> 11% of each run, Pallas kernels for 0% -> 71%
where the time goes in v1:
time: 495 us; the launch traced here: 491 us
  Pallas kernels  410 us (83%)
  local copies, waits for them, and re-layouts  25.3 us (5%)
  matrix products  22 us (4%)
  other arithmetic  16.5 us (3%)
  between operations  15.3 us (3%)
    pallas_call x1, Pallas kernels, plane_gather(): pl.pallas_call(plane_gather_kernel, out_shape=jax.ShapeDtypeStruct((32,)...  98.6 us
    pallas_call x1, Pallas kernels, everywhere(): pl.pallas_call(everywhere_kernel, out_shape=[jax.ShapeDtypeStruct(dense.s...  65.7 us
    pallas_call x1, Pallas kernels, run_experts(): pl.pallas_call(experts_kernel, out_shape=[jax.ShapeDtypeStruct((sources,...  62.3 us
    pallas_call x1, Pallas kernels, plane_scatter(): pl.pallas_call(plane_scatter_kernel, out_shape=jax.ShapeDtypeStruct((rows...  54.7 us
    pallas_call x2, Pallas kernels, line_scatter(): pl.pallas_call(line_scatter_kernel, out_shape=jax.ShapeDtypeStruct((rows,...  51.6 us
    pallas_call x2, Pallas kernels, line_gather(): pl.pallas_call(line_gather_kernel, out_shape=jax.ShapeDtypeStruct((4,) +...  49.5 us
    pallas_call x1, Pallas kernels, attend_back(): pl.pallas_call(attend_back_kernel, out_shape=[jax.ShapeDtypeStruct((total...  20.5 us
  transfers between devices with their start and end apart: 5, of which 0 were waited for; matrix products, arithmetic and copies ran while one was open for 11% of the time, Pallas kernels for 71%

profile of v1, /device:TPU:1, one launch (start us, length us, event | category | flops | bytes accessed | tf_op | source)
XLA Modules:
  0.0 490.8 jit_solution(14246116380853939402)
XLA Ops:
  8.0 1.9 pad_maximum_fusion.3
  11.9 29.6 %line_gather.2 = bf16[4,256,1024]{2,1,0:T(8,128)(2,1)} custom-call(bf16[256,1024]{1,0:T(8,128)(2,1)} %fusion.2.own_ref), custom_call_target="tpu_custom_call" | custom-call | tf_op jit(solution)/shard_map/line_gather/pallas_call | solution.py:394
  41.7 2.4 multiply_reduce_fusion.8
  45.7 2.3 multiply_reduce_fusion.5
  49.5 2.3 convolution_convert_fusion.5.values
  51.8 6.7 %attend.1 = bf16[1024,256]{1,0:T(8,128)(2,1)S(1)} custom-call(bf16[1024,256]{1,0:T(8,128)(2,1)S(1)} %copy.61.query, bf16[1024,128]{1,0:T(8,128)(2,1)S(1)} %copy.62.keys, bf16[1024,128]{1,0:T(8,128)(2,1)S(1)} %convolution_convert_fusion.5.values, s32[1024,1]{1,0:T(8,128)S(1)} %copy.63.seg_column, s32[1,1024]{1,0:T(1,128)S(1)} %bitcast.96, s32[1,1024]{1,0:T(1,128)S(1)} %bitcast.98), custom_call_target="tpu_custom_call" | custom-call | tf_op jit(solution)/shard_map/attend/pallas_call | solution.py:523
  59.2 32.8 %line_scatter.2 = f32[256,1024]{1,0:T(8,128)S(1)} custom-call(bf16[4,256,1024]{2,1,0:T(8,128)(2,1)S(1)} %bitcast.90), custom_call_target="tpu_custom_call" | custom-call | tf_op jit(solution)/shard_map/line_scatter/pallas_call | solution.py:449
  94.7 98.6 %plane_gather.1.rows_ref = bf16[32,272,1024]{2,1,0:T(8,128)(2,1)} custom-call(bf16[272,1024]{1,0:T(8,128)(2,1)} %maximum_maximum_fusion.own_ref), custom_call_target="tpu_custom_call" | custom-call | tf_op jit(solution)/shard_map/plane_gather/pallas_call | solution.py:170
  193.4 62.3 %run_experts.1 = (bf16[32,256,1024]{2,1,0:T(8,128)(2,1)}, bf16[32,272,1024]{2,1,0:T(8,128)(2,1)}, bf16[4,3072,128]{2,1,0:T(8,128)(2,1)}) custom-call(s32[1]{0:T(128)} %bitcast.13.number_ref, bf16[32,272,1024]{2,1,0:T(8,128)(2,1)} %plane_gather.1.rows_ref, bf16[32,256,1024]{2,1,0:T(8,128)(2,1)} %bitcast.100, bf16[4,2048,128]{2,1,0:T(8,128)(2,1)} %bitcast.108, ...), custom_call_target="tpu_custom_call" | custom-call | tf_op jit(solution)/shard_map/run_experts/pallas_call | solution.py:746
  256.6 54.7 %plane_scatter.1 = f32[272,1024]{1,0:T(8,128)} custom-call(bf16[32,272,1024]{2,1,0:T(8,128)(2,1)} %get-tuple-element.23.parts_ref), custom_call_target="tpu_custom_call" | custom-call | tf_op jit(solution)/shard_map/plane_scatter/pallas_call | solution.py:300
  312.1 2.7 fusion.16
  314.8 1.9 reshape.266
  316.7 3.4 multiply_reduce_fusion.1
  320.2 1.0 copy-done.14
  321.2 1.1 fusion.45.own_ref
  322.3 19.9 %line_gather.3 = bf16[4,256,1024]{2,1,0:T(8,128)(2,1)} custom-call(bf16[256,1024]{1,0:T(8,128)(2,1)} %fusion.45.own_ref), custom_call_target="tpu_custom_call" | custom-call | tf_op jit(solution)/shard_map/line_gather/pallas_call | solution.py:394
  342.2 2.3 convolution_convert_fusion.4.grad
  344.5 20.5 %attend_back.1 = (f32[1024,256]{1,0:T(8,128)S(1)}, f32[1024,128]{1,0:T(8,128)S(1)}, bf16[1024,128]{1,0:T(8,128)(2,1)S(1)}) custom-call(bf16[1024,256]{1,0:T(8,128)(2,1)S(1)} %copy.61.query, bf16[1024,256]{1,0:T(8,128)(2,1)S(1)} %convolution_convert_fusion.4.grad, bf16[1024,128]{1,0:T(8,128)(2,1)S(1)} %copy.62.keys, ...), custom_call_target="tpu_custom_call" | custom-call | tf_op jit(solution)/shard_map/attend_back/pallas_call | solution.py:601
  366.8 1.8 copy.68
  368.6 1.0 copy.69
  370.5 1.2 multiply_add_fusion.3
  374.8 1.3 convolution_convert_fusion
  376.1 18.8 %line_scatter.3 = f32[256,1024]{1,0:T(8,128)S(1)} custom-call(bf16[4,256,1024]{2,1,0:T(8,128)(2,1)S(1)} %bitcast.91), custom_call_target="tpu_custom_call" | custom-call | tf_op jit(solution)/shard_map/line_scatter/pallas_call | solution.py:449
  397.7 2.9 convolution_convert_fusion.2
  400.8 65.7 %everywhere.1 = (bf16[32,32,768]{2,1,0:T(8,128)(2,1)S(1)}, f32[32,32,128]{2,1,0:T(8,128)S(1)}) custom-call(bf16[32,32,768]{2,1,0:T(8,128)(2,1)S(1)} %pad_maximum_fusion.dense_ref, f32[32,32,128]{2,1,0:T(8,128)S(1)} %bitcast.92), custom_call_target="tpu_custom_call" | custom-call | tf_op jit(solution)/shard_map/everywhere/pallas_call | solution.py:348
  466.9 1.2 fusion.46
  468.8 1.3 reshape.269
  472.3 2.2 fusion.47
  474.5 1.2 convert_element_type.203
  476.7 2.0 copy.73
  478.7 2.1 fusion.48
  480.8 3.0 fusion.7
  (201 shorter events, 23.2 us)
Async XLA Ops:
  7.2 51.3 %copy-start = (bf16[256,1024]{1,0:T(8,128)(2,1)S(1)}, bf16[256,1024]{1,0:T(8,128)(2,1)}, u32[]{:S(2)}) copy-start(bf16[256,1024]{1,0:T(8,128)(2,1)} %param.24) | copy-start | bytes 1572868
  7.2 3.5 copy-start.60
  7.2 3.5 copy-start.10
  7.2 186.1 %all-gather.11.cloned.1.call-start = ((), (), s32[]{:S(2)}) async-start(), calls=%async_computation.6 | async-start | bytes 1310720 | tf_op jit(solution)/shard_map/all_gather | solution.py:864
  8.0 185.4 %all-gather.9.cloned.1.call-start = ((), (), s32[]{:S(2)}) async-start(), calls=%async_computation.5 | async-start | bytes 2621440 | tf_op jit(solution)/shard_map/all_gather | solution.py:863
  9.9 183.5 %all-gather.7.cloned.1.call-start = ((), (), s32[]{:S(2)}) async-start(), calls=%async_computation.4 | async-start | bytes 17301504 | tf_op jit(solution)/shard_map/all_gather | solution.py:861
  10.6 463.9 %reduce-scatter.5.cloned.1.call-start = ((), (), s32[]{:S(2)}) async-start(), calls=%async_computation.3 | async-start | bytes 3932160 | tf_op jit(solution)/shard_map/reduce_scatter | solution.py:909
  10.7 30.8 %copy-start.32 = (bf16[1024,128]{1,0:T(8,128)(2,1)S(1)}, bf16[1024,128]{1,0:T(8,128)(2,1)}, u32[]{:S(2)}) copy-start(bf16[1024,128]{1,0:T(8,128)(2,1)} %param.20) | copy-start | bytes 786436
  10.9 30.8 %copy-start.62 = (bf16[64]{0:T(256)(128)(2,1)S(1)}, bf16[64]{0:T(256)(128)(2,1)}, u32[]{:S(2)}) copy-start(bf16[64]{0:T(256)(128)(2,1)} %param.23) | copy-start | bytes 388
  41.7 330.0 %copy-start.55 = (f32[64]{0:T(128)}, f32[64]{0:T(128)S(1)}, u32[]{:S(2)}) copy-start(f32[64]{0:T(128)S(1)} %convert_element_type.178) | copy-start | bytes 772
  44.2 327.5 %copy-start.37 = (f32[1024,2]{0,1:T(2,128)}, f32[1024,2]{0,1:T(2,128)S(1)}, u32[]{:S(2)}) copy-start(f32[1024,2]{0,1:T(2,128)S(1)} %fusion.31) | copy-start | bytes 24580
  44.8 3.6 copy-start.21
  45.7 2.4 copy-start.57
  49.0 2.8 copy-start.5
  59.2 32.8 %copy-start.61 = (bf16[1024]{0:T(1024)(128)(2,1)S(1)}, bf16[1024]{0:T(1024)(128)(2,1)}, u32[]{:S(2)}) copy-start(bf16[1024]{0:T(1024)(128)(2,1)} %param.25) | copy-start | bytes 6148
  59.2 32.9 %copy-start.54 = (s32[256,8]{0,1:T(8,128)S(1)}, s32[256,8]{0,1:T(8,128)}, u32[]{:S(2)}) copy-start(s32[256,8]{0,1:T(8,128)} %param.32) | copy-start | bytes 24580
  92.1 228.1 %copy-start.35 = (f32[1024]{0:T(1024)}, f32[1024]{0:T(1024)S(1)}, u32[]{:S(2)}) copy-start(f32[1024]{0:T(1024)S(1)} %convert_element_type.182) | copy-start | bytes 12292
  92.4 227.8 %copy-start.43 = (f32[256]{0:T(256)}, f32[256]{0:T(256)S(1)}, u32[]{:S(2)}) copy-start(f32[256]{0:T(256)S(1)} %fusion.37) | copy-start | bytes 3076
  255.8 225.0 %reduce-scatter.3.cloned.1.call-start = ((), (), s32[]{:S(2)}) async-start(), calls=%async_computation.2 | async-start | bytes 17301504 | tf_op jit(solution)/shard_map/reduce_scatter | solution.py:908
  256.6 55.5 %copy-start.7 = (f32[256,1024]{1,0:T(8,128)S(1)}, f32[256,1024]{1,0:T(8,128)}, u32[]{:S(2)}) copy-start(f32[256,1024]{1,0:T(8,128)} %copy-done.6) | copy-start | bytes 3145732
  316.7 4.5 copy-start.8
  316.7 4.5 copy-start.20
  320.2 22.0 %copy-start.50 = (f32[256]{0:T(256)}, f32[256]{0:T(256)S(1)}, u32[]{:S(2)}) copy-start(f32[256]{0:T(256)S(1)} %multiply_multiply_fusion.8) | copy-start | bytes 3076
  366.8 4.9 copy-start.19
  376.1 18.8 %copy-start.17 = (bf16[4,256,1024]{2,1,0:T(8,128)(2,1)S(1)}, bf16[4,256,1024]{2,1,0:T(8,128)(2,1)}, u32[]{:S(2)}) copy-start(bf16[4,256,1024]{2,1,0:T(8,128)(2,1)} %line_gather.3) | copy-start | bytes 6291460
  468.8 2.3 copy-start.53
  468.8 2.3 copy-start.59
  475.8 5.0 %copy-start.9 = (f32[256,1024]{1,0:T(8,128)S(1)}, f32[256,1024]{1,0:T(8,128)}, u32[]{:S(2)}) copy-start(f32[256,1024]{1,0:T(8,128)} %copy-done.6) | copy-start | bytes 3145732
  475.8 5.0 %copy-start.12 = (bf16[256,1024]{1,0:T(8,128)(2,1)S(1)}, bf16[256,1024]{1,0:T(8,128)(2,1)}, u32[]{:S(2)}) copy-start(bf16[256,1024]{1,0:T(8,128)(2,1)} %param.17) | copy-start | bytes 1572868
  475.8 5.0 %copy-start.36 = (f32[1024]{0:T(1024)S(1)}, f32[1024]{0:T(1024)}, u32[]{:S(2)}) copy-start(f32[1024]{0:T(1024)} %copy-done.35) | copy-start | bytes 12292
  475.8 5.0 %copy-start.44 = (f32[256]{0:T(256)S(1)}, f32[256]{0:T(256)}, u32[]{:S(2)}) copy-start(f32[256]{0:T(256)} %copy-done.43) | copy-start | bytes 3076
  475.8 5.0 %copy-start.51 = (f32[256]{0:T(256)S(1)}, f32[256]{0:T(256)}, u32[]{:S(2)}) copy-start(f32[256]{0:T(256)} %copy-done.50) | copy-start | bytes 3076
  (37 other events, 46.0 us)
Sparse Core Ops, SparseCore 0:
  9.7 31.9 all-gather.10
  43.9 41.1 all-gather.8
  87.4 95.9 all-gather.6
  255.9 34.4 reduce-scatter.4
  294.2 113.6 reduce-scatter.2

commit v2 on v1

v2 whole, which is shorter than its diff:
```python
import jax
import jax.numpy as jnp
import numpy as np
from jax import lax
from jax.experimental import pallas as pl
from jax.experimental.pallas import tpu as pltpu
from jax.sharding import PartitionSpec as P

SEQ_LEN = 1024
HIGHEST_PRECISION = lax.Precision.HIGHEST
CONTRACT_ROWS = (((0,), (0,)), ((), ()))
CONTRACT_LAST = (((1,), (1,)), ((), ()))
MESH = pl.DeviceIdType.MESH
ANY = pl.BlockSpec(memory_space=pl.ANY)
VMEM = pl.BlockSpec(memory_space=pltpu.VMEM)
F32 = jnp.float32
BF16 = jnp.bfloat16
SLOTS = 96
EXTRA = 16


def wrap(value):
    return lax.rem(value + 4, 4)


def pick(core, first, second):
    return first * (1 - core) + second * core


def plane_place():
    ep = lax.axis_index("ep")
    core = lax.rem(ep, 2)
    z = lax.rem(lax.div(ep, 2), 4)
    x = lax.div(ep, 8)
    return (pick(core, x, z), pick(core, z, x), core)


def plane_index(a, b, core):
    a, b = wrap(a), wrap(b)
    return (pick(core, a, b) * 4 + pick(core, b, a)) * 2 + core


def plane_partners():
    a, b, core = plane_place()
    tp = lax.axis_index("tp")
    return (
        (plane_index(a + 1, b, core), tp),
        (plane_index(a - 1, b, core), tp),
        (plane_index(a, b + 1, core), tp),
        (plane_index(a, b - 1, core), tp),
        (plane_index(b, a, 1 - core), tp),
    )


def line_partners():
    ep, tp = lax.axis_index("ep"), lax.axis_index("tp")
    return ((ep, wrap(tp + 1)), (ep, wrap(tp - 1)))


def greet(partners):
    barrier = pltpu.get_barrier_semaphore()
    for partner in partners:
        pl.semaphore_signal(barrier, inc=1, device_id=partner, device_id_type=MESH)
    pl.semaphore_wait(barrier, len(partners))


def halves(ref):
    unit = 16 if ref.dtype == BF16 else 8
    rows = ref.shape[-2]
    top = (rows // 2 + unit - 1) // unit * unit
    return (pl.ds(0, top), pl.ds(top, rows - top))


def together(*tasks):
    tasks = list(tasks)
    while tasks:
        for task in list(tasks):
            if next(task, "ended") == "ended":
                tasks.remove(task)


def chain(*tasks):
    for task in tasks:
        yield from task


class Post:
    def __init__(self, send_sems, recv_sems):
        self.send_sems, self.recv_sems, self.started = send_sems, recv_sems, []

    def go(self, src, dst, partner):
        number = len(self.started)
        copy = pltpu.make_async_remote_copy(
            src_ref=src,
            dst_ref=dst,
            send_sem=self.send_sems.at[number],
            recv_sem=self.recv_sems.at[number],
            device_id=partner,
            device_id_type=MESH,
        )
        copy.start()
        self.started.append(copy)
        return copy

    def finish(self):
        for copy in self.started:
            copy.wait_send()


def plane_gather_steps(post, own_ref, all_ref):
    a, b, core = plane_place()
    me = plane_index(a, b, core)
    ahead_a, behind_a, ahead_b, behind_b, sibling = plane_partners()
    top, bottom = halves(own_ref)
    go = post.go
    a_ahead = go(own_ref, all_ref.at[me], ahead_a)
    a_behind = go(own_ref, all_ref.at[me], behind_a)

    def along_b(src, index):
        return (go(src, all_ref.at[index], ahead_b), go(src, all_ref.at[index], behind_b))

    def across(src, index):
        return go(src, all_ref.at[index], sibling)

    b_copies = {0: along_b(own_ref, me)}
    others = [across(own_ref, me)]
    from_behind = plane_index(a - 1, b, core)
    from_ahead = plane_index(a + 1, b, core)
    from_far = plane_index(a + 2, b, core)
    yield
    a_ahead.wait_recv()
    far_top = go(all_ref.at[from_behind, top], all_ref.at[from_behind, top], ahead_a)
    b_copies[1] = along_b(all_ref.at[from_behind], from_behind)
    yield
    a_behind.wait_recv()
    far_bottom = go(all_ref.at[from_ahead, bottom], all_ref.at[from_ahead, bottom], behind_a)
    others.append(across(all_ref.at[from_behind], from_behind))
    b_copies[2] = along_b(all_ref.at[from_ahead], from_ahead)
    others.append(across(all_ref.at[from_ahead], from_ahead))
    column = (a, a - 1, a + 1, a + 2)
    fars = {}

    def onward(k):
        below = plane_index(column[k], b - 1, core)
        above = plane_index(column[k], b + 1, core)
        yield
        b_copies[k][0].wait_recv()
        first = go(all_ref.at[below, top], all_ref.at[below, top], ahead_b)
        b_copies[k][1].wait_recv()
        second = go(all_ref.at[above, bottom], all_ref.at[above, bottom], behind_b)
        fars[k] = (first, second)
        others.append(across(all_ref.at[below], below))
        others.append(across(all_ref.at[above], above))

    yield from onward(0)
    yield
    far_top.wait_recv()
    far_bottom.wait_recv()
    b_copies[3] = along_b(all_ref.at[from_far], from_far)
    others.append(across(all_ref.at[from_far], from_far))
    yield from onward(1)
    yield from onward(2)
    yield from onward(3)
    for k in range(4):
        index = plane_index(column[k], b + 2, core)
        yield
        fars[k][0].wait_recv()
        fars[k][1].wait_recv()
        others.append(across(all_ref.at[index], index))
    yield
    for copy in others:
        copy.wait_recv()


PLANE_COPIES = 36


def add_rows(dst, sources, start, rows):
    step = 16 if rows % 16 == 0 else 8

    @pl.loop(0, rows // step)
    def _(i):
        at = pl.multiple_of(i * step, step)
        total = None
        for ref, first in sources:
            part = ref[pl.ds(first + at, step), :].astype(F32)
            total = part if total is None else total + part
        dst[pl.ds(start + at, step), :] = total.astype(dst.dtype)


def plane_scatter_steps(post, parts_ref, sum_ref, scratch):
    mine, other, b_far, b_near, a_far, a_near, local_sems = scratch
    a, b, core = plane_place()
    ahead_a, behind_a, ahead_b, behind_b, sibling = plane_partners()
    rows = a_far.shape[0]
    top, bottom = halves(a_far)
    high = top.size
    low = rows - high
    offsets = (2, 1, -1, 0)
    go = post.go
    crossing = {}
    order = [(k, 0) for k in range(4)] + [(k, j) for k in range(4) for j in (1, 2)]
    order += [(k, 3) for k in range(4)]
    for k, j in order:
        there = plane_index(b + offsets[k], a + offsets[j], 1 - core)
        crossing[k, j] = go(parts_ref.at[there], other.at[k, j], sibling)
    slots = mine.shape[0]
    loads = []

    def load():
        number = len(loads)
        if number < len(order):
            k, j = order[number]
            here = plane_index(a + offsets[k], b + offsets[j], core)
            slot = number % slots
            copy = pltpu.make_async_copy(
                parts_ref.at[here], mine.at[slot], local_sems.at[slot]
            )
            copy.start()
            loads.append(copy)

    for _ in range(slots - 1):
        load()

    def ready(k, j):
        number = order.index((k, j))
        load()
        crossing[k, j].wait_recv()
        loads[number].wait()
        return (other.at[k, j], mine.at[number % slots])

    far_b, near_b = {}, {}
    yield
    for k in range(4):
        block, extra = ready(k, 0)
        add_rows(block, [(block, 0), (extra, 0)], 0, rows)
        far_b[k] = (
            go(block.at[top], b_far.at[k, top], ahead_b),
            go(block.at[bottom], b_far.at[k, bottom], behind_b),
        )
    for k in range(4):
        far = b_far.at[k]
        yield
        block, extra = ready(k, 1)
        far_b[k][0].wait_recv()
        add_rows(block, [(block, 0), (extra, 0), (far, 0)], 0, high)
        add_rows(block, [(block, high), (extra, high)], high, low)
        first = go(block, b_near.at[0, k], ahead_b)
        block, extra = ready(k, 2)
        far_b[k][1].wait_recv()
        add_rows(block, [(block, 0), (extra, 0)], 0, high)
        add_rows(block, [(block, high), (extra, high), (far, high)], high, low)
        near_b[k] = (first, go(block, b_near.at[1, k], behind_b))
    far_a, near_a = [], []
    for k in range(4):
        yield
        block, extra = ready(k, 3)
        near_b[k][0].wait_recv()
        near_b[k][1].wait_recv()
        base = [block, extra, b_near.at[0, k], b_near.at[1, k]]
        upper = [(ref, 0) for ref in base]
        lower = [(ref, high) for ref in base]
        if k == 0:
            add_rows(block, upper, 0, high)
            add_rows(block, lower, high, low)
            far_a = [
                go(block.at[top], a_far.at[top], ahead_a),
                go(block.at[bottom], a_far.at[bottom], behind_a),
            ]
        elif k == 1:
            far_a[0].wait_recv()
            add_rows(block, upper + [(a_far, 0)], 0, high)
            add_rows(block, lower, high, low)
            near_a.append(go(block, a_near.at[0], ahead_a))
        elif k == 2:
            far_a[1].wait_recv()
            add_rows(block, upper, 0, high)
            add_rows(block, lower + [(a_far, high)], high, low)
            near_a.append(go(block, a_near.at[1], behind_a))
        else:
            near_a[0].wait_recv()
            near_a[1].wait_recv()
            add_rows(sum_ref, upper + [(a_near.at[0], 0), (a_near.at[1], 0)], 0, rows)


def plane_scatter_scratch(rows, columns, kind):
    return [
        pltpu.VMEM((4, rows, columns), kind),
        pltpu.VMEM((4, 4, rows, columns), kind),
        pltpu.VMEM((4, rows, columns), kind),
        pltpu.VMEM((2, 4, rows, columns), kind),
        pltpu.VMEM((rows, columns), kind),
        pltpu.VMEM((2, rows, columns), kind),
        pltpu.SemaphoreType.DMA((4,)),
    ]


OFFSETS = (2, 1, -1, 0)


def ring_places(a, b, core, tp):
    along_a = [(plane_index(a + offset, b, core), tp) for offset in OFFSETS[:3]]
    along_b = [(plane_index(a, b + offset, core), tp) for offset in OFFSETS[:3]]
    return (along_a, along_b, (plane_index(b, a, 1 - core), tp))


def brief_partners():
    along_a, along_b, sibling = ring_places(*plane_place(), lax.axis_index("tp"))
    return tuple(along_a + along_b + [sibling])


BRIEF_COPIES = 16 + 12 + 3


def brief_scatter_steps(post, parts_ref, sum_ref, scratch):
    other, from_b, from_a = scratch
    a, b, core = plane_place()
    along_a, along_b, sibling = ring_places(a, b, core, lax.axis_index("tp"))
    go = post.go
    crossing, copies_b, copies_a = {}, {}, {}
    for k in range(4):
        for j in range(4):
            there = plane_index(b + OFFSETS[k], a + OFFSETS[j], 1 - core)
            crossing[k, j] = go(parts_ref.at[there], other.at[k, j], sibling)
    yield
    for k in range(4):
        for j in range(4):
            here = plane_index(a + OFFSETS[k], b + OFFSETS[j], core)
            crossing[k, j].wait_recv()
            block = other.at[k, j]
            block[...] = (block[...].astype(F32) + parts_ref[here].astype(F32)).astype(block.dtype)
            if j < 3:
                copies_b[k, j] = go(block, from_b.at[k, j], along_b[j])
    yield
    for k in range(4):
        total = other[k, 3].astype(F32)
        for j in range(3):
            copies_b[k, j].wait_recv()
            total = total + from_b[k, j].astype(F32)
        if k < 3:
            other[k, 3] = total.astype(other.dtype)
            copies_a[k] = go(other.at[k, 3], from_a.at[k], along_a[k])
    yield
    for k in range(3):
        copies_a[k].wait_recv()
        total = total + from_a[k].astype(F32)
    sum_ref[...] = total.astype(sum_ref.dtype)


def brief_scatter_scratch(rows, columns, kind):
    return [
        pltpu.VMEM((4, 4, rows, columns), kind),
        pltpu.VMEM((4, 3, rows, columns), kind),
        pltpu.VMEM((3, rows, columns), kind),
    ]


def brief_gather_steps(post, own_ref, all_ref):
    a, b, core = plane_place()
    along_a, along_b, sibling = ring_places(a, b, core, lax.axis_index("tp"))
    go = post.go
    me = plane_index(a, b, core)
    copies_a = [go(own_ref, all_ref.at[me], place) for place in along_a]
    copies_b, crossing = [], []

    def onward(src, index):
        copies_b.extend(go(src, all_ref.at[index], place) for place in along_b)
        crossing.append(go(src, all_ref.at[index], sibling))

    onward(own_ref, me)
    yield
    for k in range(3):
        index = plane_index(a - OFFSETS[k], b, core)
        copies_a[k].wait_recv()
        onward(all_ref.at[index], index)
    yield
    for k, offset in enumerate((0, 2, 1, -1)):
        for j in range(3):
            index = plane_index(a - offset, b - OFFSETS[j], core)
            copies_b[3 * k + j].wait_recv()
            crossing.append(go(all_ref.at[index], all_ref.at[index], sibling))
    yield
    for copy in crossing:
        copy.wait_recv()


LINE_COPIES = 4


def line_gather_steps(post, own_ref, all_ref, arrived=None):
    tp = lax.axis_index("tp")
    ahead, behind = line_partners()
    top, bottom = halves(own_ref)
    before, after, far = wrap(tp - 1), wrap(tp + 1), wrap(tp + 2)
    first = post.go(own_ref, all_ref.at[tp], ahead)
    second = post.go(own_ref, all_ref.at[tp], behind)
    if arrived is not None:
        arrived(tp)
    yield
    first.wait_recv()
    third = post.go(all_ref.at[before, top], all_ref.at[before, top], ahead)
    second.wait_recv()
    fourth = post.go(all_ref.at[after, bottom], all_ref.at[after, bottom], behind)
    if arrived is not None:
        yield
        arrived(before)
        yield
        arrived(after)
    yield
    third.wait_recv()
    fourth.wait_recv()
    if arrived is not None:
        arrived(far)


def line_scatter_steps(post, make, far, near, finish):
    ahead, behind = line_partners()
    top, bottom = halves(far)
    high = top.size
    rows = far.shape[0]
    block = make(2)
    first = post.go(block.at[top], far.at[top], ahead)
    second = post.go(block.at[bottom], far.at[bottom], behind)
    yield
    block = make(1)
    yield
    first.wait_recv()
    add_rows(block, [(block, 0), (far, 0)], 0, high)
    third = post.go(block, near.at[0], ahead)
    other = make(-1)
    yield
    second.wait_recv()
    add_rows(other, [(other, high), (far, high)], high, rows - high)
    fourth = post.go(other, near.at[1], behind)
    own = make(0)
    yield
    third.wait_recv()
    fourth.wait_recv()
    finish(own, near.at[0], near.at[1])


def dispatch_kernel(own_ref, pair_ref, down_ref, all_ref, pair_all, down_all, *rest):
    send_sems, recv_sems, local_sems = rest
    me = lax.axis_index("ep")
    tp = lax.axis_index("tp")
    greet(plane_partners() + line_partners())
    post = Post(send_sems, recv_sems)
    locals_ = [
        pltpu.make_async_copy(own_ref, all_ref.at[me], local_sems.at[0]),
        pltpu.make_async_copy(pair_ref, pair_all.at[tp], local_sems.at[1]),
        pltpu.make_async_copy(down_ref, down_all.at[tp], local_sems.at[2]),
    ]
    for copy in locals_:
        copy.start()
    together(
        plane_gather_steps(post, own_ref, all_ref),
        line_gather_steps(post, pair_ref, pair_all),
        line_gather_steps(post, down_ref, down_all),
    )
    post.finish()
    for copy in locals_:
        copy.wait()


def dispatch(own, pair, down, number):
    count = PLANE_COPIES + 2 * LINE_COPIES
    return pl.pallas_call(
        dispatch_kernel,
        out_shape=[
            jax.ShapeDtypeStruct((32,) + own.shape, own.dtype),
            jax.ShapeDtypeStruct((4,) + pair.shape, pair.dtype),
            jax.ShapeDtypeStruct((4,) + down.shape, down.dtype),
        ],
        in_specs=[ANY] * 3,
        out_specs=[ANY] * 3,
        scratch_shapes=[
            pltpu.SemaphoreType.DMA((count,)),
            pltpu.SemaphoreType.DMA((count,)),
            pltpu.SemaphoreType.DMA((3,)),
        ],
        compiler_params=pltpu.CompilerParams(collective_id=number, has_side_effects=True),
        name="dispatch",
    )(own, pair, down)


def collect_kernel(parts_ref, weights_ref, sum_ref, weight_sum, *rest):
    send_sems, recv_sems = rest[-2:]
    line, line_far, line_near, line_sems = rest[7:11]
    tp = lax.axis_index("tp")
    loads = {}
    for number, offset in enumerate((2, 1, -1, 0)):
        loads[offset] = pltpu.make_async_copy(
            weights_ref.at[wrap(tp + offset)], line.at[number], line_sems.at[number]
        )
        loads[offset].start()
    greet(plane_partners() + line_partners())
    post = Post(send_sems, recv_sems)

    def make(offset):
        loads[offset].wait()
        return line.at[(2, 1, -1, 0).index(offset)]

    def finish(own, first, second):
        add_rows(weight_sum, [(own, 0), (first, 0), (second, 0)], 0, own.shape[0])

    together(
        plane_scatter_steps(post, parts_ref, sum_ref, rest[:7]),
        line_scatter_steps(post, make, line_far, line_near, finish),
    )
    post.finish()


def collect(parts, weights, number):
    _, rows, columns = parts.shape
    _, weight_rows, weight_columns = weights.shape
    count = PLANE_COPIES + LINE_COPIES
    return pl.pallas_call(
        collect_kernel,
        out_shape=[
            jax.ShapeDtypeStruct((rows, columns), F32),
            jax.ShapeDtypeStruct((weight_rows, weight_columns), F32),
        ],
        in_specs=[ANY, ANY],
        out_specs=[VMEM, VMEM],
        scratch_shapes=plane_scatter_scratch(rows, columns, parts.dtype)
        + [
            pltpu.VMEM((4, weight_rows, weight_columns), BF16),
            pltpu.VMEM((weight_rows, weight_columns), BF16),
            pltpu.VMEM((2, weight_rows, weight_columns), BF16),
            pltpu.SemaphoreType.DMA((4,)),
            pltpu.SemaphoreType.DMA((count,)),
            pltpu.SemaphoreType.DMA((count,)),
        ],
        compiler_params=pltpu.CompilerParams(
            collective_id=number, has_side_effects=True, vmem_limit_bytes=56 << 20
        ),
        name="collect",
    )(parts, weights)


def split_float(values):
    high = values.astype(BF16)
    return (high, (values - high.astype(F32)).astype(BF16))


def split_three(values):
    high = values.astype(BF16)
    rest = values - high.astype(F32)
    middle = rest.astype(BF16)
    return (high, middle, (rest - middle.astype(F32)).astype(BF16))


def head_mean(values):
    same = (
        lax.broadcasted_iota(jnp.int32, (128, 128), 0) // 64
        == lax.broadcasted_iota(jnp.int32, (128, 128), 1) // 64
    ).astype(BF16)
    high, low = split_float(values)
    total = jnp.dot(high, same, preferred_element_type=F32)
    total = total + jnp.dot(low, same, preferred_element_type=F32)
    return total * (1.0 / 64.0)


def other_half(values):
    lane = lax.broadcasted_iota(jnp.int32, values.shape, 1)
    return jnp.where(
        lax.rem(lane, 64) < 32, pltpu.roll(values, 96, 1), pltpu.roll(values, 32, 1)
    )


def head_ready(raw, gain, cosine, sine):
    normed = raw * lax.rsqrt(head_mean(raw * raw) + 1e-06) * gain
    return normed * cosine + other_half(normed) * sine


def head_back(grad, raw, gain, cosine, sine):
    grad = grad * cosine + other_half(grad * sine)
    scale = lax.rsqrt(head_mean(raw * raw) + 1e-06)
    plain = raw * scale
    grad_gain = jnp.sum(grad * plain, axis=0, keepdims=True)
    grad = grad * gain
    return (scale * (grad - plain * head_mean(grad * plain)), grad_gain)


def row_scale(values):
    return lax.rsqrt(jnp.mean(values * values, axis=1, keepdims=True) + 1e-05)


def exchange(values):
    return jnp.concatenate([values[:, 64:], values[:, :64]], axis=1)


def head_pairs(block):
    rows = block.shape[0]
    low = lax.broadcasted_iota(jnp.int32, (rows, 128), 1) < 64
    left, right = block[:, :128], block[:, 128:]
    zero = jnp.zeros_like(left)
    straight = jnp.concatenate([jnp.where(low, left, zero), jnp.where(low, zero, right)], axis=0)
    crossed = jnp.concatenate([jnp.where(low, zero, left), jnp.where(low, right, zero)], axis=0)
    return (straight, crossed)


def heads_back(straight, crossed):
    rows = straight.shape[0] // 2
    low = lax.broadcasted_iota(jnp.int32, (rows, 128), 1) < 64
    left = jnp.where(low, straight[:rows], crossed[:rows])
    right = jnp.where(low, crossed[rows:], straight[rows:])
    return jnp.concatenate([left, right], axis=1)


def attend_block(query, keys, values, bias):
    rows = query.shape[0]
    outs = []
    for pair, key_part, value_part in zip(
        head_pairs(query), (keys, exchange(keys)), (values, exchange(values)), strict=True
    ):
        halves_out = []
        for number in range(2):
            part = pair[number * rows : (number + 1) * rows]
            scores = lax.dot_general(part, key_part, CONTRACT_LAST, preferred_element_type=F32)
            weights = jnp.exp(scores * 0.125 + bias)
            total_weight = jnp.sum(weights, axis=1, keepdims=True)
            out = jnp.dot(weights.astype(BF16), value_part, preferred_element_type=F32)
            halves_out.append(out / total_weight)
        outs.append(jnp.concatenate(halves_out, axis=0))
    return heads_back(*outs).astype(BF16)


def block_rows(block):
    return pl.ds(pl.multiple_of(block * 256, 256), 256)


def opening_kernel(
    inputs, gain_one, query_weight, key_weight, value_weight, query_gain, key_gain, cosine, sine,
    seg_column, seg_row, live_row, output_weight, gain_two, router, routes, cotangent,
    normed, raw, query, keys, values, mixed, residual, block, gates, grad_all,
    parts, far, near, send_sems, recv_sems, local_sem,
):
    tp = lax.axis_index("tp")
    local = pltpu.make_async_copy(cotangent, grad_all.at[lax.axis_index("ep")], local_sem)
    local.start()
    hidden = inputs[...].astype(F32)
    normed[tp] = (hidden * row_scale(hidden) * gain_one[...]).astype(BF16)
    greet(plane_partners() + line_partners())
    post = Post(send_sems, recv_sems)

    def project(place):
        rows = block_rows(place)
        part = normed[place]
        cos, sin = cosine[rows, :], sine[rows, :]
        both = jnp.dot(part, query_weight[...], preferred_element_type=F32)
        raw[rows, :256] = both
        for lanes in (slice(0, 128), slice(128, 256)):
            query[rows, lanes] = head_ready(both[:, lanes], query_gain[...], cos, sin).astype(BF16)
        one = jnp.dot(part, key_weight[...], preferred_element_type=F32)
        raw[rows, 256:] = one
        keys[rows, :] = head_ready(one, key_gain[...], cos, sin).astype(BF16)
        values[rows, :] = jnp.dot(part, value_weight[...], preferred_element_type=F32).astype(BF16)

    def make(offset):
        place = wrap(tp + offset)
        rows = block_rows(place)
        position = place * 256 + lax.broadcasted_iota(jnp.int32, (256, 1024), 0)
        key_position = lax.broadcasted_iota(jnp.int32, (256, 1024), 1)
        allowed = (seg_column[rows, :] == seg_row[...]) & (
            (live_row[...] == 1) | (position == key_position)
        )
        bias = jnp.where(allowed, 0.0, -1e30).astype(F32)
        out = attend_block(query[rows, :], keys[...], values[...], bias)
        mixed[rows, :] = out
        part = parts.at[(2, 1, -1, 0).index(offset)]
        part[...] = jnp.dot(out, output_weight[...], preferred_element_type=F32).astype(BF16)
        return part

    def finish(own, first, second):
        total = own[...].astype(F32) + first[...].astype(F32) + second[...].astype(F32)
        total = inputs[...].astype(F32) + total
        residual[...] = total
        normed_two = total * row_scale(total) * gain_two[...]
        block[:256, :] = normed_two.astype(BF16)
        logits = jnp.zeros((32, 256), F32)
        for piece in split_three(normed_two):
            logits = logits + lax.dot_general(
                router[...], piece, CONTRACT_LAST, preferred_element_type=F32
            )
        expert = lax.broadcasted_iota(jnp.int32, (32, 256), 0)
        named = expert < 0
        for choice in range(8):
            named = named | (routes[choice : choice + 1, :] == expert)
        top_logit = jnp.max(jnp.where(named, logits, -1e30), axis=0, keepdims=True)
        raised = jnp.where(named, jnp.exp(jnp.where(named, logits - top_logit, 0.0)), 0.0)
        probs = raised / jnp.sum(raised, axis=0, keepdims=True)
        gates[...] = probs
        high, low = split_float(probs)
        block[256:, :] = jnp.concatenate([high[:16], low[:16], high[16:], low[16:]], axis=1)

    together(
        chain(
            line_gather_steps(post, normed.at[tp], normed, project),
            line_scatter_steps(post, make, far, near, finish),
        ),
        plane_gather_steps(post, cotangent, grad_all),
    )
    post.finish()
    local.wait()


def opening(arguments, number):
    count = 2 * LINE_COPIES + PLANE_COPIES
    return pl.pallas_call(
        opening_kernel,
        out_shape=[
            jax.ShapeDtypeStruct((4, 256, 1024), BF16),
            jax.ShapeDtypeStruct((1024, 384), F32),
            jax.ShapeDtypeStruct((1024, 256), BF16),
            jax.ShapeDtypeStruct((1024, 128), BF16),
            jax.ShapeDtypeStruct((1024, 128), BF16),
            jax.ShapeDtypeStruct((1024, 256), BF16),
            jax.ShapeDtypeStruct((256, 1024), F32),
            jax.ShapeDtypeStruct((256 + EXTRA, 1024), BF16),
            jax.ShapeDtypeStruct((32, 256), F32),
            jax.ShapeDtypeStruct((32, 256, 1024), BF16),
        ],
        in_specs=[VMEM] * (len(arguments) - 1) + [ANY],
        out_specs=[VMEM] * 9 + [ANY],
        scratch_shapes=[
            pltpu.VMEM((4, 256, 1024), BF16),
            pltpu.VMEM((256, 1024), BF16),
            pltpu.VMEM((2, 256, 1024), BF16),
            pltpu.SemaphoreType.DMA((count,)),
            pltpu.SemaphoreType.DMA((count,)),
            pltpu.SemaphoreType.DMA,
        ],
        compiler_params=pltpu.CompilerParams(
            collective_id=number, has_side_effects=True, vmem_limit_bytes=56 << 20
        ),
        name="opening",
    )(*arguments)


def attend_back_block(query, grad, keys, values, bias, keys_sum, values_sum):
    rows = query.shape[0]
    query_pairs = head_pairs(query)
    grad_pairs = head_pairs(grad)
    key_parts = (keys, exchange(keys))
    value_parts = (values, exchange(values))
    outs = []
    for side in range(2):
        halves_out = []
        for number in range(2):
            part = query_pairs[side][number * rows : (number + 1) * rows]
            grad_part = grad_pairs[side][number * rows : (number + 1) * rows]
            scores = lax.dot_general(
                key_parts[side], part, CONTRACT_LAST, preferred_element_type=F32
            )
            raised = jnp.exp(scores * 0.125 + bias)
            weights = raised * (1.0 / jnp.sum(raised, axis=0, keepdims=True))
            grad_weights = lax.dot_general(
                value_parts[side], grad_part, CONTRACT_LAST, preferred_element_type=F32
            )
            inner = jnp.sum(weights * grad_weights, axis=0, keepdims=True)
            grad_scores = (weights * (grad_weights - inner)).astype(BF16)
            halves_out.append(
                lax.dot_general(
                    grad_scores, key_parts[side], CONTRACT_ROWS, preferred_element_type=F32
                )
            )
            keys_sum[side] += jnp.dot(grad_scores, part, preferred_element_type=F32)
            values_sum[side] += jnp.dot(
                weights.astype(BF16), grad_part, preferred_element_type=F32
            )
        outs.append(jnp.concatenate(halves_out, axis=0))
    return heads_back(*outs) * 0.125


SMALL_ROWS = 16


def closing_kernel(
    back, residual, gates, cotangent, gain_two, router, query, keys, values, mixed,
    output_weight, query_weight, key_weight, value_weight, raw, normed, inputs, gain_one,
    query_gain, key_gain, cosine, sine, seg_column, seg_row, live_column, out_parts,
    grad_inputs, dense_all, small_all, combined,
    grad_all, grad_residual, low, keys_sum, values_sum, output_sum, parts, far, near,
    dense, dense_own, small, small_own, small_line, small_sum, query_gain_sum, gain_one_sum, *rest,
):
    out_scratch, dense_scratch, small_scratch = rest[:7], rest[7:10], rest[10:13]
    post = Post(rest[13], rest[14])
    me = lax.axis_index("ep")
    tp = lax.axis_index("tp")
    ahead, behind = line_partners()
    across = (me, wrap(tp + 2))

    lines = back[256:, :]
    grad_gates = jnp.concatenate(
        [lines[:, :256] + lines[:, 256:512], lines[:, 512:768] + lines[:, 768:]], axis=0
    )
    probs = gates[...]
    grad_logits = probs * (grad_gates - jnp.sum(probs * grad_gates, axis=0, keepdims=True))
    grad_two = back[:256, :]
    logit_pieces = split_three(grad_logits)
    for piece in logit_pieces:
        grad_two = grad_two + lax.dot_general(
            piece, router[...], CONTRACT_ROWS, preferred_element_type=F32
        )
    total = residual[...]
    scale = row_scale(total)
    plain = total * scale
    grad_gain_two = jnp.sum(grad_two * plain, axis=0, keepdims=True)
    normed_pieces = split_three(plain * gain_two[...])
    grad_router = jnp.zeros((32, 1024), F32)
    for first, second in ((0, 0), (0, 1), (1, 0), (1, 1), (0, 2), (2, 0)):
        grad_router = grad_router + jnp.dot(
            logit_pieces[first], normed_pieces[second], preferred_element_type=F32
        )
    grad_two = grad_two * gain_two[...]
    grad_total = cotangent[...].astype(F32) + scale * (
        grad_two - plain * jnp.mean(grad_two * plain, axis=1, keepdims=True)
    )
    grad_residual[...] = grad_total
    grad_all[tp] = grad_total.astype(BF16)
    greet(brief_partners() + (ahead, behind, across))

    keys_sum[...] = jnp.zeros_like(keys_sum)
    values_sum[...] = jnp.zeros_like(values_sum)
    output_sum[...] = jnp.zeros_like(output_sum)
    query_gain_sum[...] = jnp.zeros_like(query_gain_sum)
    gain_one_sum[...] = jnp.zeros_like(gain_one_sum)

    def attention(place):
        rows = block_rows(place)
        grad = grad_all[place]
        output_sum[...] += lax.dot_general(
            mixed[rows, :], grad, CONTRACT_ROWS, preferred_element_type=F32
        )
        grad_mixed = lax.dot_general(
            grad, output_weight[...], CONTRACT_LAST, preferred_element_type=F32
        ).astype(BF16)
        key_position = lax.broadcasted_iota(jnp.int32, (1024, 256), 0)
        position = place * 256 + lax.broadcasted_iota(jnp.int32, (1024, 256), 1)
        allowed = (seg_column[...] == seg_row[:, rows]) & (
            (live_column[...] == 1) | (position == key_position)
        )
        bias = jnp.where(allowed, 0.0, -1e30).astype(F32)
        grad_query = attend_back_block(
            query[rows, :], grad_mixed, keys[...], values[...], bias, keys_sum, values_sum
        )
        for lanes in (slice(0, 128), slice(128, 256)):
            grad_raw, grad_gain = head_back(
                grad_query[:, lanes],
                raw[rows, lanes],
                query_gain[...],
                cosine[rows, :],
                sine[rows, :],
            )
            low[rows, lanes] = grad_raw.astype(BF16)
            query_gain_sum[...] += grad_gain

    out_steps = plane_scatter_steps(post, out_parts, combined, out_scratch)
    line_steps = line_gather_steps(post, grad_all.at[tp], grad_all, attention)
    for _ in line_steps:
        next(out_steps, None)
    grad_raw, grad_key_gain = head_back(
        (keys_sum[0] + exchange(keys_sum[1])) * 0.125,
        raw[:, 256:],
        key_gain[...],
        cosine[...],
        sine[...],
    )
    low[:, 256:384] = grad_raw.astype(BF16)
    low[:, 384:] = (values_sum[0] + exchange(values_sum[1])).astype(BF16)

    def make(offset):
        rows = block_rows(wrap(tp + offset))
        total = lax.dot_general(
            low[rows, :256], query_weight[...], CONTRACT_LAST, preferred_element_type=F32
        )
        total = total + lax.dot_general(
            low[rows, 256:384], key_weight[...], CONTRACT_LAST, preferred_element_type=F32
        )
        total = total + lax.dot_general(
            low[rows, 384:], value_weight[...], CONTRACT_LAST, preferred_element_type=F32
        )
        gain_one_sum[...] += jnp.sum(
            total * normed[rows, :].astype(F32), axis=0, keepdims=True
        )
        part = parts.at[(2, 1, -1, 0).index(offset)]
        part[...] = total.astype(BF16)
        return part

    def finish(own, first, second):
        grad_one = own[...].astype(F32) + first[...].astype(F32) + second[...].astype(F32)
        hidden = inputs[...].astype(F32)
        scale = row_scale(hidden)
        plain = hidden * scale
        grad_one = grad_one * gain_one[...]
        grad_inputs[...] = (
            grad_residual[...]
            + scale * (grad_one - plain * jnp.mean(grad_one * plain, axis=1, keepdims=True))
        ).astype(BF16)

    def fill_small():
        grad_gain_one = gain_one_sum[...] / gain_one[...]
        small[...] = jnp.zeros_like(small)
        for part in range(8):
            lanes = slice(part * 128, (part + 1) * 128)
            small[2 * part] = grad_router[:16, lanes]
            small[2 * part + 1] = grad_router[16:, lanes]
            small[16, part : part + 1, :] = grad_gain_one[:, lanes]
            small[16, 8 + part : 9 + part, :] = grad_gain_two[:, lanes]
        small[17, 0:1, :] = query_gain_sum[...]
        small[17, 1:2, :] = grad_key_gain

    def dense_steps():
        weights = lax.dot_general(
            normed[...], low[...], CONTRACT_ROWS, preferred_element_type=F32
        ).astype(BF16)
        for part in range(32):
            dense[part, :, :512] = weights[part * 32 : (part + 1) * 32]
        for part in range(4):
            block = output_sum[:, part * 256 : (part + 1) * 256].astype(BF16)
            for piece in range(8):
                dense[part * 8 + piece, :, 512:] = block[piece * 32 : (piece + 1) * 32]
        yield from brief_scatter_steps(post, dense, dense_own, dense_scratch)
        dense_all[me] = dense_own[...]
        yield from brief_gather_steps(post, dense_own, dense_all)

    def small_steps():
        fill_small()
        yield from brief_scatter_steps(post, small, small_own, small_scratch)
        line = [
            post.go(small_own, small_line.at[0], ahead),
            post.go(small_own, small_line.at[1], behind),
            post.go(small_own, small_line.at[2], across),
        ]
        yield
        for copy in line:
            copy.wait_recv()
        small_sum[...] = small_own[...] + small_line[0] + small_line[1] + small_line[2]
        small_all[me] = small_sum[...]
        yield from brief_gather_steps(post, small_sum, small_all)

    line_steps = line_scatter_steps(post, make, far, near, finish)
    for _ in range(4):
        next(line_steps)
    together(dense_steps(), small_steps(), line_steps, out_steps)
    post.finish()


def closing(arguments, number):
    count = 2 * LINE_COPIES + PLANE_COPIES + 4 * BRIEF_COPIES + 3
    return pl.pallas_call(
        closing_kernel,
        out_shape=[
            jax.ShapeDtypeStruct((256, 1024), BF16),
            jax.ShapeDtypeStruct((32, 32, 768), BF16),
            jax.ShapeDtypeStruct((32, SMALL_ROWS, 128), F32),
            jax.ShapeDtypeStruct((256, 1024), F32),
        ],
        in_specs=[VMEM] * (len(arguments) - 1) + [ANY],
        out_specs=[VMEM] * 4,
        scratch_shapes=[
            pltpu.VMEM((4, 256, 1024), BF16),
            pltpu.VMEM((256, 1024), F32),
            pltpu.VMEM((1024, 512), BF16),
            pltpu.VMEM((2, 1024, 128), F32),
            pltpu.VMEM((2, 1024, 128), F32),
            pltpu.VMEM((256, 1024), F32),
            pltpu.VMEM((4, 256, 1024), BF16),
            pltpu.VMEM((256, 1024), BF16),
            pltpu.VMEM((2, 256, 1024), BF16),
            pltpu.VMEM((32, 32, 768), BF16),
            pltpu.VMEM((32, 768), BF16),
            pltpu.VMEM((32, SMALL_ROWS, 128), F32),
            pltpu.VMEM((SMALL_ROWS, 128), F32),
            pltpu.VMEM((3, SMALL_ROWS, 128), F32),
            pltpu.VMEM((SMALL_ROWS, 128), F32),
            pltpu.VMEM((1, 128), F32),
            pltpu.VMEM((1, 1024), F32),
        ]
        + plane_scatter_scratch(256, 1024, BF16)
        + brief_scatter_scratch(32, 768, BF16)
        + brief_scatter_scratch(SMALL_ROWS, 128, F32)
        + [pltpu.SemaphoreType.DMA((count,)), pltpu.SemaphoreType.DMA((count,))],
        compiler_params=pltpu.CompilerParams(
            collective_id=number, has_side_effects=True, vmem_limit_bytes=58 << 20
        ),
        name="closing",
    )(*arguments)


def finish_kernel(
    dense, weights, residual, combined,
    result, grad_query, grad_key, grad_value, grad_output, grad_gate, grad_up, grad_down,
):
    result[...] = (residual[...] + combined[...]).astype(BF16)
    grad_query[...] = dense[:, :256].astype(F32)
    grad_key[...] = dense[:, 256:384].astype(F32)
    grad_value[...] = dense[:, 384:512].astype(F32)
    for part in range(4):
        grad_output[:, part * 256 : (part + 1) * 256] = dense[
            part * 256 : (part + 1) * 256, 512:
        ].astype(F32)
    grad_gate[0] = weights[:1024, :]
    grad_up[0] = weights[1024:2048, :]
    grad_down[0] = weights[2048:, :].T


def finish_all(dense, weights, residual, combined):
    return pl.pallas_call(
        finish_kernel,
        out_shape=[
            jax.ShapeDtypeStruct((256, 1024), BF16),
            jax.ShapeDtypeStruct((1024, 256), F32),
            jax.ShapeDtypeStruct((1024, 128), F32),
            jax.ShapeDtypeStruct((1024, 128), F32),
            jax.ShapeDtypeStruct((256, 1024), F32),
            jax.ShapeDtypeStruct((1, 1024, 128), F32),
            jax.ShapeDtypeStruct((1, 1024, 128), F32),
            jax.ShapeDtypeStruct((1, 128, 1024), F32),
        ],
        in_specs=[VMEM] * 4,
        out_specs=[VMEM] * 8,
        compiler_params=pltpu.CompilerParams(vmem_limit_bytes=40 << 20),
        name="finish_all",
    )(dense, weights, residual, combined)


GROUP = 4


def experts_kernel(
    number_ref, rows_ref, grads_ref, pair_ref, down_ref,
    out_ref, back_ref, weight_grads_ref,
    gate_full, up_full, gate_sum, up_sum, down_sum, rows_own, grads_own, gates_own, select,
):
    step = pl.program_id(0)
    expert = number_ref[0]
    lane_row = lax.rem(expert, 16)
    upper = expert >= 16

    @pl.when(step == 0)
    def _():
        for part in range(4):
            columns = slice(part * 128, (part + 1) * 128)
            gate_full[:, columns] = pair_ref[part, :1024, :]
            up_full[:, columns] = pair_ref[part, 1024:, :]
        gate_sum[...] = jnp.zeros_like(gate_sum)
        up_sum[...] = jnp.zeros_like(up_sum)
        down_sum[...] = jnp.zeros_like(down_sum)

    earlier = (
        lax.broadcasted_iota(jnp.int32, (256, 256), 0)
        <= lax.broadcasted_iota(jnp.int32, (256, 256), 1)
    ).astype(BF16)
    slot = lax.broadcasted_iota(jnp.int32, (SLOTS, 256), 0).astype(F32)
    extra_row = lax.broadcasted_iota(jnp.int32, (EXTRA, 1024), 0) == lane_row
    for part in range(GROUP):
        extras = jnp.where(extra_row, rows_ref[part, 256:, :].astype(F32), 0.0)
        extras = jnp.sum(extras, axis=0, keepdims=True)
        gates = jnp.where(
            upper, extras[:, 512:768] + extras[:, 768:], extras[:, :256] + extras[:, 256:512]
        )
        named = jnp.broadcast_to(gates, (16, 256)) > 0.0
        rank = jnp.dot(named.astype(BF16), earlier, preferred_element_type=F32)[:1] - 1.0
        chosen = (slot == rank) & (gates > 0.0)
        chosen_low = chosen.astype(BF16)
        at = slice(part * SLOTS, (part + 1) * SLOTS)
        select[at, :] = chosen_low
        rows_own[at, :] = jnp.dot(
            chosen_low, rows_ref[part, :256, :], preferred_element_type=F32
        ).astype(BF16)
        grads_own[at, :] = jnp.dot(
            chosen_low, grads_ref[part], preferred_element_type=F32
        ).astype(BF16)
        gates_own[at, :] = jnp.sum(jnp.where(chosen, gates, 0.0), axis=1, keepdims=True)

    rows_in = rows_own[...]
    gate_pre = jnp.dot(rows_in, gate_full[...], preferred_element_type=F32)
    up_pre = jnp.dot(rows_in, up_full[...], preferred_element_type=F32)
    sigmoid = 1.0 / (1.0 + jnp.exp(-gate_pre))
    silu = gate_pre * sigmoid
    act = (silu * up_pre).astype(BF16)
    out = jnp.dot(act, down_ref[...], preferred_element_type=F32).astype(BF16).astype(F32)
    gate_factor = gates_own[...]
    grads_in = grads_own[...].astype(F32)
    grad_gates = jnp.sum(grads_in * out, axis=1, keepdims=True)
    weighted = (gate_factor * out).astype(BF16)
    grad_out = (gate_factor * grads_in).astype(BF16)
    grad_act = lax.dot_general(
        grad_out, down_ref[...], CONTRACT_LAST, preferred_element_type=F32
    )
    down_sum[...] += lax.dot_general(
        grad_out, act, CONTRACT_ROWS, preferred_element_type=F32
    )
    grad_gate_pre = (grad_act * up_pre * sigmoid * (1.0 + gate_pre * (1.0 - sigmoid))).astype(BF16)
    grad_up_pre = (grad_act * silu).astype(BF16)
    gate_sum[...] += lax.dot_general(
        rows_in, grad_gate_pre, CONTRACT_ROWS, preferred_element_type=F32
    )
    up_sum[...] += lax.dot_general(
        rows_in, grad_up_pre, CONTRACT_ROWS, preferred_element_type=F32
    )
    grad_rows = lax.dot_general(
        grad_gate_pre, gate_full[...], CONTRACT_LAST, preferred_element_type=F32
    )
    grad_rows = grad_rows + lax.dot_general(
        grad_up_pre, up_full[...], CONTRACT_LAST, preferred_element_type=F32
    )
    grad_rows = grad_rows.astype(BF16)
    nothing = jnp.zeros((1, 512), F32)
    for part in range(GROUP):
        at = slice(part * SLOTS, (part + 1) * SLOTS)
        chosen_low = select[at, :]
        out_ref[part] = lax.dot_general(
            chosen_low, weighted[at], CONTRACT_ROWS, preferred_element_type=F32
        ).astype(BF16)
        back_ref[part, :256, :] = lax.dot_general(
            chosen_low, grad_rows[at], CONTRACT_ROWS, preferred_element_type=F32
        ).astype(BF16)
        spread = jnp.sum(chosen_low.astype(F32) * grad_gates[at], axis=0, keepdims=True)
        high = spread.astype(BF16).astype(F32)
        both = jnp.concatenate([high, spread - high], axis=1)
        line = jnp.concatenate(
            [jnp.where(upper, nothing, both), jnp.where(upper, both, nothing)], axis=1
        )
        back_ref[part, 256:, :] = jnp.where(extra_row, line, 0.0).astype(BF16)

    @pl.when(step == pl.num_programs(0) - 1)
    def _():
        for part in range(4):
            columns = slice(part * 128, (part + 1) * 128)
            weight_grads_ref[part, :1024, :] = gate_sum[:, columns].astype(BF16)
            weight_grads_ref[part, 1024:2048, :] = up_sum[:, columns].astype(BF16)
            weight_grads_ref[part, 2048:, :] = down_sum[:, columns].astype(BF16)


def run_experts(number, rows, grads, pair, down):
    sources = rows.shape[0]
    count = GROUP * SLOTS
    return pl.pallas_call(
        experts_kernel,
        out_shape=[
            jax.ShapeDtypeStruct((sources, 256, 1024), BF16),
            jax.ShapeDtypeStruct((sources, 256 + EXTRA, 1024), BF16),
            jax.ShapeDtypeStruct((4, 3072, 128), BF16),
        ],
        grid=(sources // GROUP,),
        in_specs=[
            pl.BlockSpec(memory_space=pltpu.SMEM),
            pl.BlockSpec((GROUP, 256 + EXTRA, 1024), lambda i: (i, 0, 0)),
            pl.BlockSpec((GROUP, 256, 1024), lambda i: (i, 0, 0)),
            pl.BlockSpec((4, 2048, 128), lambda i: (0, 0, 0)),
            pl.BlockSpec((512, 1024), lambda i: (0, 0)),
        ],
        out_specs=[
            pl.BlockSpec((GROUP, 256, 1024), lambda i: (i, 0, 0)),
            pl.BlockSpec((GROUP, 256 + EXTRA, 1024), lambda i: (i, 0, 0)),
            pl.BlockSpec((4, 3072, 128), lambda i: (0, 0, 0)),
        ],
        scratch_shapes=[
            pltpu.VMEM((1024, 512), BF16),
            pltpu.VMEM((1024, 512), BF16),
            pltpu.VMEM((1024, 512), F32),
            pltpu.VMEM((1024, 512), F32),
            pltpu.VMEM((1024, 512), F32),
            pltpu.VMEM((count, 1024), BF16),
            pltpu.VMEM((count, 1024), BF16),
            pltpu.VMEM((count, 1), F32),
            pltpu.VMEM((count, 256), BF16),
        ],
        compiler_params=pltpu.CompilerParams(vmem_limit_bytes=60 << 20),
        name="run_experts",
    )(number, rows, grads, pair, down)


def rotary_constants():
    position = np.arange(SEQ_LEN, dtype=np.float32)
    power = -(np.arange(32, dtype=np.float32) * np.float32(2.0)) / np.float32(64.0)
    frequency = np.float32(10000.0) ** power
    angles = position[:, None] * frequency[None, :]
    cosine, sine = np.cos(angles), np.sin(angles)
    return (np.tile(cosine, (1, 4)), np.concatenate([-sine, sine, -sine, sine], axis=1))


def shards(
    inputs,
    first_gain,
    query_weight,
    key_weight,
    value_weight,
    query_gain,
    key_gain,
    output_weight,
    second_gain,
    router_weight,
    gate_weight,
    up_weight,
    down_weight,
    segments,
    live_mask,
    routes,
    cotangent,
):
    gain_one = first_gain.astype(F32).reshape(1, -1)
    gain_two = second_gain.astype(F32).reshape(1, -1)
    query_scale = jnp.tile(query_gain.astype(F32), 2).reshape(1, -1)
    key_scale = jnp.tile(key_gain.astype(F32), 2).reshape(1, -1)
    cosine, sine = rotary_constants()
    seg_column, seg_row = segments.reshape(-1, 1), segments.reshape(1, -1)
    live_column, live_row = live_mask.reshape(-1, 1), live_mask.reshape(1, -1)
    router = router_weight.T
    normed, raw, query, keys, values, mixed, residual, block, gates, grad_all = opening(
        (
            inputs, gain_one, query_weight, key_weight, value_weight, query_scale, key_scale,
            cosine, sine, seg_column, seg_row, live_row, output_weight, gain_two, router, routes.T,
            cotangent,
        ),
        1,
    )
    pair = jnp.concatenate([gate_weight[0], up_weight[0]], axis=0)
    rows_all, pair_all, down_all = dispatch(block, pair, down_weight[0], 2)
    number = lax.axis_index("ep").astype(jnp.int32).reshape(1)
    out_parts, back_parts, weight_parts = run_experts(
        number, rows_all, grad_all, pair_all, down_all.reshape(512, 1024)
    )
    back, weight_sums = collect(back_parts, weight_parts, 3)
    grad_inputs, dense, small, combined = closing(
        (
            back, residual, gates, cotangent, gain_two, router, query, keys, values, mixed,
            output_weight, query_weight, key_weight, value_weight, raw, normed.reshape(1024, 1024),
            inputs, gain_one, query_scale, key_scale, cosine, sine, seg_column, seg_row,
            live_column, out_parts,
        ),
        4,
    )
    result, grad_query, grad_key, grad_value, grad_output, grad_gate, grad_up, grad_down = (
        finish_all(dense.reshape(1024, 768), weight_sums, residual, combined)
    )
    grad_router = small[:16].reshape(8, 32, 128).transpose(0, 2, 1).reshape(1024, 32)
    query_gain_sum, key_gain_sum = small[17, 0], small[17, 1]
    return (
        result,
        grad_inputs,
        small[16, :8].reshape(-1),
        grad_query,
        grad_key,
        grad_value,
        query_gain_sum[:64] + query_gain_sum[64:],
        key_gain_sum[:64] + key_gain_sum[64:],
        grad_output,
        small[16, 8:].reshape(-1),
        grad_router,
        grad_gate,
        grad_up,
        grad_down,
    )


def solution(mesh):
    return jax.shard_map(
        shards,
        mesh=mesh,
        in_specs=(
            P(("ep", "tp"), None),
            P(),
            P(None, "tp"),
            P(None, "tp"),
            P(None, "tp"),
            P(),
            P(),
            P("tp", None),
            P(),
            P(),
            P("ep", None, "tp"),
            P("ep", None, "tp"),
            P("ep", "tp", None),
            P("ep"),
            P("ep"),
            P(("ep", "tp"), None),
            P(("ep", "tp"), None),
        ),
        out_specs=(
            P(("ep", "tp"), None),
            P(("ep", "tp"), None),
            P(),
            P(None, "tp"),
            P(None, "tp"),
            P(None, "tp"),
            P(),
            P(),
            P("tp", None),
            P(),
            P(),
            P("ep", None, "tp"),
            P("ep", None, "tp"),
            P("ep", "tp", None),
        ),
        check_vma=False,
    )
```

time: 495 us -> 369 us (0.75)
  Pallas kernels: 410 us -> 348 us
  matrix products: 22 us -> 0 us
  local copies, waits for them, and re-layouts: 25.3 us -> 9.95 us
  between operations: 15.3 us -> 1.2 us
  other arithmetic: 16.5 us -> 3.96 us
    pallas_call x9 -> x5, Pallas kernels: 347 us -> 286 us  [the longest x1 109 us: closing(): pl.pallas_call(closing_kernel, out_shape=[jax.ShapeDtypeStruct((256, 1024...]
    dot_general x11 -> x0, matrix products: 22 us -> none  [the longest x1 3.42 us: shards(): lax.dot_general(grad_logits, router_float, CONTRACT_LAST, precision=HIGHE...]
    convert_element_type x14 -> x0, other arithmetic: 7.33 us -> none  [the longest x1 3.02 us: shards(): grad_inputs = (grad_residual + grad_hidden_norm).astype(BF16)]
    slice x7 -> x1, local copies, waits for them, and re-layouts: 6.73 us -> 0.01 us  [shards(): small[:16].reshape(8, 32, 128).transpose(0, 2, 1).reshape(1024, 32)]
    unnamed x132 -> x19, local copies, waits for them, and re-layouts: 8.85 us -> 3.45 us
  transfers between devices with their start and end apart: 5 -> 0, of which waited for: 0 -> 0; matrix products, arithmetic and copies ran while one was open for 11% -> 0% of each run, Pallas kernels for 71% -> 0%
where the time goes in v2:
time: 369 us; the launch traced here: 363 us
  Pallas kernels  348 us (94%)
  local copies, waits for them, and re-layouts  9.95 us (3%)
  other arithmetic  3.96 us (1%)
    pallas_call x1, Pallas kernels, closing(): pl.pallas_call(closing_kernel, out_shape=[jax.ShapeDtypeStruct((256, 1024...  109 us
    pallas_call x1, Pallas kernels, run_experts(): pl.pallas_call(experts_kernel, out_shape=[jax.ShapeDtypeStruct((sources,...  62.8 us
    pallas_call x1, Pallas kernels, opening(): pl.pallas_call(opening_kernel, out_shape=[jax.ShapeDtypeStruct((4, 256, 1...  62.4 us
    pallas_call x1, Pallas kernels, dispatch(): pl.pallas_call(dispatch_kernel, out_shape=[jax.ShapeDtypeStruct((32,) + o...  56 us
    pallas_call x1, Pallas kernels, collect(): pl.pallas_call(collect_kernel, out_shape=[jax.ShapeDtypeStruct((rows, col...  55.3 us

profile of v2, /device:TPU:1, one launch (start us, length us, event | category | flops | bytes accessed | tf_op | source)
XLA Modules:
  0.0 363.5 jit_solution(9597881624937526411)
XLA Ops:
  0.6 1.7 copy.34.seg_column
  2.4 1.3 reshape.90
  3.6 1.3 reshape.92
  4.9 0.7 tile.4
  5.6 0.6 reshape_tile.6.query_gain
  6.2 0.7 tile.5
  6.8 0.6 reshape_tile.7.key_gain
  7.4 0.0 copy-start.5
  7.4 62.4 %opening.1 = (bf16[4,256,1024]{2,1,0:T(8,128)(2,1)}, f32[1024,384]{1,0:T(8,128)}, bf16[1024,256]{1,0:T(8,128)(2,1)}, bf16[1024,128]{1,0:T(8,128)(2,1)}, bf16[102...) custom-call(bf16[256,1024]{1,0:T(8,128)(2,1)} %inputs.3, ...), custom_call_target="tpu_custom_call" | custom-call | tf_op jit(solution)/shard_map/opening/pallas_call | solution.py:710
  69.9 0.0 copy-done.5
  69.9 0.0 copy-done.6
  69.9 0.8 pad_maximum_fusion.pair_ref
  70.7 56.0 %dispatch.1 = (bf16[32,272,1024]{2,1,0:T(8,128)(2,1)}, bf16[4,2048,128]{2,1,0:T(8,128)(2,1)}, bf16[4,128,1024]{2,1,0:T(8,128)(2,1)}) custom-call(bf16[272,1024]{1,0:T(8,128)(2,1)} %get-tuple-element.44.own_ref, bf16[2048,128]{1,0:T(8,128)(2,1)} %pad_maximum_fusion.pair_ref, bf16[128,1024]{1,0:T(8,128)(2,1)} %bitcast.38), custom_call_target="tpu_custom_call" | custom-call | tf_op jit(solution)/shard_map/dispatch/pallas_call | solution.py:467
  126.7 62.8 %run_experts.1 = (bf16[32,256,1024]{2,1,0:T(8,128)(2,1)}, bf16[32,272,1024]{2,1,0:T(8,128)(2,1)}, bf16[4,3072,128]{2,1,0:T(8,128)(2,1)}) custom-call(s32[1]{0:T(128)} %bitcast.number_ref, bf16[32,272,1024]{2,1,0:T(8,128)(2,1)} %get-tuple-element.45.rows_ref, bf16[32,256,1024]{2,1,0:T(8,128)(2,1)} %get-tuple-element.46.grads_ref, ...), custom_call_target="tpu_custom_call" | custom-call | tf_op jit(solution)/shard_map/run_experts/pallas_call | solution.py:1141
  189.5 0.0 copy-start.8
  189.5 55.3 %collect.1 = (f32[272,1024]{1,0:T(8,128)}, f32[3072,128]{1,0:T(8,128)}) custom-call(bf16[32,272,1024]{2,1,0:T(8,128)(2,1)} %get-tuple-element.49.parts_ref, bf16[4,3072,128]{2,1,0:T(8,128)(2,1)} %get-tuple-element.50.weights_ref), custom_call_target="tpu_custom_call" | custom-call | tf_op jit(solution)/shard_map/collect/pallas_call | solution.py:517
  244.8 0.0 copy-done.8
  244.8 1.0 copy.36.live_column
  245.8 0.0 copy-start
  245.8 109.3 %closing.1 = (bf16[256,1024]{1,0:T(8,128)(2,1)}, bf16[32,32,768]{2,1,0:T(8,128)(2,1)}, f32[32,16,128]{2,1,0:T(8,128)}, f32[256,1024]{1,0:T(8,128)}) custom-call(f32[272,1024]{1,0:T(8,128)} %get-tuple-element.51.back, f32[256,1024]{1,0:T(8,128)} %get-tuple-element.52.residual, f32[32,256]{1,0:T(8,128)} %get-tuple-element.53.gates, ...), custom_call_target="tpu_custom_call" | custom-call | tf_op jit(solution)/shard_map/closing/pallas_call | solution.py:952
  355.1 0.0 copy-done
  355.2 0.0 copy-done.1
  355.2 0.0 copy-start.2
  355.2 1.4 copy-done.2
  356.6 1.2 copy-done.3
  357.8 2.5 finish_all.1
  360.4 0.0 copy-done.7
  360.4 0.7 copy.40
  361.0 0.6 slice_bitcast_fusion
  361.6 0.6 add_bitcast_fusion
  362.2 0.0 copy-done.4
  362.2 0.8 copy.42
  (6 shorter events, 0.0 us)
Async XLA Ops:
  7.4 62.5 %copy-start.5 = (bf16[1,1024,128]{2,1,0:T(8,128)(2,1)S(1)}, bf16[1,1024,128]{2,1,0:T(8,128)(2,1)}, u32[]{:S(2)}) copy-start(bf16[1,1024,128]{2,1,0:T(8,128)(2,1)} %param.30) | copy-start | bytes 786436
  7.4 62.5 %copy-start.6 = (bf16[1,1024,128]{2,1,0:T(8,128)(2,1)S(1)}, bf16[1,1024,128]{2,1,0:T(8,128)(2,1)}, u32[]{:S(2)}) copy-start(bf16[1,1024,128]{2,1,0:T(8,128)(2,1)} %param.29) | copy-start | bytes 786436
  189.5 55.3 %copy-start.8 = (s32[1024]{0:T(1024)S(1)}, s32[1024]{0:T(1024)}, u32[]{:S(2)}) copy-start(s32[1024]{0:T(1024)} %param.33) | copy-start | bytes 12292
  245.8 109.3 %copy-start = (f32[256,1024]{1,0:T(8,128)S(1)}, f32[256,1024]{1,0:T(8,128)}, u32[]{:S(2)}) copy-start(f32[256,1024]{1,0:T(8,128)} %get-tuple-element.52.residual) | copy-start | bytes 3145732
  245.8 109.3 %copy-start.1 = (f32[3072,128]{1,0:T(8,128)S(1)}, f32[3072,128]{1,0:T(8,128)}, u32[]{:S(2)}) copy-start(f32[3072,128]{1,0:T(8,128)} %get-tuple-element.62.weights) | copy-start | bytes 4718596
  355.2 1.4 copy-start.2
  356.6 1.2 copy-start.3
  357.8 2.6 copy-start.7
  357.8 4.4 %copy-start.4 = (bf16[256,1024]{1,0:T(8,128)(2,1)S(1)}, bf16[256,1024]{1,0:T(8,128)(2,1)}, u32[]{:S(2)}) copy-start(bf16[256,1024]{1,0:T(8,128)(2,1)} %get-tuple-element.93) | copy-start | bytes 1572868

commit v3 on v2

--- a/solution.py
+++ b/solution.py
@@ -72,16 +72,94 @@
 
 
 def together(*tasks):
-    tasks = list(tasks)
-    while tasks:
-        for task in list(tasks):
-            if next(task, "ended") == "ended":
-                tasks.remove(task)
-
-
-def chain(*tasks):
-    for task in tasks:
-        yield from task
+    waiting = [(0.0, number, task) for number, task in enumerate(tasks)]
+    while waiting:
+        waiting.sort(key=lambda entry: entry[:2])
+        _, number, task = waiting.pop(0)
+        due = next(task, None)
+        if due is not None:
+            waiting.append((due, number, task))
+
+
+def resumed(due, task):
+    yield due
+    yield from task
+
+
+def until_count(task, count):
+    for number in range(count):
+        due = next(task)
+        if number < count - 1:
+            yield due
+    return due
+
+
+def side_by_side(*tasks):
+    waiting = [(due, number, task) for number, (due, task) in enumerate(tasks)]
+    while waiting:
+        waiting.sort(key=lambda entry: entry[:2])
+        due, number, task = waiting.pop(0)
+        yield due
+        due = next(task, None)
+        if due is not None:
+            waiting.append((due, number, task))
+
+
+class Clock:
+    def __init__(self, now=0.0):
+        self.now = now
+
+    def spend(self, amount):
+        self.now += amount
+        return self.now
+
+    def until(self, moment):
+        self.now = max(self.now, moment)
+        return self.now
+
+
+def at(ref, *where):
+    return lambda: ref.at[where]
+
+
+def part_of(place):
+    return place() if callable(place) else place
+
+
+class Remote:
+    def __init__(self, src, dst, send_sem, recv_sem, partner):
+        self.all = (src, dst, send_sem, recv_sem, partner)
+
+    def copy(self):
+        src, dst, send_sem, recv_sem, partner = self.all
+        return pltpu.make_async_remote_copy(
+            src_ref=part_of(src),
+            dst_ref=part_of(dst),
+            send_sem=part_of(send_sem),
+            recv_sem=part_of(recv_sem),
+            device_id=partner,
+            device_id_type=MESH,
+        )
+
+    def start(self):
+        self.copy().start()
+
+    def wait_send(self):
+        self.copy().wait_send()
+
+    def wait_recv(self):
+        self.copy().wait_recv()
+
+
+class Local:
+    def __init__(self, src, dst, sem):
+        self.all = (src, dst, sem)
+
+    def start(self):
+        pltpu.make_async_copy(*map(part_of, self.all)).start()
+
+    def wait(self):
+        pltpu.make_async_copy(*map(part_of, self.all)).wait()
 
 
 class Post:
@@ -89,16 +167,13 @@
         self.send_sems, self.recv_sems, self.started = send_sems, recv_sems, []
 
     def go(self, src, dst, partner):
+        copy = self.prepare(src, dst, partner)
+        copy.start()
+        return copy
+
+    def prepare(self, src, dst, partner):
         number = len(self.started)
-        copy = pltpu.make_async_remote_copy(
-            src_ref=src,
-            dst_ref=dst,
-            send_sem=self.send_sems.at[number],
-            recv_sem=self.recv_sems.at[number],
-            device_id=partner,
-            device_id_type=MESH,
-        )
-        copy.start()
+        copy = Remote(src, dst, at(self.send_sems, number), at(self.recv_sems, number), partner)
         self.started.append(copy)
         return copy
 
@@ -107,68 +182,89 @@
             copy.wait_send()
 
 
+ARRIVAL = (
+    (0, 0), (-1, 0), (1, 0), (0, -1), (0, 1), (2, 0), (-1, -1), (-1, 1),
+    (1, -1), (1, 1), (2, -1), (2, 1), (0, 2), (-1, 2), (1, 2), (2, 2),
+)
+
+
+def plane_gather_events(post, own_ref, all_ref):
+    a, b, core = plane_place()
+    ahead_a, behind_a, ahead_b, behind_b, sibling = plane_partners()
+    index = {place: plane_index(a + place[0], b + place[1], core) for place in ARRIVAL}
+    top, bottom = halves(own_ref)
+
+    def block(place):
+        return own_ref if place == (0, 0) else at(all_ref, index[place])
+
+    def copy(place, partner):
+        return post.prepare(block(place), at(all_ref, index[place]), partner)
+
+    def half_copy(place, half, partner):
+        part = at(all_ref, index[place], half)
+        return post.prepare(part, part, partner)
+
+    a_copies = (copy((0, 0), ahead_a), copy((0, 0), behind_a))
+    a_halves = (half_copy((-1, 0), top, ahead_a), half_copy((1, 0), bottom, behind_a))
+    column = (0, -1, 1, 2)
+    b_copies = [(copy((k, 0), ahead_b), copy((k, 0), behind_b)) for k in column]
+    b_halves = [
+        (half_copy((k, -1), top, ahead_b), half_copy((k, 1), bottom, behind_b)) for k in column
+    ]
+    crossing = [copy(place, sibling) for place in ARRIVAL]
+
+    def start(*copies):
+        for one in copies:
+            one.start()
+
+    def begin():
+        start(*a_copies, *b_copies[0], crossing[0])
+
+    def near_a(number):
+        a_copies[number].wait_recv()
+        start(a_halves[number], *b_copies[1 + number], crossing[1 + number])
+
+    def far_a():
+        a_halves[0].wait_recv()
+        a_halves[1].wait_recv()
+        start(*b_copies[3], crossing[5])
+
+    def near_b(k):
+        first = ARRIVAL.index((column[k], -1))
+        for number in range(2):
+            b_copies[k][number].wait_recv()
+            start(b_halves[k][number], crossing[first + number])
+
+    def far_b(k):
+        b_halves[k][0].wait_recv()
+        b_halves[k][1].wait_recv()
+        start(crossing[12 + k])
+
+    events = [
+        (0.0, begin),
+        (6.5, lambda: near_a(0)),
+        (6.5, lambda: near_a(1)),
+        (7.5, lambda: near_b(0)),
+        (11.0, far_a),
+        (15.0, lambda: near_b(1)),
+        (21.0, lambda: near_b(2)),
+        (24.0, lambda: far_b(0)),
+        (28.0, lambda: near_b(3)),
+        (32.0, lambda: far_b(1)),
+        (40.0, lambda: far_b(2)),
+        (44.0, lambda: far_b(3)),
+    ]
+    return (events, crossing)
+
+
 def plane_gather_steps(post, own_ref, all_ref):
-    a, b, core = plane_place()
-    me = plane_index(a, b, core)
-    ahead_a, behind_a, ahead_b, behind_b, sibling = plane_partners()
-    top, bottom = halves(own_ref)
-    go = post.go
-    a_ahead = go(own_ref, all_ref.at[me], ahead_a)
-    a_behind = go(own_ref, all_ref.at[me], behind_a)
-
-    def along_b(src, index):
-        return (go(src, all_ref.at[index], ahead_b), go(src, all_ref.at[index], behind_b))
-
-    def across(src, index):
-        return go(src, all_ref.at[index], sibling)
-
-    b_copies = {0: along_b(own_ref, me)}
-    others = [across(own_ref, me)]
-    from_behind = plane_index(a - 1, b, core)
-    from_ahead = plane_index(a + 1, b, core)
-    from_far = plane_index(a + 2, b, core)
-    yield
-    a_ahead.wait_recv()
-    far_top = go(all_ref.at[from_behind, top], all_ref.at[from_behind, top], ahead_a)
-    b_copies[1] = along_b(all_ref.at[from_behind], from_behind)
-    yield
-    a_behind.wait_recv()
-    far_bottom = go(all_ref.at[from_ahead, bottom], all_ref.at[from_ahead, bottom], behind_a)
-    others.append(across(all_ref.at[from_behind], from_behind))
-    b_copies[2] = along_b(all_ref.at[from_ahead], from_ahead)
-    others.append(across(all_ref.at[from_ahead], from_ahead))
-    column = (a, a - 1, a + 1, a + 2)
-    fars = {}
-
-    def onward(k):
-        below = plane_index(column[k], b - 1, core)
-        above = plane_index(column[k], b + 1, core)
-        yield
-        b_copies[k][0].wait_recv()
-        first = go(all_ref.at[below, top], all_ref.at[below, top], ahead_b)
-        b_copies[k][1].wait_recv()
-        second = go(all_ref.at[above, bottom], all_ref.at[above, bottom], behind_b)
-        fars[k] = (first, second)
-        others.append(across(all_ref.at[below], below))
-        others.append(across(all_ref.at[above], above))
-
-    yield from onward(0)
-    yield
-    far_top.wait_recv()
-    far_bottom.wait_recv()
-    b_copies[3] = along_b(all_ref.at[from_far], from_far)
-    others.append(across(all_ref.at[from_far], from_far))
-    yield from onward(1)
-    yield from onward(2)
-    yield from onward(3)
-    for k in range(4):
-        index = plane_index(column[k], b + 2, core)
-        yield
-        fars[k][0].wait_recv()
-        fars[k][1].wait_recv()
-        others.append(across(all_ref.at[index], index))
-    yield
-    for copy in others:
+    events, crossing = plane_gather_events(post, own_ref, all_ref)
+    for due, event in events:
+        if due > 0.0:
+            yield due
+        event()
+    yield 46.0
+    for copy in crossing:
         copy.wait_recv()
 
 
@@ -188,7 +284,7 @@
         dst[pl.ds(start + at, step), :] = total.astype(dst.dtype)
 
 
-def plane_scatter_steps(post, parts_ref, sum_ref, scratch):
+def plane_scatter_steps(post, parts_ref, sum_ref, scratch, begin=0.0):
     mine, other, b_far, b_near, a_far, a_near, local_sems = scratch
     a, b, core = plane_place()
     ahead_a, behind_a, ahead_b, behind_b, sibling = plane_partners()
@@ -230,8 +326,8 @@
         return (other.at[k, j], mine.at[number % slots])
 
     far_b, near_b = {}, {}
-    yield
     for k in range(4):
+        yield begin + 2.0 + 1.5 * k
         block, extra = ready(k, 0)
         add_rows(block, [(block, 0), (extra, 0)], 0, rows)
         far_b[k] = (
@@ -240,7 +336,7 @@
         )
     for k in range(4):
         far = b_far.at[k]
-        yield
+        yield begin + 9.0 + 3.0 * k
         block, extra = ready(k, 1)
         far_b[k][0].wait_recv()
         add_rows(block, [(block, 0), (extra, 0), (far, 0)], 0, high)
@@ -253,7 +349,7 @@
         near_b[k] = (first, go(block, b_near.at[1, k], behind_b))
     far_a, near_a = [], []
     for k in range(4):
-        yield
+        yield begin + (25.0, 31.0, 37.0, 45.0)[k]
         block, extra = ready(k, 3)
         near_b[k][0].wait_recv()
         near_b[k][1].wait_recv()
@@ -312,7 +408,7 @@
 BRIEF_COPIES = 16 + 12 + 3
 
 
-def brief_scatter_steps(post, parts_ref, sum_ref, scratch):
+def brief_scatter_steps(post, parts_ref, sum_ref, scratch, begin=0.0):
     other, from_b, from_a = scratch
     a, b, core = plane_place()
     along_a, along_b, sibling = ring_places(a, b, core, lax.axis_index("tp"))
@@ -322,7 +418,7 @@
         for j in range(4):
             there = plane_index(b + OFFSETS[k], a + OFFSETS[j], 1 - core)
             crossing[k, j] = go(parts_ref.at[there], other.at[k, j], sibling)
-    yield
+    yield begin + 3.0
     for k in range(4):
         for j in range(4):
             here = plane_index(a + OFFSETS[k], b + OFFSETS[j], core)
@@ -331,7 +427,7 @@
             block[...] = (block[...].astype(F32) + parts_ref[here].astype(F32)).astype(block.dtype)
             if j < 3:
                 copies_b[k, j] = go(block, from_b.at[k, j], along_b[j])
-    yield
+    yield begin + 6.5
     for k in range(4):
         total = other[k, 3].astype(F32)
         for j in range(3):
@@ -340,7 +436,7 @@
         if k < 3:
             other[k, 3] = total.astype(other.dtype)
             copies_a[k] = go(other.at[k, 3], from_a.at[k], along_a[k])
-    yield
+    yield begin + 10.0
     for k in range(3):
         copies_a[k].wait_recv()
         total = total + from_a[k].astype(F32)
@@ -355,7 +451,7 @@
     ]
 
 
-def brief_gather_steps(post, own_ref, all_ref):
+def brief_gather_steps(post, own_ref, all_ref, begin=0.0):
     a, b, core = plane_place()
     along_a, along_b, sibling = ring_places(a, b, core, lax.axis_index("tp"))
     go = post.go
@@ -368,18 +464,18 @@
         crossing.append(go(src, all_ref.at[index], sibling))
 
     onward(own_ref, me)
-    yield
+    yield begin + 3.0
     for k in range(3):
         index = plane_index(a - OFFSETS[k], b, core)
         copies_a[k].wait_recv()
         onward(all_ref.at[index], index)
-    yield
+    yield begin + 6.0
     for k, offset in enumerate((0, 2, 1, -1)):
         for j in range(3):
             index = plane_index(a - offset, b - OFFSETS[j], core)
             copies_b[3 * k + j].wait_recv()
             crossing.append(go(all_ref.at[index], all_ref.at[index], sibling))
-    yield
+    yield begin + 9.0
     for copy in crossing:
         copy.wait_recv()
 
@@ -387,155 +483,55 @@
 LINE_COPIES = 4
 
 
-def line_gather_steps(post, own_ref, all_ref, arrived=None):
+def line_gather_steps(post, own_ref, all_ref, clock, near_time, far_time, arrived=None):
     tp = lax.axis_index("tp")
     ahead, behind = line_partners()
     top, bottom = halves(own_ref)
     before, after, far = wrap(tp - 1), wrap(tp + 1), wrap(tp + 2)
+    begin = clock.now
     first = post.go(own_ref, all_ref.at[tp], ahead)
     second = post.go(own_ref, all_ref.at[tp], behind)
     if arrived is not None:
-        arrived(tp)
-    yield
+        yield from arrived(tp)
+    yield clock.until(begin + near_time)
     first.wait_recv()
     third = post.go(all_ref.at[before, top], all_ref.at[before, top], ahead)
     second.wait_recv()
     fourth = post.go(all_ref.at[after, bottom], all_ref.at[after, bottom], behind)
     if arrived is not None:
-        yield
-        arrived(before)
-        yield
-        arrived(after)
-    yield
+        yield from arrived(before)
+        yield from arrived(after)
+    yield clock.until(begin + far_time)
     third.wait_recv()
     fourth.wait_recv()
     if arrived is not None:
-        arrived(far)
-
-
-def line_scatter_steps(post, make, far, near, finish):
+        yield from arrived(far)
+
+
+def line_scatter_steps(post, make, far, near, finish, clock, far_time, near_time):
     ahead, behind = line_partners()
     top, bottom = halves(far)
     high = top.size
     rows = far.shape[0]
-    block = make(2)
+    block = yield from make(2)
+    begin = clock.now
     first = post.go(block.at[top], far.at[top], ahead)
     second = post.go(block.at[bottom], far.at[bottom], behind)
-    yield
-    block = make(1)
-    yield
+    block = yield from make(1)
+    yield clock.until(begin + far_time)
     first.wait_recv()
     add_rows(block, [(block, 0), (far, 0)], 0, high)
     third = post.go(block, near.at[0], ahead)
-    other = make(-1)
-    yield
+    other = yield from make(-1)
     second.wait_recv()
     add_rows(other, [(other, high), (far, high)], high, rows - high)
     fourth = post.go(other, near.at[1], behind)
-    own = make(0)
-    yield
+    begin = clock.now
+    own = yield from make(0)
+    yield clock.until(begin + near_time)
     third.wait_recv()
     fourth.wait_recv()
     finish(own, near.at[0], near.at[1])
-
-
-def dispatch_kernel(own_ref, pair_ref, down_ref, all_ref, pair_all, down_all, *rest):
-    send_sems, recv_sems, local_sems = rest
-    me = lax.axis_index("ep")
-    tp = lax.axis_index("tp")
-    greet(plane_partners() + line_partners())
-    post = Post(send_sems, recv_sems)
-    locals_ = [
-        pltpu.make_async_copy(own_ref, all_ref.at[me], local_sems.at[0]),
-        pltpu.make_async_copy(pair_ref, pair_all.at[tp], local_sems.at[1]),
-        pltpu.make_async_copy(down_ref, down_all.at[tp], local_sems.at[2]),
-    ]
-    for copy in locals_:
-        copy.start()
-    together(
-        plane_gather_steps(post, own_ref, all_ref),
-        line_gather_steps(post, pair_ref, pair_all),
-        line_gather_steps(post, down_ref, down_all),
-    )
-    post.finish()
-    for copy in locals_:
-        copy.wait()
-
-
-def dispatch(own, pair, down, number):
-    count = PLANE_COPIES + 2 * LINE_COPIES
-    return pl.pallas_call(
-        dispatch_kernel,
-        out_shape=[
-            jax.ShapeDtypeStruct((32,) + own.shape, own.dtype),
-            jax.ShapeDtypeStruct((4,) + pair.shape, pair.dtype),
-            jax.ShapeDtypeStruct((4,) + down.shape, down.dtype),
-        ],
-        in_specs=[ANY] * 3,
-        out_specs=[ANY] * 3,
-        scratch_shapes=[
-            pltpu.SemaphoreType.DMA((count,)),
-            pltpu.SemaphoreType.DMA((count,)),
-            pltpu.SemaphoreType.DMA((3,)),
-        ],
-        compiler_params=pltpu.CompilerParams(collective_id=number, has_side_effects=True),
-        name="dispatch",
-    )(own, pair, down)
-
-
-def collect_kernel(parts_ref, weights_ref, sum_ref, weight_sum, *rest):
-    send_sems, recv_sems = rest[-2:]
-    line, line_far, line_near, line_sems = rest[7:11]
-    tp = lax.axis_index("tp")
-    loads = {}
-    for number, offset in enumerate((2, 1, -1, 0)):
-        loads[offset] = pltpu.make_async_copy(
-            weights_ref.at[wrap(tp + offset)], line.at[number], line_sems.at[number]
-        )
-        loads[offset].start()
-    greet(plane_partners() + line_partners())
-    post = Post(send_sems, recv_sems)
-
-    def make(offset):
-        loads[offset].wait()
-        return line.at[(2, 1, -1, 0).index(offset)]
-
-    def finish(own, first, second):
-        add_rows(weight_sum, [(own, 0), (first, 0), (second, 0)], 0, own.shape[0])
-
-    together(
-        plane_scatter_steps(post, parts_ref, sum_ref, rest[:7]),
-        line_scatter_steps(post, make, line_far, line_near, finish),
-    )
-    post.finish()
-
-
-def collect(parts, weights, number):
-    _, rows, columns = parts.shape
-    _, weight_rows, weight_columns = weights.shape
-    count = PLANE_COPIES + LINE_COPIES
-    return pl.pallas_call(
-        collect_kernel,
-        out_shape=[
-            jax.ShapeDtypeStruct((rows, columns), F32),
-            jax.ShapeDtypeStruct((weight_rows, weight_columns), F32),
-        ],
-        in_specs=[ANY, ANY],
-        out_specs=[VMEM, VMEM],
-        scratch_shapes=plane_scatter_scratch(rows, columns, parts.dtype)
-        + [
-            pltpu.VMEM((4, weight_rows, weight_columns), BF16),
-            pltpu.VMEM((weight_rows, weight_columns), BF16),
-            pltpu.VMEM((2, weight_rows, weight_columns), BF16),
-            pltpu.SemaphoreType.DMA((4,)),
-            pltpu.SemaphoreType.DMA((count,)),
-            pltpu.SemaphoreType.DMA((count,)),
-        ],
-        compiler_params=pltpu.CompilerParams(
-            collective_id=number, has_side_effects=True, vmem_limit_bytes=56 << 20
-        ),
-        name="collect",
-    )(parts, weights)
 
 
 def split_float(values):
@@ -608,7 +604,7 @@
     return jnp.concatenate([left, right], axis=1)
 
 
-def attend_block(query, keys, values, bias):
+def attend_block(query, keys, values, bias, clock):
     rows = query.shape[0]
     outs = []
     for pair, key_part, value_part in zip(
@@ -622,27 +618,63 @@
             total_weight = jnp.sum(weights, axis=1, keepdims=True)
             out = jnp.dot(weights.astype(BF16), value_part, preferred_element_type=F32)
             halves_out.append(out / total_weight)
+            yield clock.spend(0.45)
         outs.append(jnp.concatenate(halves_out, axis=0))
     return heads_back(*outs).astype(BF16)
 
 
+def document_bounds(segments, live_mask):
+    one = jnp.ones_like(segments)
+    zero = jnp.zeros_like(segments)
+
+    def count(chosen):
+        return jnp.sum(jnp.where(chosen, one, zero), axis=1, keepdims=True)
+
+    return (count(segments < 1), count(segments < 2), count(live_mask == 1))
+
+
+def score_bias(bounds, query, key):
+    first, second, living = bounds
+
+    def document(position):
+        return (position >= first).astype(jnp.int32) + (position >= second).astype(jnp.int32)
+
+    seen = jnp.where(key < living, 1, 0)
+    same = document(query) == document(key)
+    return jnp.where(same & ((seen == 1) | (query == key)), 0.0, -1e30).astype(F32)
+
+
 def block_rows(block):
     return pl.ds(pl.multiple_of(block * 256, 256), 256)
 
 
 def opening_kernel(
     inputs, gain_one, query_weight, key_weight, value_weight, query_gain, key_gain, cosine, sine,
-    seg_column, seg_row, live_row, output_weight, gain_two, router, routes, cotangent,
+    segments, live_mask, output_weight, gain_two, router, routes, cotangent,
+    gate,
     normed, raw, query, keys, values, mixed, residual, block, gates, grad_all,
-    parts, far, near, send_sems, recv_sems, local_sem,
+    gate_all,
+    parts, far, near, hold, send_sems, recv_sems, local_sems,
 ):
     tp = lax.axis_index("tp")
-    local = pltpu.make_async_copy(cotangent, grad_all.at[lax.axis_index("ep")], local_sem)
-    local.start()
-    hidden = inputs[...].astype(F32)
-    normed[tp] = (hidden * row_scale(hidden) * gain_one[...]).astype(BF16)
+    own_parts = (
+        (cotangent, parts.at[0], grad_all.at[lax.axis_index("ep")]),
+        (gate, hold, gate_all.at[tp]),
+    )
+    inward = [
+        pltpu.make_async_copy(src, through, local_sems.at[number])
+        for number, (src, through, _) in enumerate(own_parts)
+    ]
+    outward = [
+        pltpu.make_async_copy(through, dst, local_sems.at[number])
+        for number, (_, through, dst) in enumerate(own_parts)
+    ]
+    for copy in inward:
+        copy.start()
     greet(plane_partners() + line_partners())
     post = Post(send_sems, recv_sems)
+    clock = Clock()
+    bounds = document_bounds(segments[...], live_mask[...])
 
     def project(place):
         rows = block_rows(place)
@@ -656,20 +688,21 @@
         raw[rows, 256:] = one
         keys[rows, :] = head_ready(one, key_gain[...], cos, sin).astype(BF16)
         values[rows, :] = jnp.dot(part, value_weight[...], preferred_element_type=F32).astype(BF16)
+        yield clock.spend(1.5)
 
     def make(offset):
         place = wrap(tp + offset)
         rows = block_rows(place)
-        position = place * 256 + lax.broadcasted_iota(jnp.int32, (256, 1024), 0)
-        key_position = lax.broadcasted_iota(jnp.int32, (256, 1024), 1)
-        allowed = (seg_column[rows, :] == seg_row[...]) & (
-            (live_row[...] == 1) | (position == key_position)
-        )
-        bias = jnp.where(allowed, 0.0, -1e30).astype(F32)
-        out = attend_block(query[rows, :], keys[...], values[...], bias)
+        bias = score_bias(
+            bounds,
+            place * 256 + lax.broadcasted_iota(jnp.int32, (256, 1), 0),
+            lax.broadcasted_iota(jnp.int32, (1, 1024), 1),
+        )
+        out = yield from attend_block(query[rows, :], keys[...], values[...], bias, clock)
         mixed[rows, :] = out
         part = parts.at[(2, 1, -1, 0).index(offset)]
         part[...] = jnp.dot(out, output_weight[...], preferred_element_type=F32).astype(BF16)
+        yield clock.spend(0.4)
         return part
 
     def finish(own, first, second):
@@ -694,19 +727,32 @@
         high, low = split_float(probs)
         block[256:, :] = jnp.concatenate([high[:16], low[:16], high[16:], low[16:]], axis=1)
 
+    def attention_steps():
+        hidden = inputs[...].astype(F32)
+        normed[tp] = (hidden * row_scale(hidden) * gain_one[...]).astype(BF16)
+        for copy, onward in zip(inward, outward, strict=True):
+            copy.wait()
+            onward.start()
+        clock.spend(1.0)
+        yield from line_gather_steps(post, normed.at[tp], normed, clock, 11.5, 17.5, project)
+        for copy in outward:
+            copy.wait()
+        yield from line_scatter_steps(post, make, far, near, finish, clock, 3.0, 12.0)
+
+    def weight_steps(own, everyone, begin, near_time, far_time):
+        yield begin
+        yield from line_gather_steps(post, own, everyone, Clock(begin), near_time, far_time)
+
     together(
-        chain(
-            line_gather_steps(post, normed.at[tp], normed, project),
-            line_scatter_steps(post, make, far, near, finish),
-        ),
+        attention_steps(),
         plane_gather_steps(post, cotangent, grad_all),
+        weight_steps(gate, gate_all, 20.5, 22.0, 32.0),
     )
     post.finish()
-    local.wait()
 
 
 def opening(arguments, number):
-    count = 2 * LINE_COPIES + PLANE_COPIES
+    count = 3 * LINE_COPIES + PLANE_COPIES
     return pl.pallas_call(
         opening_kernel,
         out_shape=[
@@ -720,16 +766,18 @@
             jax.ShapeDtypeStruct((256 + EXTRA, 1024), BF16),
             jax.ShapeDtypeStruct((32, 256), F32),
             jax.ShapeDtypeStruct((32, 256, 1024), BF16),
+            jax.ShapeDtypeStruct((4, 1024, 128), BF16),
         ],
-        in_specs=[VMEM] * (len(arguments) - 1) + [ANY],
-        out_specs=[VMEM] * 9 + [ANY],
+        in_specs=[VMEM] * (len(arguments) - 2) + [ANY] * 2,
+        out_specs=[VMEM] * 9 + [ANY] * 2,
         scratch_shapes=[
             pltpu.VMEM((4, 256, 1024), BF16),
             pltpu.VMEM((256, 1024), BF16),
             pltpu.VMEM((2, 256, 1024), BF16),
+            pltpu.VMEM((1024, 128), BF16),
             pltpu.SemaphoreType.DMA((count,)),
             pltpu.SemaphoreType.DMA((count,)),
-            pltpu.SemaphoreType.DMA,
+            pltpu.SemaphoreType.DMA((2,)),
         ],
         compiler_params=pltpu.CompilerParams(
             collective_id=number, has_side_effects=True, vmem_limit_bytes=56 << 20
@@ -738,7 +786,7 @@
     )(*arguments)
 
 
-def attend_back_block(query, grad, keys, values, bias, keys_sum, values_sum):
+def attend_back_block(query, grad, keys, values, bias, keys_sum, values_sum, clock):
     rows = query.shape[0]
     query_pairs = head_pairs(query)
     grad_pairs = head_pairs(grad)
@@ -769,6 +817,7 @@
             values_sum[side] += jnp.dot(
                 weights.astype(BF16), grad_part, preferred_element_type=F32
             )
+            yield clock.spend(1.4)
         outs.append(jnp.concatenate(halves_out, axis=0))
     return heads_back(*outs) * 0.125
 
@@ -779,10 +828,11 @@
 def closing_kernel(
     back, residual, gates, cotangent, gain_two, router, query, keys, values, mixed,
     output_weight, query_weight, key_weight, value_weight, raw, normed, inputs, gain_one,
-    query_gain, key_gain, cosine, sine, seg_column, seg_row, live_column, out_parts,
+    query_gain, key_gain, cosine, sine, segments, live_mask, out_parts,
     grad_inputs, dense_all, small_all, combined,
     grad_all, grad_residual, low, keys_sum, values_sum, output_sum, parts, far, near,
-    dense, dense_own, small, small_own, small_line, small_sum, query_gain_sum, gain_one_sum, *rest,
+    dense, dense_own, small, small_own, small_line, small_sum, query_gain_sum, gain_one_sum,
+    *rest,
 ):
     out_scratch, dense_scratch, small_scratch = rest[:7], rest[7:10], rest[10:13]
     post = Post(rest[13], rest[14])
@@ -790,6 +840,10 @@
     tp = lax.axis_index("tp")
     ahead, behind = line_partners()
     across = (me, wrap(tp + 2))
+    greet(brief_partners() + (ahead, behind, across))
+    clock = Clock()
+    out_steps = plane_scatter_steps(post, out_parts, combined, out_scratch)
+    out_due = next(out_steps)
 
     lines = back[256:, :]
     grad_gates = jnp.concatenate(
@@ -807,20 +861,15 @@
     scale = row_scale(total)
     plain = total * scale
     grad_gain_two = jnp.sum(grad_two * plain, axis=0, keepdims=True)
-    normed_pieces = split_three(plain * gain_two[...])
-    grad_router = jnp.zeros((32, 1024), F32)
-    for first, second in ((0, 0), (0, 1), (1, 0), (1, 1), (0, 2), (2, 0)):
-        grad_router = grad_router + jnp.dot(
-            logit_pieces[first], normed_pieces[second], preferred_element_type=F32
-        )
     grad_two = grad_two * gain_two[...]
     grad_total = cotangent[...].astype(F32) + scale * (
         grad_two - plain * jnp.mean(grad_two * plain, axis=1, keepdims=True)
     )
     grad_residual[...] = grad_total
     grad_all[tp] = grad_total.astype(BF16)
-    greet(brief_partners() + (ahead, behind, across))
-
+    clock.spend(4.0)
+
+    bounds = document_bounds(segments[...], live_mask[...])
     keys_sum[...] = jnp.zeros_like(keys_sum)
     values_sum[...] = jnp.zeros_like(values_sum)
     output_sum[...] = jnp.zeros_like(output_sum)
@@ -836,14 +885,14 @@
         grad_mixed = lax.dot_general(
             grad, output_weight[...], CONTRACT_LAST, preferred_element_type=F32
         ).astype(BF16)
-        key_position = lax.broadcasted_iota(jnp.int32, (1024, 256), 0)
-        position = place * 256 + lax.broadcasted_iota(jnp.int32, (1024, 256), 1)
-        allowed = (seg_column[...] == seg_row[:, rows]) & (
-            (live_column[...] == 1) | (position == key_position)
-        )
-        bias = jnp.where(allowed, 0.0, -1e30).astype(F32)
-        grad_query = attend_back_block(
-            query[rows, :], grad_mixed, keys[...], values[...], bias, keys_sum, values_sum
+        bias = score_bias(
+            bounds,
+            place * 256 + lax.broadcasted_iota(jnp.int32, (1, 256), 1),
+            lax.broadcasted_iota(jnp.int32, (1024, 1), 0),
+        )
+        clock.spend(0.8)
+        grad_query = yield from attend_back_block(
+            query[rows, :], grad_mixed, keys[...], values[...], bias, keys_sum, values_sum, clock
         )
         for lanes in (slice(0, 128), slice(128, 256)):
             grad_raw, grad_gain = head_back(
@@ -855,20 +904,7 @@
             )
             low[rows, lanes] = grad_raw.astype(BF16)
             query_gain_sum[...] += grad_gain
-
-    out_steps = plane_scatter_steps(post, out_parts, combined, out_scratch)
-    line_steps = line_gather_steps(post, grad_all.at[tp], grad_all, attention)
-    for _ in line_steps:
-        next(out_steps, None)
-    grad_raw, grad_key_gain = head_back(
-        (keys_sum[0] + exchange(keys_sum[1])) * 0.125,
-        raw[:, 256:],
-        key_gain[...],
-        cosine[...],
-        sine[...],
-    )
-    low[:, 256:384] = grad_raw.astype(BF16)
-    low[:, 384:] = (values_sum[0] + exchange(values_sum[1])).astype(BF16)
+        yield clock.spend(0.5)
 
     def make(offset):
         rows = block_rows(wrap(tp + offset))
@@ -886,6 +922,7 @@
         )
         part = parts.at[(2, 1, -1, 0).index(offset)]
         part[...] = total.astype(BF16)
+        yield clock.spend(0.8)
         return part
 
     def finish(own, first, second):
@@ -899,7 +936,17 @@
             + scale * (grad_one - plain * jnp.mean(grad_one * plain, axis=1, keepdims=True))
         ).astype(BF16)
 
-    def fill_small():
+    def router_gradient():
+        normed_pieces = split_three(plain * gain_two[...])
+        total = jnp.zeros((32, 1024), F32)
+        for first, second in ((0, 0), (0, 1), (1, 0), (1, 1), (0, 2), (2, 0)):
+            total = total + jnp.dot(
+                logit_pieces[first], normed_pieces[second], preferred_element_type=F32
+            )
+        return total
+
+    def fill_small(grad_key_gain):
+        grad_router = router_gradient()
         grad_gain_one = gain_one_sum[...] / gain_one[...]
         small[...] = jnp.zeros_like(small)
         for part in range(8):
@@ -911,7 +958,29 @@
         small[17, 0:1, :] = query_gain_sum[...]
         small[17, 1:2, :] = grad_key_gain
 
-    def dense_steps():
+    def attention_steps():
+        yield from line_gather_steps(
+            post, grad_all.at[tp], grad_all, clock, 11.5, 17.5, attention
+        )
+        grad_raw, grad_key_gain = head_back(
+            (keys_sum[0] + exchange(keys_sum[1])) * 0.125,
+            raw[:, 256:],
+            key_gain[...],
+            cosine[...],
+            sine[...],
+        )
+        low[:, 256:384] = grad_raw.astype(BF16)
+        low[:, 384:] = (values_sum[0] + exchange(values_sum[1])).astype(BF16)
+        yield clock.spend(2.0)
+        line_steps = line_scatter_steps(post, make, far, near, finish, clock, 3.5, 11.5)
+        last = yield from until_count(line_steps, 6)
+        fill_small(grad_key_gain)
+        now = clock.now
+        yield from side_by_side(
+            (last, line_steps), (now, dense_steps(now)), (now, small_steps(now))
+        )
+
+    def dense_steps(begin):
         weights = lax.dot_general(
             normed[...], low[...], CONTRACT_ROWS, preferred_element_type=F32
         ).astype(BF16)
@@ -921,29 +990,25 @@
             block = output_sum[:, part * 256 : (part + 1) * 256].astype(BF16)
             for piece in range(8):
                 dense[part * 8 + piece, :, 512:] = block[piece * 32 : (piece + 1) * 32]
-        yield from brief_scatter_steps(post, dense, dense_own, dense_scratch)
+        yield from brief_scatter_steps(post, dense, dense_own, dense_scratch, begin + 3.0)
         dense_all[me] = dense_own[...]
-        yield from brief_gather_steps(post, dense_own, dense_all)
-
-    def small_steps():
-        fill_small()
-        yield from brief_scatter_steps(post, small, small_own, small_scratch)
+        yield from brief_gather_steps(post, dense_own, dense_all, begin + 16.0)
+
+    def small_steps(begin):
+        yield from brief_scatter_steps(post, small, small_own, small_scratch, begin)
         line = [
             post.go(small_own, small_line.at[0], ahead),
             post.go(small_own, small_line.at[1], behind),
             post.go(small_own, small_line.at[2], across),
         ]
-        yield
+        yield begin + 12.0
         for copy in line:
             copy.wait_recv()
         small_sum[...] = small_own[...] + small_line[0] + small_line[1] + small_line[2]
         small_all[me] = small_sum[...]
-        yield from brief_gather_steps(post, small_sum, small_all)
-
-    line_steps = line_scatter_steps(post, make, far, near, finish)
-    for _ in range(4):
-        next(line_steps)
-    together(dense_steps(), small_steps(), line_steps, out_steps)
+        yield from brief_gather_steps(post, small_sum, small_all, begin + 14.0)
+
+    together(attention_steps(), resumed(out_due, out_steps))
     post.finish()
 
 
@@ -983,7 +1048,7 @@
         + brief_scatter_scratch(SMALL_ROWS, 128, F32)
         + [pltpu.SemaphoreType.DMA((count,)), pltpu.SemaphoreType.DMA((count,))],
         compiler_params=pltpu.CompilerParams(
-            collective_id=number, has_side_effects=True, vmem_limit_bytes=58 << 20
+            collective_id=number, has_side_effects=True, vmem_limit_bytes=63 << 20
         ),
         name="closing",
     )(*arguments)
@@ -1026,152 +1091,412 @@
     )(dense, weights, residual, combined)
 
 
+STEPS = ((0, 1), (3, 4), (6, 7), (12, 13), (14, 15), (10, 11), (8, 9), (2, 5))
 GROUP = 4
 
 
 def experts_kernel(
-    number_ref, rows_ref, grads_ref, pair_ref, down_ref,
-    out_ref, back_ref, weight_grads_ref,
-    gate_full, up_full, gate_sum, up_sum, down_sum, rows_own, grads_own, gates_own, select,
+    block, grads, gate_all, up, down,
+    rows_all, out_parts, back_sum, weight_sum,
+    rows_in, grads_in, both_full, down_full, both_sum, down_sum, rows_own, grads_own, gates_own,
+    select, weighted, grad_rows, grad_gates, mine, other, stage, out_stage,
+    b_far, b_near, a_far, a_near, line, line_far, line_near, send_sems, recv_sems, credit, load_sems, store_sems, weight_sems, own_sem,
 ):
-    step = pl.program_id(0)
-    expert = number_ref[0]
-    lane_row = lax.rem(expert, 16)
-    upper = expert >= 16
-
-    @pl.when(step == 0)
-    def _():
-        for part in range(4):
-            columns = slice(part * 128, (part + 1) * 128)
-            gate_full[:, columns] = pair_ref[part, :1024, :]
-            up_full[:, columns] = pair_ref[part, 1024:, :]
-        gate_sum[...] = jnp.zeros_like(gate_sum)
-        up_sum[...] = jnp.zeros_like(up_sum)
-        down_sum[...] = jnp.zeros_like(down_sum)
-
-    earlier = (
-        lax.broadcasted_iota(jnp.int32, (256, 256), 0)
-        <= lax.broadcasted_iota(jnp.int32, (256, 256), 1)
-    ).astype(BF16)
-    slot = lax.broadcasted_iota(jnp.int32, (SLOTS, 256), 0).astype(F32)
+    a, b, core = plane_place()
+    me = lax.axis_index("ep")
+    ahead_a, behind_a, ahead_b, behind_b, sibling = plane_partners()
+    here = [plane_index(a + place[0], b + place[1], core) for place in ARRIVAL]
+    there = [plane_index(b + place[0], a + place[1], 1 - core) for place in ARRIVAL]
+    lane_row = lax.rem(me, 16)
+    upper = me >= 16
+    tp = lax.axis_index("tp")
+    ahead, behind = line_partners()
+    greet(plane_partners() + (ahead, behind))
+    post = Post(send_sems, recv_sems)
+    go = post.go
+    events, held = plane_gather_events(post, block, rows_all)
+    events[0][1]()
+    own_copy = pltpu.make_async_copy(block, stage.at[0], own_sem)
+    own_copy.start()
+    before_me, after_me = wrap(tp - 1), wrap(tp + 1)
+
+    def up_part(place, rows=slice(None)):
+        return at(both_full, rows, pl.ds(pl.multiple_of(512 + place * 128, 128), 128))
+
+    def down_part(place, first=0, count=128):
+        return at(down_full, pl.ds(pl.multiple_of(place * 128 + first, 64), count))
+
+    up_near = (
+        post.go(up, up_part(tp), ahead), post.go(up, up_part(tp), behind)
+    )
+    down_near = (
+        post.go(down, down_part(tp), ahead), post.go(down, down_part(tp), behind)
+    )
+    up_top, up_bottom = up_part(before_me, pl.ds(0, 512)), up_part(after_me, pl.ds(512, 512))
+    up_far = (
+        post.prepare(up_top, up_top, ahead), post.prepare(up_bottom, up_bottom, behind)
+    )
+    down_top, down_bottom = down_part(before_me, 0, 64), down_part(after_me, 64, 64)
+    down_far = (
+        post.prepare(down_top, down_top, ahead), post.prepare(down_bottom, down_bottom, behind)
+    )
+
+    def relay(near, far):
+        for one, other_one in zip(near, far, strict=True):
+            one.wait_recv()
+            other_one.start()
+
+    weight_loads = [
+        pltpu.make_async_copy(
+            gate_all.at[part], both_full.at[:, part * 128 : (part + 1) * 128], weight_sems.at[part]
+        )
+        for part in range(4)
+    ]
+    weight_loads.append(pltpu.make_async_copy(up, up_part(tp)(), weight_sems.at[4]))
+    weight_loads.append(pltpu.make_async_copy(down, down_part(tp)(), weight_sems.at[5]))
+    for copy in weight_loads:
+        copy.start()
+    both_sum[...] = jnp.zeros_like(both_sum)
+    down_sum[...] = jnp.zeros_like(down_sum)
+
+    def blocks(step):
+        first, second = STEPS[step]
+        return (here[first], here[second], there[first], there[second])
+
+    loads, crossing, stores = {}, {}, {}
+    for step in range(len(STEPS)):
+        slot = step % 2
+        loads[step], stores[step] = [], []
+        crossing[step] = [
+            post.prepare(at(stage, part), at(other, slot, part), sibling) for part in range(2)
+        ]
+        for part, index in enumerate(blocks(step)):
+            loads[step] += [
+                Local(
+                    at(rows_all, index), at(rows_in, slot, part), at(load_sems, slot, 0, part)
+                ),
+                Local(at(grads, index), at(grads_in, slot, part), at(load_sems, slot, 1, part)),
+            ]
+            stores[step].append(
+                Local(at(out_stage, part), at(out_parts, index), at(store_sems, part))
+            )
+
+    def load(step):
+        for place in STEPS[step]:
+            held[place].wait_recv()
+        for copy in loads[step]:
+            copy.start()
+
+    def take(step):
+        for part, place in enumerate(STEPS[step]):
+            crossing[step][part].wait_recv()
+            add_rows(
+                mine.at[place], [(mine.at[place], 0), (other.at[step % 2, part], 0)], 0, rows
+            )
+        if step + 2 < len(STEPS):
+            pl.semaphore_signal(credit, inc=1, device_id=sibling, device_id_type=MESH)
+
+    rows = a_far.shape[0]
+    top, bottom = halves(a_far)
+    high = top.size
+    low = rows - high
+    far_b, near_b = {}, {}
+
+    def number_of(k, j):
+        return ARRIVAL.index((OFFSETS[k], OFFSETS[j]))
+
+    def slot_of(k, j):
+        return mine.at[number_of(k, j)]
+
+    def far_step(k):
+        part = number_of(k, 0)
+        far_b[k] = (
+            go(at(mine, part, top), at(b_far, k, top), ahead_b),
+            go(at(mine, part, bottom), at(b_far, k, bottom), behind_b),
+        )
+
+    def near_step(k):
+        far = b_far.at[k]
+        far_b[k][0].wait_recv()
+        part = slot_of(k, 1)
+        add_rows(part, [(part, 0), (far, 0)], 0, high)
+        first = go(at(mine, number_of(k, 1)), at(b_near, 0, k), ahead_b)
+        far_b[k][1].wait_recv()
+        part = slot_of(k, 2)
+        add_rows(part, [(part, high), (far, high)], high, low)
+        near_b[k] = (first, go(at(mine, number_of(k, 2)), at(b_near, 1, k), behind_b))
+
+    def before(step):
+        for copy in loads[step]:
+            copy.wait()
+
+    def between(step):
+        if step > 0:
+            for copy in crossing[step - 1]:
+                copy.wait_send()
+            for copy in stores[step - 1]:
+                copy.wait()
+        onward({0: (4,), 1: (6,), 2: (7, 8, 9), 3: (10, 11)}.get(step, ()))
+        if step + 1 < len(STEPS):
+            load(step + 1)
+        if step > 0:
+            take(step - 1)
+        if step == 4:
+            far_step(2)
+            far_step(3)
+        if step == 5:
+            far_step(0)
+            far_step(1)
+            near_step(3)
+            near_step(2)
+        if step == 6:
+            near_step(0)
+        if step == 7:
+            near_step(1)
+
+    def onward(numbers):
+        for number in numbers:
+            events[number][1]()
+
+    def early(step):
+        if step == 0:
+            for copy in down_far:
+                copy.wait_recv()
+
+    def after(step):
+        onward({0: (5,)}.get(step, ()))
+        if step >= 2:
+            pl.semaphore_wait(credit, 1)
+        for copy in crossing[step] + stores[step]:
+            copy.start()
+
+    def at_step(step, task):
+        for number in range(len(STEPS)):
+
+            @pl.when(step == number)
+            def _(number=number):
+                task(number)
+
+    def from_table(step, table):
+        value = step * 0 + table[0]
+        for number in range(1, len(table)):
+            value = jnp.where(step == number, table[number], value)
+        return value
+
+    own_copy.wait()
+    own_copy = pltpu.make_async_copy(stage.at[0], rows_all.at[me], own_sem)
+    own_copy.start()
+    onward((1, 2))
+    own_copy.wait()
+    load(0)
+    relay(up_near, up_far)
+    onward((3,))
+    relay(down_near, down_far)
+    for copy in weight_loads:
+        copy.wait()
+    for copy in up_far:
+        copy.wait_recv()
     extra_row = lax.broadcasted_iota(jnp.int32, (EXTRA, 1024), 0) == lane_row
-    for part in range(GROUP):
-        extras = jnp.where(extra_row, rows_ref[part, 256:, :].astype(F32), 0.0)
-        extras = jnp.sum(extras, axis=0, keepdims=True)
-        gates = jnp.where(
-            upper, extras[:, 512:768] + extras[:, 768:], extras[:, :256] + extras[:, 256:512]
-        )
-        named = jnp.broadcast_to(gates, (16, 256)) > 0.0
-        rank = jnp.dot(named.astype(BF16), earlier, preferred_element_type=F32)[:1] - 1.0
-        chosen = (slot == rank) & (gates > 0.0)
-        chosen_low = chosen.astype(BF16)
-        at = slice(part * SLOTS, (part + 1) * SLOTS)
-        select[at, :] = chosen_low
-        rows_own[at, :] = jnp.dot(
-            chosen_low, rows_ref[part, :256, :], preferred_element_type=F32
+
+    def one_step(step, carry):
+        slot = lax.rem(step, 2)
+        at_step(step, before)
+        earlier = (
+            lax.broadcasted_iota(jnp.int32, (256, 256), 0)
+            <= lax.broadcasted_iota(jnp.int32, (256, 256), 1)
         ).astype(BF16)
-        grads_own[at, :] = jnp.dot(
-            chosen_low, grads_ref[part], preferred_element_type=F32
+        place = lax.broadcasted_iota(jnp.int32, (SLOTS, 256), 0).astype(F32)
+        for part in range(GROUP):
+            extras = jnp.where(extra_row, rows_in[slot, part, 256:, :].astype(F32), 0.0)
+            extras = jnp.sum(extras, axis=0, keepdims=True)
+            gates = jnp.where(
+                upper, extras[:, 512:768] + extras[:, 768:], extras[:, :256] + extras[:, 256:512]
+            )
+            named = jnp.broadcast_to(gates, (16, 256)) > 0.0
+            rank = jnp.dot(named.astype(BF16), earlier, preferred_element_type=F32)[:1] - 1.0
+            chosen = (place == rank) & (gates > 0.0)
+            chosen_low = chosen.astype(BF16)
+            at = slice(part * SLOTS, (part + 1) * SLOTS)
+            select[at, :] = chosen_low
+            rows_own[at, :] = jnp.dot(
+                chosen_low, rows_in[slot, part, :256, :], preferred_element_type=F32
+            ).astype(BF16)
+            grads_own[at, :] = jnp.dot(
+                chosen_low, grads_in[slot, part], preferred_element_type=F32
+            ).astype(BF16)
+            gates_own[at, :] = jnp.sum(jnp.where(chosen, gates, 0.0), axis=1, keepdims=True)
+
+        at_step(step, early)
+        both_pre = jnp.dot(rows_own[...], both_full[...], preferred_element_type=F32)
+        gate_pre, up_pre = both_pre[:, :512], both_pre[:, 512:]
+        sigmoid = 1.0 / (1.0 + jnp.exp(-gate_pre))
+        silu = gate_pre * sigmoid
+        act = (silu * up_pre).astype(BF16)
+        out = jnp.dot(act, down_full[...], preferred_element_type=F32).astype(BF16).astype(F32)
+        gate_factor = gates_own[...]
+        grads_float = grads_own[...].astype(F32)
+        grad_gates[...] = jnp.sum(grads_float * out, axis=1, keepdims=True)
+        weighted[...] = (gate_factor * out).astype(BF16)
+        grad_out = (gate_factor * grads_float).astype(BF16)
+        grad_act = lax.dot_general(
+            grad_out, down_full[...], CONTRACT_LAST, preferred_element_type=F32
+        )
+        down_sum[...] += lax.dot_general(
+            grad_out, act, CONTRACT_ROWS, preferred_element_type=F32
+        )
+        grad_gate_pre = grad_act * up_pre * sigmoid * (1.0 + gate_pre * (1.0 - sigmoid))
+        grad_up_pre = grad_act * silu
+        grad_pre = jnp.concatenate(
+            [grad_gate_pre.astype(BF16), grad_up_pre.astype(BF16)], axis=1
+        )
+        both_sum[...] += lax.dot_general(
+            rows_own[...], grad_pre, CONTRACT_ROWS, preferred_element_type=F32
+        )
+        grad_rows[...] = lax.dot_general(
+            grad_pre, both_full[...], CONTRACT_LAST, preferred_element_type=F32
         ).astype(BF16)
-        gates_own[at, :] = jnp.sum(jnp.where(chosen, gates, 0.0), axis=1, keepdims=True)
-
-    rows_in = rows_own[...]
-    gate_pre = jnp.dot(rows_in, gate_full[...], preferred_element_type=F32)
-    up_pre = jnp.dot(rows_in, up_full[...], preferred_element_type=F32)
-    sigmoid = 1.0 / (1.0 + jnp.exp(-gate_pre))
-    silu = gate_pre * sigmoid
-    act = (silu * up_pre).astype(BF16)
-    out = jnp.dot(act, down_ref[...], preferred_element_type=F32).astype(BF16).astype(F32)
-    gate_factor = gates_own[...]
-    grads_in = grads_own[...].astype(F32)
-    grad_gates = jnp.sum(grads_in * out, axis=1, keepdims=True)
-    weighted = (gate_factor * out).astype(BF16)
-    grad_out = (gate_factor * grads_in).astype(BF16)
-    grad_act = lax.dot_general(
-        grad_out, down_ref[...], CONTRACT_LAST, preferred_element_type=F32
+        at_step(step, between)
+        nothing = jnp.zeros((1, 512), F32)
+        slots = [from_table(step, [pair[part] for pair in STEPS]) for part in range(2)]
+        for part in range(GROUP):
+            at = slice(part * SLOTS, (part + 1) * SLOTS)
+            chosen_low = select[at, :]
+            out_stage[part] = lax.dot_general(
+                chosen_low, weighted[at], CONTRACT_ROWS, preferred_element_type=F32
+            ).astype(BF16)
+            target = mine.at[slots[part]] if part < 2 else stage.at[part - 2]
+            target[:256, :] = lax.dot_general(
+                chosen_low, grad_rows[at], CONTRACT_ROWS, preferred_element_type=F32
+            ).astype(BF16)
+            spread = jnp.sum(chosen_low.astype(F32) * grad_gates[at], axis=0, keepdims=True)
+            upper_bits = spread.astype(BF16).astype(F32)
+            both = jnp.concatenate([upper_bits, spread - upper_bits], axis=1)
+            line_now = jnp.concatenate(
+                [jnp.where(upper, nothing, both), jnp.where(upper, both, nothing)], axis=1
+            )
+            target[256:, :] = jnp.where(extra_row, line_now, 0.0).astype(BF16)
+        at_step(step, after)
+        return carry
+
+    lax.fori_loop(0, len(STEPS), one_step, 0)
+    last = len(STEPS) - 1
+
+    def make_weights(offset):
+        place = wrap(tp + offset)
+        lanes = pl.ds(pl.multiple_of(place * 128, 128), 128)
+        upper_lanes = pl.ds(pl.multiple_of(512 + place * 128, 128), 128)
+        part = line.at[OFFSETS.index(offset)]
+        part[:1024, :] = both_sum[:, lanes].astype(BF16)
+        part[1024:2048, :] = both_sum[:, upper_lanes].astype(BF16)
+        part[2048:, :] = down_sum[:, lanes].astype(BF16)
+        yield 1.0
+        return part
+
+    def finish_weights(own, first, second):
+        add_rows(weight_sum, [(own, 0), (first, 0), (second, 0)], 0, own.shape[0])
+
+    def back_steps():
+        yield 0.0
+        take(last)
+        far_a, near_a = [], []
+        for k in range(4):
+            yield (2.0, 4.0, 8.0, 12.0)[k]
+            part = slot_of(k, 3)
+            near_b[k][0].wait_recv()
+            near_b[k][1].wait_recv()
+            base = [part, b_near.at[0, k], b_near.at[1, k]]
+            first_rows = [(ref, 0) for ref in base]
+            last_rows = [(ref, high) for ref in base]
+            if k == 0:
+                add_rows(part, first_rows, 0, high)
+                add_rows(part, last_rows, high, low)
+                far_a = [
+                    go(part.at[top], a_far.at[top], ahead_a),
+                    go(part.at[bottom], a_far.at[bottom], behind_a),
+                ]
+            elif k == 1:
+                far_a[0].wait_recv()
+                add_rows(part, first_rows + [(a_far, 0)], 0, high)
+                add_rows(part, last_rows, high, low)
+                near_a.append(go(part, a_near.at[0], ahead_a))
+            elif k == 2:
+                far_a[1].wait_recv()
+                add_rows(part, first_rows, 0, high)
+                add_rows(part, last_rows + [(a_far, high)], high, low)
+                near_a.append(go(part, a_near.at[1], behind_a))
+            else:
+                near_a[0].wait_recv()
+                near_a[1].wait_recv()
+                add_rows(
+                    back_sum, first_rows + [(a_near.at[0], 0), (a_near.at[1], 0)], 0, rows
+                )
+
+    together(
+        line_scatter_steps(post, make_weights, line_far, line_near, finish_weights, Clock(), 7.0, 24.0),
+        back_steps(),
     )
-    down_sum[...] += lax.dot_general(
-        grad_out, act, CONTRACT_ROWS, preferred_element_type=F32
-    )
-    grad_gate_pre = (grad_act * up_pre * sigmoid * (1.0 + gate_pre * (1.0 - sigmoid))).astype(BF16)
-    grad_up_pre = (grad_act * silu).astype(BF16)
-    gate_sum[...] += lax.dot_general(
-        rows_in, grad_gate_pre, CONTRACT_ROWS, preferred_element_type=F32
-    )
-    up_sum[...] += lax.dot_general(
-        rows_in, grad_up_pre, CONTRACT_ROWS, preferred_element_type=F32
-    )
-    grad_rows = lax.dot_general(
-        grad_gate_pre, gate_full[...], CONTRACT_LAST, preferred_element_type=F32
-    )
-    grad_rows = grad_rows + lax.dot_general(
-        grad_up_pre, up_full[...], CONTRACT_LAST, preferred_element_type=F32
-    )
-    grad_rows = grad_rows.astype(BF16)
-    nothing = jnp.zeros((1, 512), F32)
-    for part in range(GROUP):
-        at = slice(part * SLOTS, (part + 1) * SLOTS)
-        chosen_low = select[at, :]
-        out_ref[part] = lax.dot_general(
-            chosen_low, weighted[at], CONTRACT_ROWS, preferred_element_type=F32
-        ).astype(BF16)
-        back_ref[part, :256, :] = lax.dot_general(
-            chosen_low, grad_rows[at], CONTRACT_ROWS, preferred_element_type=F32
-        ).astype(BF16)
-        spread = jnp.sum(chosen_low.astype(F32) * grad_gates[at], axis=0, keepdims=True)
-        high = spread.astype(BF16).astype(F32)
-        both = jnp.concatenate([high, spread - high], axis=1)
-        line = jnp.concatenate(
-            [jnp.where(upper, nothing, both), jnp.where(upper, both, nothing)], axis=1
-        )
-        back_ref[part, 256:, :] = jnp.where(extra_row, line, 0.0).astype(BF16)
-
-    @pl.when(step == pl.num_programs(0) - 1)
-    def _():
-        for part in range(4):
-            columns = slice(part * 128, (part + 1) * 128)
-            weight_grads_ref[part, :1024, :] = gate_sum[:, columns].astype(BF16)
-            weight_grads_ref[part, 1024:2048, :] = up_sum[:, columns].astype(BF16)
-            weight_grads_ref[part, 2048:, :] = down_sum[:, columns].astype(BF16)
-
-
-def run_experts(number, rows, grads, pair, down):
-    sources = rows.shape[0]
+    for copy in stores[last]:
+        copy.wait()
+    waited = [copy for step in range(last) for copy in crossing[step]]
+    for copy in post.started:
+        if not any(copy is other_copy for other_copy in waited):
+            copy.wait_send()
+
+
+def run_experts(block, grads, gate_all, up, down, number):
+    rows, columns = block.shape
+    sources = grads.shape[0]
     count = GROUP * SLOTS
+    copies = PLANE_COPIES + 16 + 8 + 8 + 4 + 3 * LINE_COPIES
+    whole = (rows, columns)
     return pl.pallas_call(
         experts_kernel,
         out_shape=[
-            jax.ShapeDtypeStruct((sources, 256, 1024), BF16),
-            jax.ShapeDtypeStruct((sources, 256 + EXTRA, 1024), BF16),
-            jax.ShapeDtypeStruct((4, 3072, 128), BF16),
+            jax.ShapeDtypeStruct((sources,) + whole, BF16),
+            jax.ShapeDtypeStruct((sources, 256, columns), BF16),
+            jax.ShapeDtypeStruct(whole, F32),
+            jax.ShapeDtypeStruct((3072, 128), F32),
         ],
-        grid=(sources // GROUP,),
-        in_specs=[
-            pl.BlockSpec(memory_space=pltpu.SMEM),
-            pl.BlockSpec((GROUP, 256 + EXTRA, 1024), lambda i: (i, 0, 0)),
-            pl.BlockSpec((GROUP, 256, 1024), lambda i: (i, 0, 0)),
-            pl.BlockSpec((4, 2048, 128), lambda i: (0, 0, 0)),
-            pl.BlockSpec((512, 1024), lambda i: (0, 0)),
-        ],
-        out_specs=[
-            pl.BlockSpec((GROUP, 256, 1024), lambda i: (i, 0, 0)),
-            pl.BlockSpec((GROUP, 256 + EXTRA, 1024), lambda i: (i, 0, 0)),
-            pl.BlockSpec((4, 3072, 128), lambda i: (0, 0, 0)),
-        ],
+        in_specs=[ANY] * 5,
+        out_specs=[ANY, ANY, VMEM, VMEM],
         scratch_shapes=[
-            pltpu.VMEM((1024, 512), BF16),
-            pltpu.VMEM((1024, 512), BF16),
-            pltpu.VMEM((1024, 512), F32),
-            pltpu.VMEM((1024, 512), F32),
+            pltpu.VMEM((2, GROUP) + whole, BF16),
+            pltpu.VMEM((2, GROUP, 256, columns), BF16),
+            pltpu.VMEM((1024, 1024), BF16),
+            pltpu.VMEM((512, 1024), BF16),
+            pltpu.VMEM((1024, 1024), F32),
             pltpu.VMEM((1024, 512), F32),
             pltpu.VMEM((count, 1024), BF16),
             pltpu.VMEM((count, 1024), BF16),
             pltpu.VMEM((count, 1), F32),
             pltpu.VMEM((count, 256), BF16),
+            pltpu.VMEM((count, 1024), BF16),
+            pltpu.VMEM((count, 1024), BF16),
+            pltpu.VMEM((count, 1), F32),
+            pltpu.VMEM((16,) + whole, BF16),
+            pltpu.VMEM((2, 2) + whole, BF16),
+            pltpu.VMEM((2,) + whole, BF16),
+            pltpu.VMEM((GROUP, 256, columns), BF16),
+            pltpu.VMEM((4,) + whole, BF16),
+            pltpu.VMEM((2, 4) + whole, BF16),
+            pltpu.VMEM(whole, BF16),
+            pltpu.VMEM((2,) + whole, BF16),
+            pltpu.VMEM((4, 3072, 128), BF16),
+            pltpu.VMEM((3072, 128), BF16),
+            pltpu.VMEM((2, 3072, 128), BF16),
+            pltpu.SemaphoreType.DMA((copies,)),
+            pltpu.SemaphoreType.DMA((copies,)),
+            pltpu.SemaphoreType.REGULAR,
+            pltpu.SemaphoreType.DMA((2, 2, GROUP)),
+            pltpu.SemaphoreType.DMA((GROUP,)),
+            pltpu.SemaphoreType.DMA((12,)),
+            pltpu.SemaphoreType.DMA,
         ],
-        compiler_params=pltpu.CompilerParams(vmem_limit_bytes=60 << 20),
+        compiler_params=pltpu.CompilerParams(
+            collective_id=number, has_side_effects=True, vmem_limit_bytes=63 << 20
+        ),
         name="run_experts",
-    )(number, rows, grads, pair, down)
+    )(block, grads, gate_all, up, down)
 
 
 def rotary_constants():
@@ -1207,30 +1532,27 @@
     query_scale = jnp.tile(query_gain.astype(F32), 2).reshape(1, -1)
     key_scale = jnp.tile(key_gain.astype(F32), 2).reshape(1, -1)
     cosine, sine = rotary_constants()
-    seg_column, seg_row = segments.reshape(-1, 1), segments.reshape(1, -1)
-    live_column, live_row = live_mask.reshape(-1, 1), live_mask.reshape(1, -1)
+    seg_row, live_row = segments.reshape(1, -1), live_mask.reshape(1, -1)
     router = router_weight.T
-    normed, raw, query, keys, values, mixed, residual, block, gates, grad_all = opening(
+    (
+        normed, raw, query, keys, values, mixed, residual, block, gates, grad_all, gate_all,
+    ) = opening(
         (
             inputs, gain_one, query_weight, key_weight, value_weight, query_scale, key_scale,
-            cosine, sine, seg_column, seg_row, live_row, output_weight, gain_two, router, routes.T,
-            cotangent,
+            cosine, sine, seg_row, live_row, output_weight, gain_two, router, routes.T,
+            cotangent, gate_weight[0],
         ),
         1,
     )
-    pair = jnp.concatenate([gate_weight[0], up_weight[0]], axis=0)
-    rows_all, pair_all, down_all = dispatch(block, pair, down_weight[0], 2)
-    number = lax.axis_index("ep").astype(jnp.int32).reshape(1)
-    out_parts, back_parts, weight_parts = run_experts(
-        number, rows_all, grad_all, pair_all, down_all.reshape(512, 1024)
+    rows_all, out_parts, back, weight_sums = run_experts(
+        block, grad_all, gate_all, up_weight[0], down_weight[0], 2
     )
-    back, weight_sums = collect(back_parts, weight_parts, 3)
     grad_inputs, dense, small, combined = closing(
         (
             back, residual, gates, cotangent, gain_two, router, query, keys, values, mixed,
             output_weight, query_weight, key_weight, value_weight, raw, normed.reshape(1024, 1024),
-            inputs, gain_one, query_scale, key_scale, cosine, sine, seg_column, seg_row,
-            live_column, out_parts,
+            inputs, gain_one, query_scale, key_scale, cosine, sine, seg_row,
+            live_row, out_parts,
         ),
         4,
     )

time: 369 us -> 338 us (0.916)
  Pallas kernels: 348 us -> 319 us
    pallas_call x3 -> x1, Pallas kernels: 174 us -> 147 us  [run_experts(): pl.pallas_call(experts_kernel, out_shape=[jax.ShapeDtypeStruct((sources,)...]
    pallas_call x1, Pallas kernels: 109 us -> 97.5 us  [closing(): pl.pallas_call(closing_kernel, out_shape=[jax.ShapeDtypeStruct((256, 1024...]
    pallas_call x1, Pallas kernels: 62.4 us -> 71.8 us  [opening(): pl.pallas_call(opening_kernel, out_shape=[jax.ShapeDtypeStruct((4, 256, 1...]
where the time goes in v3:
time: 338 us; the launch traced here: 332 us
  Pallas kernels  319 us (94%)
  local copies, waits for them, and re-layouts  9.83 us (3%)
    pallas_call x1, Pallas kernels, run_experts(): pl.pallas_call(experts_kernel, out_shape=[jax.ShapeDtypeStruct((sources,)...  147 us
    pallas_call x1, Pallas kernels, closing(): pl.pallas_call(closing_kernel, out_shape=[jax.ShapeDtypeStruct((256, 1024...  97.5 us
    pallas_call x1, Pallas kernels, opening(): pl.pallas_call(opening_kernel, out_shape=[jax.ShapeDtypeStruct((4, 256, 1...  71.8 us

profile of v3, /device:TPU:1, one launch (start us, length us, event | category | flops | bytes accessed | tf_op | source)
XLA Modules:
  0.0 332.4 jit_solution(11013090028214201685)
XLA Ops:
  0.6 0.7 tile.4
  1.3 0.6 reshape_tile.6.query_gain
  1.9 0.7 tile.5
  2.6 0.6 reshape_tile.7.key_gain
  3.1 1.3 reshape.74
  4.4 1.3 reshape.76
  5.7 71.8 %opening.1 = (bf16[4,256,1024]{2,1,0:T(8,128)(2,1)}, f32[1024,384]{1,0:T(8,128)}, bf16[1024,256]{1,0:T(8,128)(2,1)}, bf16[1024,128]{1,0:T(8,128)(2,1)}, bf16[102...) custom-call(bf16[256,1024]{1,0:T(8,128)(2,1)} %inputs.3, ...), custom_call_target="tpu_custom_call" | custom-call | tf_op jit(solution)/shard_map/opening/pallas_call | solution.py:756
  77.5 146.7 %run_experts.1 = (bf16[32,272,1024]{2,1,0:T(8,128)(2,1)}, bf16[32,256,1024]{2,1,0:T(8,128)(2,1)}, f32[272,1024]{1,0:T(8,128)}, f32[3072,128]{1,0:T(8,128)}) custom-call(bf16[272,1024]{1,0:T(8,128)(2,1)} %get-tuple-element.40.block, bf16[32,256,1024]{2,1,0:T(8,128)(2,1)} %get-tuple-element.41.grads, bf16[4,1024,128]{2,1,0:T(8,128)(2,1)} %get-tuple-element.42.gate_all, ...), custom_call_target="tpu_custom_call" | custom-call | tf_op jit(solution)/shard_map/run_experts/pallas_call | solution.py:1452
  224.2 97.5 %closing.1 = (bf16[256,1024]{1,0:T(8,128)(2,1)}, bf16[32,32,768]{2,1,0:T(8,128)(2,1)}, f32[32,16,128]{2,1,0:T(8,128)}, f32[256,1024]{1,0:T(8,128)}) custom-call(f32[272,1024]{1,0:T(8,128)} %get-tuple-element.43.back, f32[256,1024]{1,0:T(8,128)} %get-tuple-element.44.residual, f32[32,256]{1,0:T(8,128)} %get-tuple-element.45.gates, ...), custom_call_target="tpu_custom_call" | custom-call | tf_op jit(solution)/shard_map/closing/pallas_call | solution.py:1017
  321.7 0.0 copy-start
  321.7 1.2 copy-done
  322.9 0.0 copy-start.1
  322.9 1.4 copy-done.1
  324.4 0.0 copy-start.2
  324.4 1.4 copy-done.2
  325.8 0.0 copy-start.3
  325.8 1.2 copy-done.3
  327.0 0.0 copy-start.5
  327.0 0.0 copy-start.4
  327.0 2.5 finish_all.1
  329.5 0.0 copy-done.5
  329.5 0.6 add_bitcast_fusion
  330.1 0.6 slice_bitcast_fusion
  330.7 0.7 copy.36
  331.4 0.0 copy-done.4
  331.4 0.8 copy.38
  (1 shorter events, 0.0 us)
Async XLA Ops:
  321.7 1.2 copy-start
  322.9 1.4 copy-start.1
  324.4 1.4 copy-start.2
  325.8 1.2 copy-start.3
  327.0 2.6 copy-start.5
  327.0 4.4 %copy-start.4 = (bf16[256,1024]{1,0:T(8,128)(2,1)S(1)}, bf16[256,1024]{1,0:T(8,128)(2,1)}, u32[]{:S(2)}) copy-start(bf16[256,1024]{1,0:T(8,128)(2,1)} %get-tuple-element.85) | copy-start | bytes 1572868

commit v4 on v3

--- a/solution.py
+++ b/solution.py
@@ -84,14 +84,6 @@
 def resumed(due, task):
     yield due
     yield from task
-
-
-def until_count(task, count):
-    for number in range(count):
-        due = next(task)
-        if number < count - 1:
-            yield due
-    return due
 
 
 def side_by_side(*tasks):
@@ -405,48 +397,50 @@
     return tuple(along_a + along_b + [sibling])
 
 
-BRIEF_COPIES = 16 + 12 + 3
+BRIEF_COPIES = 1 + 3 + 3
+
+
+def brief_number(number):
+    return (number // 16, number // 4 % 4, number % 4)
 
 
 def brief_scatter_steps(post, parts_ref, sum_ref, scratch, begin=0.0):
-    other, from_b, from_a = scratch
+    other, from_b, total, from_a = scratch
     a, b, core = plane_place()
     along_a, along_b, sibling = ring_places(a, b, core, lax.axis_index("tp"))
-    go = post.go
-    crossing, copies_b, copies_a = {}, {}, {}
-    for k in range(4):
-        for j in range(4):
-            there = plane_index(b + OFFSETS[k], a + OFFSETS[j], 1 - core)
-            crossing[k, j] = go(parts_ref.at[there], other.at[k, j], sibling)
+    crossing = post.go(at(parts_ref, 1 - core), other, sibling)
     yield begin + 3.0
-    for k in range(4):
-        for j in range(4):
-            here = plane_index(a + OFFSETS[k], b + OFFSETS[j], core)
-            crossing[k, j].wait_recv()
-            block = other.at[k, j]
-            block[...] = (block[...].astype(F32) + parts_ref[here].astype(F32)).astype(block.dtype)
-            if j < 3:
-                copies_b[k, j] = go(block, from_b.at[k, j], along_b[j])
-    yield begin + 6.5
-    for k in range(4):
-        total = other[k, 3].astype(F32)
+    crossing.wait_recv()
+    for i in range(4):
+        other[i] = (other[i].astype(F32) + parts_ref[core, i].astype(F32)).astype(other.dtype)
+    copies = [
+        post.go(at(other, slice(None), wrap(b + OFFSETS[j])), at(from_b, j), along_b[j])
+        for j in range(3)
+    ]
+    yield begin + 8.0
+    for copy in copies:
+        copy.wait_recv()
+    for i in range(4):
+        part = other[i, b].astype(F32)
         for j in range(3):
-            copies_b[k, j].wait_recv()
-            total = total + from_b[k, j].astype(F32)
-        if k < 3:
-            other[k, 3] = total.astype(other.dtype)
-            copies_a[k] = go(other.at[k, 3], from_a.at[k], along_a[k])
-    yield begin + 10.0
-    for k in range(3):
-        copies_a[k].wait_recv()
-        total = total + from_a[k].astype(F32)
-    sum_ref[...] = total.astype(sum_ref.dtype)
+            part = part + from_b[j, i].astype(F32)
+        total[i] = part.astype(total.dtype)
+    copies = [
+        post.go(at(total, wrap(a + OFFSETS[j])), at(from_a, j), along_a[j]) for j in range(3)
+    ]
+    yield begin + 11.0
+    part = total[a].astype(F32)
+    for j in range(3):
+        copies[j].wait_recv()
+        part = part + from_a[j].astype(F32)
+    sum_ref[...] = part.astype(sum_ref.dtype)
 
 
 def brief_scatter_scratch(rows, columns, kind):
     return [
         pltpu.VMEM((4, 4, rows, columns), kind),
-        pltpu.VMEM((4, 3, rows, columns), kind),
+        pltpu.VMEM((3, 4, rows, columns), kind),
+        pltpu.VMEM((4, rows, columns), kind),
         pltpu.VMEM((3, rows, columns), kind),
     ]
 
@@ -454,30 +448,19 @@
 def brief_gather_steps(post, own_ref, all_ref, begin=0.0):
     a, b, core = plane_place()
     along_a, along_b, sibling = ring_places(a, b, core, lax.axis_index("tp"))
-    go = post.go
-    me = plane_index(a, b, core)
-    copies_a = [go(own_ref, all_ref.at[me], place) for place in along_a]
-    copies_b, crossing = [], []
-
-    def onward(src, index):
-        copies_b.extend(go(src, all_ref.at[index], place) for place in along_b)
-        crossing.append(go(src, all_ref.at[index], sibling))
-
-    onward(own_ref, me)
+    all_ref[core, a, b] = own_ref[...]
+    copies = [post.go(own_ref, at(all_ref, core, a, b), place) for place in along_a]
     yield begin + 3.0
-    for k in range(3):
-        index = plane_index(a - OFFSETS[k], b, core)
-        copies_a[k].wait_recv()
-        onward(all_ref.at[index], index)
-    yield begin + 6.0
-    for k, offset in enumerate((0, 2, 1, -1)):
-        for j in range(3):
-            index = plane_index(a - offset, b - OFFSETS[j], core)
-            copies_b[3 * k + j].wait_recv()
-            crossing.append(go(all_ref.at[index], all_ref.at[index], sibling))
-    yield begin + 9.0
-    for copy in crossing:
+    for copy in copies:
         copy.wait_recv()
+    line = at(all_ref, core, slice(None), b)
+    copies = [post.go(line, line, place) for place in along_b]
+    yield begin + 8.0
+    for copy in copies:
+        copy.wait_recv()
+    crossing = post.go(at(all_ref, core), at(all_ref, core), sibling)
+    yield begin + 11.0
+    crossing.wait_recv()
 
 
 LINE_COPIES = 4
@@ -578,6 +561,16 @@
     return (scale * (grad - plain * head_mean(grad * plain)), grad_gain)
 
 
+def wide(gain):
+    gain = gain.astype(F32)
+    return jnp.concatenate([gain[part : part + 1] for part in range(8)], axis=1)
+
+
+def both_heads(gain):
+    gain = gain.astype(F32)
+    return jnp.concatenate([gain, gain], axis=1)
+
+
 def row_scale(values):
     return lax.rsqrt(jnp.mean(values * values, axis=1, keepdims=True) + 1e-05)
 
@@ -652,9 +645,10 @@
     inputs, gain_one, query_weight, key_weight, value_weight, query_gain, key_gain, cosine, sine,
     segments, live_mask, output_weight, gain_two, router, routes, cotangent,
     gate,
-    normed, raw, query, keys, values, mixed, residual, block, gates, grad_all,
-    gate_all,
-    parts, far, near, hold, send_sems, recv_sems, local_sems,
+    normed_out, raw_out, query_out, keys_out, values_out, mixed_out,
+    residual, block, gates, grad_all, gate_all,
+    normed, raw, query, keys, values, mixed,
+    parts, far, near, hold, send_sems, recv_sems, local_sems, out_sems,
 ):
     tp = lax.axis_index("tp")
     own_parts = (
@@ -683,10 +677,10 @@
         both = jnp.dot(part, query_weight[...], preferred_element_type=F32)
         raw[rows, :256] = both
         for lanes in (slice(0, 128), slice(128, 256)):
-            query[rows, lanes] = head_ready(both[:, lanes], query_gain[...], cos, sin).astype(BF16)
+            query[rows, lanes] = head_ready(both[:, lanes], both_heads(query_gain[...]), cos, sin).astype(BF16)
         one = jnp.dot(part, key_weight[...], preferred_element_type=F32)
         raw[rows, 256:] = one
-        keys[rows, :] = head_ready(one, key_gain[...], cos, sin).astype(BF16)
+        keys[rows, :] = head_ready(one, both_heads(key_gain[...]), cos, sin).astype(BF16)
         values[rows, :] = jnp.dot(part, value_weight[...], preferred_element_type=F32).astype(BF16)
         yield clock.spend(1.5)
 
@@ -705,11 +699,22 @@
         yield clock.spend(0.4)
         return part
 
+    results = [
+        pltpu.make_async_copy(src, dst, out_sems.at[number])
+        for number, (src, dst) in enumerate(
+            (
+                (normed, normed_out), (raw, raw_out), (query, query_out), (keys, keys_out),
+                (values, values_out), (mixed, mixed_out),
+            )
+        )
+    ]
+
     def finish(own, first, second):
+        results[5].start()
         total = own[...].astype(F32) + first[...].astype(F32) + second[...].astype(F32)
         total = inputs[...].astype(F32) + total
         residual[...] = total
-        normed_two = total * row_scale(total) * gain_two[...]
+        normed_two = total * row_scale(total) * wide(gain_two[...])
         block[:256, :] = normed_two.astype(BF16)
         logits = jnp.zeros((32, 256), F32)
         for piece in split_three(normed_two):
@@ -729,7 +734,7 @@
 
     def attention_steps():
         hidden = inputs[...].astype(F32)
-        normed[tp] = (hidden * row_scale(hidden) * gain_one[...]).astype(BF16)
+        normed[tp] = (hidden * row_scale(hidden) * wide(gain_one[...])).astype(BF16)
         for copy, onward in zip(inward, outward, strict=True):
             copy.wait()
             onward.start()
@@ -737,6 +742,8 @@
         yield from line_gather_steps(post, normed.at[tp], normed, clock, 11.5, 17.5, project)
         for copy in outward:
             copy.wait()
+        for copy in results[:5]:
+            copy.start()
         yield from line_scatter_steps(post, make, far, near, finish, clock, 3.0, 12.0)
 
     def weight_steps(own, everyone, begin, near_time, far_time):
@@ -749,6 +756,8 @@
         weight_steps(gate, gate_all, 20.5, 22.0, 32.0),
     )
     post.finish()
+    for copy in results:
+        copy.wait()
 
 
 def opening(arguments, number):
@@ -769,8 +778,14 @@
             jax.ShapeDtypeStruct((4, 1024, 128), BF16),
         ],
         in_specs=[VMEM] * (len(arguments) - 2) + [ANY] * 2,
-        out_specs=[VMEM] * 9 + [ANY] * 2,
+        out_specs=[ANY] * 6 + [VMEM] * 3 + [ANY] * 2,
         scratch_shapes=[
+            pltpu.VMEM((4, 256, 1024), BF16),
+            pltpu.VMEM((1024, 384), F32),
+            pltpu.VMEM((1024, 256), BF16),
+            pltpu.VMEM((1024, 128), BF16),
+            pltpu.VMEM((1024, 128), BF16),
+            pltpu.VMEM((1024, 256), BF16),
             pltpu.VMEM((4, 256, 1024), BF16),
             pltpu.VMEM((256, 1024), BF16),
             pltpu.VMEM((2, 256, 1024), BF16),
@@ -778,6 +793,7 @@
             pltpu.SemaphoreType.DMA((count,)),
             pltpu.SemaphoreType.DMA((count,)),
             pltpu.SemaphoreType.DMA((2,)),
+            pltpu.SemaphoreType.DMA((6,)),
         ],
         compiler_params=pltpu.CompilerParams(
             collective_id=number, has_side_effects=True, vmem_limit_bytes=56 << 20
@@ -823,23 +839,41 @@
 
 
 SMALL_ROWS = 16
+WEIGHTS_AT = 20.0
 
 
 def closing_kernel(
-    back, residual, gates, cotangent, gain_two, router, query, keys, values, mixed,
-    output_weight, query_weight, key_weight, value_weight, raw, normed, inputs, gain_one,
-    query_gain, key_gain, cosine, sine, segments, live_mask, out_parts,
-    grad_inputs, dense_all, small_all, combined,
+    back, residual, gates, cotangent, gain_two, router, query_far, keys_far, values_far, mixed_far,
+    output_weight, query_weight_far, key_weight_far, value_weight_far, raw_far, normed_far,
+    inputs_far, gain_one, query_gain, key_gain, cosine, sine, segments, live_mask, out_parts,
+    weight_parts, grad_inputs, dense_all, small_all, combined, weight_sum,
     grad_all, grad_residual, low, keys_sum, values_sum, output_sum, parts, far, near,
-    dense, dense_own, small, small_own, small_line, small_sum, query_gain_sum, gain_one_sum,
-    *rest,
+    dense, dense_own, small, small_own, small_early, small_late, small_total, query_gain_sum,
+    weights, weights_far, weights_near, query, keys, values, mixed, query_weight, key_weight, value_weight, raw, normed, inputs,
+    late_sems, *rest,
 ):
-    out_scratch, dense_scratch, small_scratch = rest[:7], rest[7:10], rest[10:13]
-    post = Post(rest[13], rest[14])
+    out_scratch, dense_scratch, small_scratch = rest[:7], rest[7:11], rest[11:15]
+    post = Post(rest[15], rest[16])
     me = lax.axis_index("ep")
     tp = lax.axis_index("tp")
     ahead, behind = line_partners()
     across = (me, wrap(tp + 2))
+    late = [
+        pltpu.make_async_copy(src, dst, late_sems.at[number])
+        for number, (src, dst) in enumerate(
+            (
+                (query_far, query), (keys_far, keys), (values_far, values), (mixed_far, mixed),
+                (query_weight_far, query_weight), (key_weight_far, key_weight),
+                (value_weight_far, value_weight), (raw_far, raw), (normed_far, normed),
+                (inputs_far, inputs),
+                (weight_parts.at[wrap(tp + 1)], weights.at[0]),
+                (weight_parts.at[wrap(tp - 1)], weights.at[1]),
+                (weight_parts.at[tp], weights.at[2]),
+            )
+        )
+    ]
+    for copy in late:
+        copy.start()
     greet(brief_partners() + (ahead, behind, across))
     clock = Clock()
     out_steps = plane_scatter_steps(post, out_parts, combined, out_scratch)
@@ -861,7 +895,7 @@
     scale = row_scale(total)
     plain = total * scale
     grad_gain_two = jnp.sum(grad_two * plain, axis=0, keepdims=True)
-    grad_two = grad_two * gain_two[...]
+    grad_two = grad_two * wide(gain_two[...])
     grad_total = cotangent[...].astype(F32) + scale * (
         grad_two - plain * jnp.mean(grad_two * plain, axis=1, keepdims=True)
     )
@@ -874,7 +908,6 @@
     values_sum[...] = jnp.zeros_like(values_sum)
     output_sum[...] = jnp.zeros_like(output_sum)
     query_gain_sum[...] = jnp.zeros_like(query_gain_sum)
-    gain_one_sum[...] = jnp.zeros_like(gain_one_sum)
 
     def attention(place):
         rows = block_rows(place)
@@ -898,7 +931,7 @@
             grad_raw, grad_gain = head_back(
                 grad_query[:, lanes],
                 raw[rows, lanes],
-                query_gain[...],
+                both_heads(query_gain[...]),
                 cosine[rows, :],
                 sine[rows, :],
             )
@@ -917,9 +950,6 @@
         total = total + lax.dot_general(
             low[rows, 384:], value_weight[...], CONTRACT_LAST, preferred_element_type=F32
         )
-        gain_one_sum[...] += jnp.sum(
-            total * normed[rows, :].astype(F32), axis=0, keepdims=True
-        )
         part = parts.at[(2, 1, -1, 0).index(offset)]
         part[...] = total.astype(BF16)
         yield clock.spend(0.8)
@@ -930,14 +960,14 @@
         hidden = inputs[...].astype(F32)
         scale = row_scale(hidden)
         plain = hidden * scale
-        grad_one = grad_one * gain_one[...]
+        grad_one = grad_one * wide(gain_one[...])
         grad_inputs[...] = (
             grad_residual[...]
             + scale * (grad_one - plain * jnp.mean(grad_one * plain, axis=1, keepdims=True))
         ).astype(BF16)
 
     def router_gradient():
-        normed_pieces = split_three(plain * gain_two[...])
+        normed_pieces = split_three(plain * wide(gain_two[...]))
         total = jnp.zeros((32, 1024), F32)
         for first, second in ((0, 0), (0, 1), (1, 0), (1, 1), (0, 2), (2, 0)):
             total = total + jnp.dot(
@@ -945,85 +975,138 @@
             )
         return total
 
-    def fill_small(grad_key_gain):
+    gain_rows = small.at[brief_number(16)]
+    head_rows = small.at[brief_number(17)]
+
+    def fill_router():
         grad_router = router_gradient()
-        grad_gain_one = gain_one_sum[...] / gain_one[...]
         small[...] = jnp.zeros_like(small)
         for part in range(8):
             lanes = slice(part * 128, (part + 1) * 128)
-            small[2 * part] = grad_router[:16, lanes]
-            small[2 * part + 1] = grad_router[16:, lanes]
-            small[16, part : part + 1, :] = grad_gain_one[:, lanes]
-            small[16, 8 + part : 9 + part, :] = grad_gain_two[:, lanes]
-        small[17, 0:1, :] = query_gain_sum[...]
-        small[17, 1:2, :] = grad_key_gain
+            small[brief_number(2 * part)] = grad_router[:16, lanes]
+            small[brief_number(2 * part + 1)] = grad_router[16:, lanes]
+            gain_rows[8 + part : 9 + part, :] = grad_gain_two[:, lanes]
+
+    def fill_small(weights, grad_key_gain):
+        grad_gain_one = jnp.zeros((8, 1024), F32)
+        ones = jnp.ones((8, 128), BF16)
+        parts = [query_weight[:, :128], query_weight[:, 128:], key_weight[...], value_weight[...]]
+        for number, part in enumerate(parts):
+            product = weights[:, number * 128 : (number + 1) * 128] * part.astype(F32)
+            for piece in split_float(product):
+                grad_gain_one = grad_gain_one + lax.dot_general(
+                    ones, piece, CONTRACT_LAST, preferred_element_type=F32
+                )
+        grad_gain_one = grad_gain_one[:1] / wide(gain_one[...])
+        for part in range(8):
+            gain_rows[part : part + 1, :] = grad_gain_one[:, part * 128 : (part + 1) * 128]
+        head_rows[0:1, :] = query_gain_sum[...]
+        head_rows[1:2, :] = grad_key_gain
 
     def attention_steps():
+        filled, early_line = [], []
+
+        def send_line(part, slots):
+            return [
+                post.go(part, at(slots, number), partner)
+                for number, partner in enumerate((ahead, behind, across))
+            ]
+
+        def arrived(place):
+            if not filled:
+                filled.append(place)
+                fill_router()
+                early_line.extend(send_line(at(small, 0), small_early))
+                for copy in late:
+                    copy.wait()
+            yield from attention(place)
+
         yield from line_gather_steps(
-            post, grad_all.at[tp], grad_all, clock, 11.5, 17.5, attention
+            post, grad_all.at[tp], grad_all, clock, 11.5, 17.5, arrived
         )
         grad_raw, grad_key_gain = head_back(
             (keys_sum[0] + exchange(keys_sum[1])) * 0.125,
             raw[:, 256:],
-            key_gain[...],
+            both_heads(key_gain[...]),
             cosine[...],
             sine[...],
         )
         low[:, 256:384] = grad_raw.astype(BF16)
         low[:, 384:] = (values_sum[0] + exchange(values_sum[1])).astype(BF16)
-        yield clock.spend(2.0)
-        line_steps = line_scatter_steps(post, make, far, near, finish, clock, 3.5, 11.5)
-        last = yield from until_count(line_steps, 6)
-        fill_small(grad_key_gain)
-        now = clock.now
-        yield from side_by_side(
-            (last, line_steps), (now, dense_steps(now)), (now, small_steps(now))
-        )
-
-    def dense_steps(begin):
         weights = lax.dot_general(
             normed[...], low[...], CONTRACT_ROWS, preferred_element_type=F32
-        ).astype(BF16)
+        )
+        fill_small(weights, grad_key_gain)
+        line = early_line + send_line(at(small, 1, 0, pl.ds(0, 2)), small_late)
+        fill_dense(weights)
+        now = clock.spend(8.0)
+        yield from side_by_side(
+            (now, dense_steps(now)),
+            (now, small_steps(now, line)),
+            (now, line_scatter_steps(post, make, far, near, finish, clock, 3.5, 11.5)),
+        )
+
+    def fill_dense(weights):
+        weights = weights.astype(BF16)
         for part in range(32):
-            dense[part, :, :512] = weights[part * 32 : (part + 1) * 32]
+            dense[(*brief_number(part), slice(None), slice(0, 512))] = weights[
+                part * 32 : (part + 1) * 32
+            ]
         for part in range(4):
             block = output_sum[:, part * 256 : (part + 1) * 256].astype(BF16)
             for piece in range(8):
-                dense[part * 8 + piece, :, 512:] = block[piece * 32 : (piece + 1) * 32]
-        yield from brief_scatter_steps(post, dense, dense_own, dense_scratch, begin + 3.0)
-        dense_all[me] = dense_own[...]
-        yield from brief_gather_steps(post, dense_own, dense_all, begin + 16.0)
-
-    def small_steps(begin):
-        yield from brief_scatter_steps(post, small, small_own, small_scratch, begin)
-        line = [
-            post.go(small_own, small_line.at[0], ahead),
-            post.go(small_own, small_line.at[1], behind),
-            post.go(small_own, small_line.at[2], across),
-        ]
-        yield begin + 12.0
+                dense[(*brief_number(part * 8 + piece), slice(None), slice(512, 768))] = block[
+                    piece * 32 : (piece + 1) * 32
+                ]
+
+    def dense_steps(begin):
+        yield from brief_scatter_steps(post, dense, dense_own, dense_scratch, begin)
+        yield from brief_gather_steps(post, dense_own, dense_all, begin + 12.0)
+
+    def small_steps(begin, line):
         for copy in line:
             copy.wait_recv()
-        small_sum[...] = small_own[...] + small_line[0] + small_line[1] + small_line[2]
-        small_all[me] = small_sum[...]
-        yield from brief_gather_steps(post, small_sum, small_all, begin + 14.0)
-
-    together(attention_steps(), resumed(out_due, out_steps))
+        small_total[...] = jnp.zeros_like(small_total)
+        for place in range(4):
+            small_total[0, place] = small[0, place] + (
+                small_early[0, place] + small_early[1, place] + small_early[2, place]
+            )
+        small_total[1, 0, :2] = small[1, 0, :2] + small_late[0] + small_late[1] + small_late[2]
+        yield from brief_scatter_steps(post, small_total, small_own, small_scratch, begin)
+        yield from brief_gather_steps(post, small_own, small_all, begin + 12.0)
+
+    def make_weights(offset):
+        yield 0.0
+        if offset == 2:
+            return weight_parts.at[wrap(tp + 2)]
+        return weights.at[(1, -1, 0).index(offset)]
+
+    def finish_weights(own, first, second):
+        add_rows(weight_sum, [(own, 0), (first, 0), (second, 0)], 0, own.shape[0])
+
+    def weight_steps():
+        yield WEIGHTS_AT
+        yield from line_scatter_steps(
+            post, make_weights, weights_far, weights_near, finish_weights, Clock(WEIGHTS_AT), 14.0, 60.0
+        )
+
+    together(attention_steps(), resumed(out_due, out_steps), weight_steps())
     post.finish()
 
 
 def closing(arguments, number):
-    count = 2 * LINE_COPIES + PLANE_COPIES + 4 * BRIEF_COPIES + 3
+    count = 3 * LINE_COPIES + PLANE_COPIES + 4 * BRIEF_COPIES + 6
     return pl.pallas_call(
         closing_kernel,
         out_shape=[
             jax.ShapeDtypeStruct((256, 1024), BF16),
-            jax.ShapeDtypeStruct((32, 32, 768), BF16),
-            jax.ShapeDtypeStruct((32, SMALL_ROWS, 128), F32),
+            jax.ShapeDtypeStruct((2, 4, 4, 32, 768), BF16),
+            jax.ShapeDtypeStruct((2, 4, 4, SMALL_ROWS, 128), F32),
             jax.ShapeDtypeStruct((256, 1024), F32),
+            jax.ShapeDtypeStruct((3072, 128), F32),
         ],
-        in_specs=[VMEM] * (len(arguments) - 1) + [ANY],
-        out_specs=[VMEM] * 4,
+        in_specs=[VMEM] * 6 + [ANY] * 4 + [VMEM] + [ANY] * 6 + [VMEM] * 7 + [ANY] * 2,
+        out_specs=[VMEM] * 5,
         scratch_shapes=[
             pltpu.VMEM((4, 256, 1024), BF16),
             pltpu.VMEM((256, 1024), F32),
@@ -1034,14 +1117,28 @@
             pltpu.VMEM((4, 256, 1024), BF16),
             pltpu.VMEM((256, 1024), BF16),
             pltpu.VMEM((2, 256, 1024), BF16),
-            pltpu.VMEM((32, 32, 768), BF16),
+            pltpu.VMEM((2, 4, 4, 32, 768), BF16),
             pltpu.VMEM((32, 768), BF16),
-            pltpu.VMEM((32, SMALL_ROWS, 128), F32),
+            pltpu.VMEM((2, 4, 4, SMALL_ROWS, 128), F32),
             pltpu.VMEM((SMALL_ROWS, 128), F32),
-            pltpu.VMEM((3, SMALL_ROWS, 128), F32),
-            pltpu.VMEM((SMALL_ROWS, 128), F32),
+            pltpu.VMEM((3, 4, 4, SMALL_ROWS, 128), F32),
+            pltpu.VMEM((3, 2, SMALL_ROWS, 128), F32),
+            pltpu.VMEM((2, 4, 4, SMALL_ROWS, 128), F32),
             pltpu.VMEM((1, 128), F32),
-            pltpu.VMEM((1, 1024), F32),
+            pltpu.VMEM((3, 3072, 128), BF16),
+            pltpu.VMEM((3072, 128), BF16),
+            pltpu.VMEM((2, 3072, 128), BF16),
+            pltpu.VMEM((1024, 256), BF16),
+            pltpu.VMEM((1024, 128), BF16),
+            pltpu.VMEM((1024, 128), BF16),
+            pltpu.VMEM((1024, 256), BF16),
+            pltpu.VMEM((1024, 256), BF16),
+            pltpu.VMEM((1024, 128), BF16),
+            pltpu.VMEM((1024, 128), BF16),
+            pltpu.VMEM((1024, 384), F32),
+            pltpu.VMEM((1024, 1024), BF16),
+            pltpu.VMEM((256, 1024), BF16),
+            pltpu.SemaphoreType.DMA((13,)),
         ]
         + plane_scatter_scratch(256, 1024, BF16)
         + brief_scatter_scratch(32, 768, BF16)
@@ -1055,10 +1152,27 @@
 
 
 def finish_kernel(
-    dense, weights, residual, combined,
-    result, grad_query, grad_key, grad_value, grad_output, grad_gate, grad_up, grad_down,
+    dense_far, weights_far, residual_far, combined_far, small_far, inputs_far,
+    result, grad_inputs, grad_query, grad_key, grad_value, grad_output, grad_gate, grad_up,
+    grad_down, gain_one, gain_two, query_gain, key_gain, router,
+    dense, weights, residual, combined, small, sems,
 ):
-    result[...] = (residual[...] + combined[...]).astype(BF16)
+    copies = [
+        pltpu.make_async_copy(src, dst, sems.at[number])
+        for number, (src, dst) in enumerate(
+            (
+                (weights_far, weights), (dense_far, dense), (residual_far, residual),
+                (combined_far, combined), (small_far, small), (inputs_far, grad_inputs),
+            )
+        )
+    ]
+    for copy in copies:
+        copy.start()
+    copies[0].wait()
+    grad_gate[0] = weights[:1024, :]
+    grad_up[0] = weights[1024:2048, :]
+    grad_down[0] = weights[2048:, :].T
+    copies[1].wait()
     grad_query[...] = dense[:, :256].astype(F32)
     grad_key[...] = dense[:, 256:384].astype(F32)
     grad_value[...] = dense[:, 384:512].astype(F32)
@@ -1066,15 +1180,28 @@
         grad_output[:, part * 256 : (part + 1) * 256] = dense[
             part * 256 : (part + 1) * 256, 512:
         ].astype(F32)
-    grad_gate[0] = weights[:1024, :]
-    grad_up[0] = weights[1024:2048, :]
-    grad_down[0] = weights[2048:, :].T
-
-
-def finish_all(dense, weights, residual, combined):
+    copies[2].wait()
+    copies[3].wait()
+    result[...] = (residual[...] + combined[...]).astype(BF16)
+    copies[4].wait()
+    for part in range(8):
+        lanes = slice(part * 128, (part + 1) * 128)
+        router[:16, lanes] = small[2 * part]
+        router[16:, lanes] = small[2 * part + 1]
+        gain_one[:, lanes] = small[16, part : part + 1, :]
+        gain_two[:, lanes] = small[16, 8 + part : 9 + part, :]
+    heads = small[17]
+    heads = heads[:, :64] + heads[:, 64:]
+    query_gain[...] = heads[0:1]
+    key_gain[...] = heads[1:2]
+    copies[5].wait()
+
+
+def finish_all(arguments):
     return pl.pallas_call(
         finish_kernel,
         out_shape=[
+            jax.ShapeDtypeStruct((256, 1024), BF16),
             jax.ShapeDtypeStruct((256, 1024), BF16),
             jax.ShapeDtypeStruct((1024, 256), F32),
             jax.ShapeDtypeStruct((1024, 128), F32),
@@ -1083,12 +1210,25 @@
             jax.ShapeDtypeStruct((1, 1024, 128), F32),
             jax.ShapeDtypeStruct((1, 1024, 128), F32),
             jax.ShapeDtypeStruct((1, 128, 1024), F32),
+            jax.ShapeDtypeStruct((1, 1024), F32),
+            jax.ShapeDtypeStruct((1, 1024), F32),
+            jax.ShapeDtypeStruct((1, 64), F32),
+            jax.ShapeDtypeStruct((1, 64), F32),
+            jax.ShapeDtypeStruct((32, 1024), F32),
         ],
-        in_specs=[VMEM] * 4,
-        out_specs=[VMEM] * 8,
-        compiler_params=pltpu.CompilerParams(vmem_limit_bytes=40 << 20),
+        in_specs=[ANY] * 6,
+        out_specs=[VMEM] * 14,
+        scratch_shapes=[
+            pltpu.VMEM((1024, 768), BF16),
+            pltpu.VMEM((3072, 128), F32),
+            pltpu.VMEM((256, 1024), F32),
+            pltpu.VMEM((256, 1024), F32),
+            pltpu.VMEM((32, SMALL_ROWS, 128), F32),
+            pltpu.SemaphoreType.DMA((6,)),
+        ],
+        compiler_params=pltpu.CompilerParams(vmem_limit_bytes=60 << 20),
         name="finish_all",
-    )(dense, weights, residual, combined)
+    )(*arguments)
 
 
 STEPS = ((0, 1), (3, 4), (6, 7), (12, 13), (14, 15), (10, 11), (8, 9), (2, 5))
@@ -1097,10 +1237,10 @@
 
 def experts_kernel(
     block, grads, gate_all, up, down,
-    rows_all, out_parts, back_sum, weight_sum,
+    rows_all, out_parts, back_sum, weight_parts,
     rows_in, grads_in, both_full, down_full, both_sum, down_sum, rows_own, grads_own, gates_own,
     select, weighted, grad_rows, grad_gates, mine, other, stage, out_stage,
-    b_far, b_near, a_far, a_near, line, line_far, line_near, send_sems, recv_sems, credit, load_sems, store_sems, weight_sems, own_sem,
+    b_far, b_near, a_far, a_near, line, send_sems, recv_sems, credit, load_sems, store_sems, weight_sems, own_sem,
 ):
     a, b, core = plane_place()
     me = lax.axis_index("ep")
@@ -1260,7 +1400,7 @@
 
     def early(step):
         if step == 0:
-            for copy in down_far:
+            for copy in up_far + down_far:
                 copy.wait_recv()
 
     def after(step):
@@ -1294,8 +1434,6 @@
     relay(down_near, down_far)
     for copy in weight_loads:
         copy.wait()
-    for copy in up_far:
-        copy.wait_recv()
     extra_row = lax.broadcasted_iota(jnp.int32, (EXTRA, 1024), 0) == lane_row
 
     def one_step(step, carry):
@@ -1381,19 +1519,18 @@
     lax.fori_loop(0, len(STEPS), one_step, 0)
     last = len(STEPS) - 1
 
-    def make_weights(offset):
-        place = wrap(tp + offset)
-        lanes = pl.ds(pl.multiple_of(place * 128, 128), 128)
-        upper_lanes = pl.ds(pl.multiple_of(512 + place * 128, 128), 128)
-        part = line.at[OFFSETS.index(offset)]
-        part[:1024, :] = both_sum[:, lanes].astype(BF16)
-        part[1024:2048, :] = both_sum[:, upper_lanes].astype(BF16)
-        part[2048:, :] = down_sum[:, lanes].astype(BF16)
-        yield 1.0
-        return part
-
-    def finish_weights(own, first, second):
-        add_rows(weight_sum, [(own, 0), (first, 0), (second, 0)], 0, own.shape[0])
+    def weight_steps():
+        for part in range(4):
+            yield 2.5 + part
+            lanes = slice(part * 128, (part + 1) * 128)
+            upper_lanes = slice(512 + part * 128, 512 + (part + 1) * 128)
+            line[part, :1024, :] = both_sum[:, lanes].astype(BF16)
+            line[part, 1024:2048, :] = both_sum[:, upper_lanes].astype(BF16)
+            line[part, 2048:, :] = down_sum[:, lanes].astype(BF16)
+            Local(at(line, part), at(weight_parts, part), at(weight_sems, part)).start()
+        yield 100.0
+        for part in range(4):
+            Local(at(line, part), at(weight_parts, part), at(weight_sems, part)).wait()
 
     def back_steps():
         yield 0.0
@@ -1431,10 +1568,7 @@
                     back_sum, first_rows + [(a_near.at[0], 0), (a_near.at[1], 0)], 0, rows
                 )
 
-    together(
-        line_scatter_steps(post, make_weights, line_far, line_near, finish_weights, Clock(), 7.0, 24.0),
-        back_steps(),
-    )
+    together(back_steps(), weight_steps())
     for copy in stores[last]:
         copy.wait()
     waited = [copy for step in range(last) for copy in crossing[step]]
@@ -1447,7 +1581,7 @@
     rows, columns = block.shape
     sources = grads.shape[0]
     count = GROUP * SLOTS
-    copies = PLANE_COPIES + 16 + 8 + 8 + 4 + 3 * LINE_COPIES
+    copies = PLANE_COPIES + 16 + 8 + 8 + 4 + 2 * LINE_COPIES
     whole = (rows, columns)
     return pl.pallas_call(
         experts_kernel,
@@ -1455,10 +1589,10 @@
             jax.ShapeDtypeStruct((sources,) + whole, BF16),
             jax.ShapeDtypeStruct((sources, 256, columns), BF16),
             jax.ShapeDtypeStruct(whole, F32),
-            jax.ShapeDtypeStruct((3072, 128), F32),
+            jax.ShapeDtypeStruct((4, 3072, 128), BF16),
         ],
         in_specs=[ANY] * 5,
-        out_specs=[ANY, ANY, VMEM, VMEM],
+        out_specs=[ANY, ANY, VMEM, ANY],
         scratch_shapes=[
             pltpu.VMEM((2, GROUP) + whole, BF16),
             pltpu.VMEM((2, GROUP, 256, columns), BF16),
@@ -1482,8 +1616,6 @@
             pltpu.VMEM(whole, BF16),
             pltpu.VMEM((2,) + whole, BF16),
             pltpu.VMEM((4, 3072, 128), BF16),
-            pltpu.VMEM((3072, 128), BF16),
-            pltpu.VMEM((2, 3072, 128), BF16),
             pltpu.SemaphoreType.DMA((copies,)),
             pltpu.SemaphoreType.DMA((copies,)),
             pltpu.SemaphoreType.REGULAR,
@@ -1527,10 +1659,8 @@
     routes,
     cotangent,
 ):
-    gain_one = first_gain.astype(F32).reshape(1, -1)
-    gain_two = second_gain.astype(F32).reshape(1, -1)
-    query_scale = jnp.tile(query_gain.astype(F32), 2).reshape(1, -1)
-    key_scale = jnp.tile(key_gain.astype(F32), 2).reshape(1, -1)
+    gain_one, gain_two = first_gain.reshape(8, 128), second_gain.reshape(8, 128)
+    query_scale, key_scale = query_gain.reshape(1, -1), key_gain.reshape(1, -1)
     cosine, sine = rotary_constants()
     seg_row, live_row = segments.reshape(1, -1), live_mask.reshape(1, -1)
     router = router_weight.T
@@ -1544,35 +1674,39 @@
         ),
         1,
     )
-    rows_all, out_parts, back, weight_sums = run_experts(
+    rows_all, out_parts, back, weight_parts = run_experts(
         block, grad_all, gate_all, up_weight[0], down_weight[0], 2
     )
-    grad_inputs, dense, small, combined = closing(
+    grad_inputs, dense, small, combined, weight_sums = closing(
         (
             back, residual, gates, cotangent, gain_two, router, query, keys, values, mixed,
             output_weight, query_weight, key_weight, value_weight, raw, normed.reshape(1024, 1024),
             inputs, gain_one, query_scale, key_scale, cosine, sine, seg_row,
-            live_row, out_parts,
+            live_row, out_parts, weight_parts,
         ),
         4,
     )
-    result, grad_query, grad_key, grad_value, grad_output, grad_gate, grad_up, grad_down = (
-        finish_all(dense.reshape(1024, 768), weight_sums, residual, combined)
+    (
+        result, grad_inputs, grad_query, grad_key, grad_value, grad_output, grad_gate, grad_up,
+        grad_down, grad_gain_one, grad_gain_two, grad_query_gain, grad_key_gain, grad_router,
+    ) = finish_all(
+        (
+            dense.reshape(1024, 768), weight_sums, residual, combined,
+            small.reshape(32, SMALL_ROWS, 128), grad_inputs,
+        )
     )
-    grad_router = small[:16].reshape(8, 32, 128).transpose(0, 2, 1).reshape(1024, 32)
-    query_gain_sum, key_gain_sum = small[17, 0], small[17, 1]
     return (
         result,
         grad_inputs,
-        small[16, :8].reshape(-1),
+        grad_gain_one.reshape(-1),
         grad_query,
         grad_key,
         grad_value,
-        query_gain_sum[:64] + query_gain_sum[64:],
-        key_gain_sum[:64] + key_gain_sum[64:],
+        grad_query_gain.reshape(-1),
+        grad_key_gain.reshape(-1),
         grad_output,
-        small[16, 8:].reshape(-1),
-        grad_router,
+        grad_gain_two.reshape(-1),
+        grad_router.T,
         grad_gate,
         grad_up,
         grad_down,

time: 338 us -> 316 us (0.935)
  local copies, waits for them, and re-layouts: 9.83 us -> 0 us
  Pallas kernels: 319 us -> 310 us
    pallas_call x1, Pallas kernels: 147 us -> 133 us  [run_experts(): pl.pallas_call(experts_kernel, out_shape=[jax.ShapeDtypeStruct((sources,)...]
    unnamed x13 -> x0, local copies, waits for them, and re-layouts: 6.06 us -> none
    pallas_call x1, Pallas kernels: 97.5 us -> 102 us  [closing(): pl.pallas_call(closing_kernel, out_shape=[jax.ShapeDtypeStruct((256, 1024...]
where the time goes in v4:
time: 316 us; the launch traced here: 311 us
  Pallas kernels  310 us (98%)
    pallas_call x1, Pallas kernels, run_experts(): pl.pallas_call(experts_kernel, out_shape=[jax.ShapeDtypeStruct((sources,)...  133 us
    pallas_call x1, Pallas kernels, closing(): pl.pallas_call(closing_kernel, out_shape=[jax.ShapeDtypeStruct((256, 1024...  102 us
    pallas_call x1, Pallas kernels, opening(): pl.pallas_call(opening_kernel, out_shape=[jax.ShapeDtypeStruct((4, 256, 1...  70.3 us

profile of v4, /device:TPU:1, one launch (start us, length us, event | category | flops | bytes accessed | tf_op | source)
XLA Modules:
  0.0 310.9 jit_solution(5055460747817240971)
XLA Ops:
  0.6 70.3 %opening.1 = (bf16[4,256,1024]{2,1,0:T(8,128)(2,1)}, f32[1024,384]{1,0:T(8,128)}, bf16[1024,256]{1,0:T(8,128)(2,1)}, bf16[1024,128]{1,0:T(8,128)(2,1)}, bf16[102...) custom-call(bf16[256,1024]{1,0:T(8,128)(2,1)} %inputs_far.1, ...), custom_call_target="tpu_custom_call" | custom-call | tf_op jit(solution)/shard_map/opening/pallas_call | solution.py:765
  70.9 132.9 %run_experts.1 = (bf16[32,272,1024]{2,1,0:T(8,128)(2,1)}, bf16[32,256,1024]{2,1,0:T(8,128)(2,1)}, f32[272,1024]{1,0:T(8,128)}, bf16[4,3072,128]{2,1,0:T(8,128)(2,1)}) custom-call(bf16[272,1024]{1,0:T(8,128)(2,1)} %get-tuple-element.47.block, bf16[32,256,1024]{2,1,0:T(8,128)(2,1)} %get-tuple-element.48.grads, ...), custom_call_target="tpu_custom_call" | custom-call | tf_op jit(solution)/shard_map/run_experts/pallas_call | solution.py:1586
  203.8 101.5 %closing.1 = (bf16[256,1024]{1,0:T(8,128)(2,1)}, bf16[2,4,4,32,768]{4,3,2,1,0:T(8,128)(2,1)}, f32[2,4,4,16,128]{4,3,2,1,0:T(8,128)}, f32[256,1024]{1,0:T(8,128)}, f32[3072,128]{1,0:T(8,128)}) custom-call(f32[272,1024]{1,0:T(8,128)} %get-tuple-element.50.back, f32[256,1024]{1,0:T(8,128)} %get-tuple-element.51.residual.residual_far, ...), custom_call_target="tpu_custom_call" | custom-call | tf_op jit(solution)/shard_map/closing/pallas_call | solution.py:1099
  305.4 5.3 %finish_all.1 = (bf16[256,1024]{1,0:T(8,128)(2,1)}, bf16[256,1024]{1,0:T(8,128)(2,1)}, f32[1024,256]{1,0:T(8,128)}, f32[1024,128]{1,0:T(8,128)}, f32[1024,128]{1...) custom-call(bf16[1024,768]{1,0:T(8,128)(2,1)} %bitcast.20, ...), custom_call_target="tpu_custom_call" | custom-call | tf_op jit(solution)/shard_map/finish_all/pallas_call | solution.py:1201
